TPU v7x, 256 devices: a whole 4x4x8 slice. The times are simulated.
256 devices in a mesh: batch: 4 (over x), seq: 64 (over z, y, core).
Axes of the slice: x: 4, y: 4, z: 8, core: 2. Of those that a mesh axis runs over, the one named last changes fastest.
Arguments:
- tokens: bfloat16 [4, 32768, 1024], P('batch', 'seq'), may hold values from -20 to 20
- slot_parameters: bfloat16 [1024, 256], replicated, may hold values from -0.3125 to 0.3125
- w_in: bfloat16 [128, 1024, 4096], P('seq', None, 'batch'), may hold values from -0.1875 to 0.1875
- w_out: bfloat16 [128, 4096, 1024], P('seq', 'batch'), may hold values from -0.09375 to 0.09375
- grad_out: bfloat16 [4, 32768, 1024], P('batch', 'seq'), may hold values from -6 to 6
Outputs:
- mixed: bfloat16 [4, 32768, 1024], P('batch', 'seq')
- grad_tokens: bfloat16 [4, 32768, 1024], P('batch', 'seq')
- grad_params: float32 [1024, 256], P(('batch', 'seq'))
All inputs are finite; a program needn't handle non-finite values.
Results may differ from a plain program's by a relative error of at most 0.024.
Values may be sent and summed in bfloat16 or wider, within the bound.
No kernel may reach another device: no remote copies, remote signals or barrier semaphores. Data moves between devices by JAX's collectives and lax.ppermute only.
A program may use at most 64 MiB of HBM per device.

v0:
```python
import jax
import jax.numpy as jnp
from jax import lax
from jax.sharding import PartitionSpec as P


def gelu_exact(value_rows):
    return jax.nn.gelu(value_rows, approximate=False)


def on_device(tokens, slot_parameters, w_in, w_out, grad_out):
    source = tokens[0]
    cotan = grad_out[0]
    sequence_count = lax.axis_size("seq")
    video_batch = lax.axis_size("batch")
    seq_id = lax.axis_index("seq")
    batch_id = lax.axis_index("batch")
    slot_number = slot_parameters.shape[1]
    width_size = slot_parameters.shape[0]
    slots_per_device = slot_number // sequence_count
    exp_dev = w_in.shape[0]
    per_expert = slots_per_device // exp_dev
    logits = jnp.dot(source, slot_parameters, preferred_element_type=jnp.float32)
    peak = lax.pmax(jnp.max(logits, axis=0), "seq")
    dexp = jnp.exp(logits - peak).astype(jnp.bfloat16)
    dexp_wide = dexp.astype(jnp.float32)
    local_total = jnp.sum(dexp_wide, axis=0)
    combine = jax.nn.softmax(logits, axis=1)
    combine_b = combine.astype(jnp.bfloat16)
    total = lax.psum(local_total, "seq")
    own_total = lax.dynamic_slice_in_dim(total, seq_id * slots_per_device, slots_per_device)
    block = dexp
    numer = lax.psum_scatter(
        jnp.einsum("tn,td->nd", block, source, preferred_element_type=jnp.float32),
        "seq",
        scatter_dimension=0,
        tiled=True,
    )
    slot_full = numer / own_total[:, None]
    slot_in = slot_full.astype(jnp.bfloat16)
    stacked = lax.all_gather(slot_in[None], "batch", axis=0, tiled=True)
    expert_rows = stacked.reshape(video_batch, exp_dev, per_expert, width_size)
    pre = jnp.einsum("vesd,edh->vesh", expert_rows, w_in, preferred_element_type=jnp.float32)
    act = gelu_exact(pre).astype(jnp.bfloat16)
    partial_out = jnp.einsum("vesh,ehd->vesd", act, w_out, preferred_element_type=jnp.float32)
    partial_out = partial_out.reshape(video_batch, slots_per_device, width_size)
    summed = lax.psum(partial_out, "batch")
    own_out = lax.dynamic_index_in_dim(summed, batch_id, 0, keepdims=False)
    slot_out = lax.all_gather(own_out.astype(jnp.bfloat16), "seq", axis=0, tiled=True)
    block = combine_b
    dslot_out = lax.psum_scatter(
        jnp.einsum("tn,td->nd", block, cotan, preferred_element_type=jnp.float32),
        "seq",
        scatter_dimension=0,
        tiled=True,
    ).astype(jnp.bfloat16)
    grad_stack = lax.all_gather(dslot_out[None], "batch", axis=0, tiled=True)
    grad_rows_all = grad_stack.reshape(video_batch, exp_dev, per_expert, width_size)
    dact = jnp.einsum("vesd,ehd->vesh", grad_rows_all, w_out, preferred_element_type=jnp.float32)
    unused, pullback = jax.vjp(gelu_exact, pre)
    dpre = pullback(dact)[0].astype(jnp.bfloat16)
    partial_in = jnp.einsum("vesh,edh->vesd", dpre, w_in, preferred_element_type=jnp.float32)
    partial_in = partial_in.reshape(video_batch, slots_per_device, width_size)
    summed_in = lax.psum(partial_in, "batch")
    dslot_in = lax.dynamic_index_in_dim(summed_in, batch_id, 0, keepdims=False)
    scaled_own = (dslot_in / own_total[:, None]).astype(jnp.bfloat16)
    scaled = lax.all_gather(scaled_own, "seq", axis=0, tiled=True)
    inner = jnp.einsum("td,nd->tn", source, scaled, preferred_element_type=jnp.float32)
    local_products = jnp.sum(dexp_wide * inner, axis=0)
    shift = lax.psum(local_products, "seq") / total
    mixed = jnp.dot(combine_b, slot_out, preferred_element_type=jnp.float32).astype(jnp.bfloat16)
    dcomb = jnp.einsum("td,nd->tn", cotan, slot_out, preferred_element_type=jnp.float32)
    dlog_comb = combine * (dcomb - jnp.sum(combine * dcomb, axis=1, keepdims=True))
    dlog = dlog_comb + dexp_wide * (inner - shift)
    dlog_b = dlog.astype(jnp.bfloat16)
    grad_in = jnp.einsum("tn,dn->td", dlog_b, slot_parameters, preferred_element_type=jnp.float32)
    grad_in = grad_in + jnp.dot(dexp, scaled, preferred_element_type=jnp.float32)
    grad_tokens = grad_in.astype(jnp.bfloat16)
    block = source
    grad_params = lax.psum_scatter(
        jnp.einsum("td,tn->dn", block, dlog_b, preferred_element_type=jnp.float32),
        ("batch", "seq"),
        scatter_dimension=0,
        tiled=True,
    )
    return (mixed[None], grad_tokens[None], grad_params)


def solution(mesh):
    placed = (
        P("batch", "seq", None),
        P(),
        P("seq", None, "batch"),
        P("seq", "batch", None),
        P("batch", "seq", None),
    )
    return jax.shard_map(
        on_device,
        mesh=mesh,
        in_specs=placed,
        out_specs=(P("batch", "seq", None), P("batch", "seq", None), P(("batch", "seq"), None)),
        check_vma=False,
    )
```

profile of v0, /device:TPU:6, one launch (start us, length us, event | category | flops | bytes accessed | tf_op | source)
XLA Modules:
  0.0 949.9 jit_solution(5271493828684739989)
XLA Ops:
  7.2 0.0 copy-start
  7.2 0.0 copy-start.3
  7.2 0.0 all-reduce.11.cloned.1.call-start
  7.2 1.2 copy-done
  8.4 1.6 fusion.70
  10.0 0.2 fusion.28
  10.2 131.8 %pmax.7 = f32[256]{0:T(256)S(1)} all-reduce(f32[256]{0:T(256)S(1)} %get-tuple-element.13), channel_id=1, replica_groups=mesh['batch'=4,'seq'=64] {'seq'}, use_global_device_ids=true, to_apply=%region_3.0 | all-reduce | flops 256 | bytes 2048 | tf_op jit(solution)/shard_map/pmax | solution.py:24
  142.0 0.1 convert_reduce_fusion
  142.1 1.4 fusion.18
  143.6 0.0 all-reduce.11.cloned.1.call-update
  143.6 0.0 all-reduce.9.cloned.1.call-start
  143.6 0.0 copy-done.3
  143.7 0.6 dynamic-slice
  144.9 1.9 fusion.13
  146.8 258.9 %all-reduce.14 = (f32[256]{0:T(256)S(1)}, bf16[256,1024]{1,0:T(8,128)(2,1)}) all-reduce(f32[256]{0:T(256)S(1)} %get-tuple-element.16, f32[256,1024]{1,0:T(8,128)S(1)} %fusion.13), channel_id=1, replica_groups=mesh['batch'=4,'seq'=64] {'seq'}, use_global_device_ids=true, to_apply=%region_6.0 | all-reduce | flops 262400 | bytes 1574912 | tf_op jit(solution)/shard_map/psum | solution.py:30
  405.7 0.7 fusion.57
  406.4 11.9 %all-gather.4 = bf16[4,4,1024]{2,1,0:T(4,128)(2,1)S(1)} all-gather(bf16[1,4,1024]{2,1,0:T(4,128)(2,1)S(1)} %fusion.57), channel_id=4, replica_groups=mesh['batch'=4,'seq'=64] {'batch'}, dimensions={0}, use_global_device_ids=true | all-gather | bytes 40960 | tf_op jit(solution)/shard_map/all_gather | solution.py:57
  418.3 0.1 dynamic_slice.10
  418.4 0.0 all-reduce.11.cloned.1.call-done
  418.4 0.0 copy-start.1
  418.4 1.0 fusion.59
  419.4 12.0 %all-gather.3 = bf16[4,4,1024]{2,1,0:T(4,128)(2,1)S(1)} all-gather(bf16[1,4,1024]{2,1,0:T(4,128)(2,1)S(1)} %fusion.59), channel_id=2, replica_groups=mesh['batch'=4,'seq'=64] {'batch'}, dimensions={0}, use_global_device_ids=true | all-gather | bytes 40960 | tf_op jit(solution)/shard_map/all_gather | solution.py:41
  431.4 2.9 fusion.2
  434.3 0.0 copy-done.1
  434.3 0.9 fusion.6
  435.2 6.5 fusion
  441.7 14.5 %psum.29 = bf16[4,4,1024]{2,0,1:T(4,128)(2,1)S(1)} all-reduce(f32[4,4,1024]{2,0,1:T(4,128)S(1)} %bitcast.170), channel_id=1, replica_groups=mesh['batch'=4,'seq'=64] {'batch'}, use_global_device_ids=true, to_apply=%region_7.0 | all-reduce | flops 16384 | bytes 98304 | tf_op jit(solution)/shard_map/psum | solution.py:47
  456.2 0.0 all-reduce.9.cloned.1.call-update
  456.2 0.0 all-reduce.13.cloned.1.call-start
  456.3 47.2 %all-gather.1 = bf16[1,256,1024]{2,0,1:T(2,128)(2,1)S(1)} all-gather(bf16[1,4,1024]{2,0,1:T(2,128)(2,1)S(1)} %dynamic-slice_convert_fusion.1), channel_id=3, replica_groups=mesh['batch'=4,'seq'=64] {'seq'}, dimensions={1}, use_global_device_ids=true | all-gather | bytes 532480 | tf_op jit(solution)/shard_map/all_gather | solution.py:49
  503.5 2.5 multiply_reduce_fusion
  506.0 1.5 fusion.8
  507.5 0.0 all-reduce.9.cloned.1.call-done
  507.5 0.9 constant_dynamic-slice_fusion.1
  508.3 0.1 fusion.58
  508.4 50.3 %all-gather.5 = bf16[64,4,1024]{2,1,0:T(4,128)(2,1)S(1)} all-gather(bf16[1,4,1024]{2,1,0:T(4,128)(2,1)S(1)} %fusion.58), channel_id=1, replica_groups=mesh['batch'=4,'seq'=64] {'seq'}, dimensions={0}, use_global_device_ids=true | all-gather | bytes 532480 | tf_op jit(solution)/shard_map/all_gather | solution.py:67
  558.7 0.1 reshape.39
  558.8 0.0 copy-start.2
  558.8 1.3 fusion.22
  560.1 126.7 %psum.31 = f32[256]{0:T(256)S(1)} all-reduce(f32[256]{0:T(256)S(1)} %get-tuple-element.20), channel_id=1, replica_groups=mesh['batch'=4,'seq'=64] {'seq'}, use_global_device_ids=true, to_apply=%region_12.13 | all-reduce | flops 256 | bytes 2048 | tf_op jit(solution)/shard_map/psum | solution.py:70
  686.8 1.5 fusion.24
  688.3 1.5 convolution_bitcast_fusion
  689.8 0.0 all-reduce.13.cloned.1.call-update
  689.8 0.0 copy-done.2
  689.8 0.5 fusion.71
  690.3 1.4 fusion.9
  691.7 250.0 %all-reduce.13.cloned.1.call-done = f32[1024,256]{0,1:T(8,128)} async-done(((f32[1024,256]{0,1:T(8,128)}), f32[1024,256]{0,1:T(8,128)}) %all-reduce.13.cloned.1.call-update) | async-done | bytes 1048592
  941.7 1.0 constant_dynamic-slice_fusion
  942.7 0.7 copy.25
  (4 shorter events, 0.1 us)
Async XLA Ops:
  7.2 1.2 copy-start
  7.2 136.5 %copy-start.3 = (u32[256]{0:T(256)S(1)}, u32[256]{0:T(256)}, u32[]{:S(2)}) copy-start(u32[256]{0:T(256)} %constant.93) | copy-start | bytes 3076
  7.2 411.2 %all-reduce.11.cloned.1.call-start = ((), (), s32[]{:S(2)}) async-start(), calls=%async_computation.1 | async-start | bytes 2097152
  143.6 363.9 %all-reduce.9.cloned.1.call-start = ((), (), s32[]{:S(2)}) async-start(), calls=%async_computation | async-start | bytes 131072 | tf_op jit(solution)/shard_map/psum | solution.py:64
  418.4 15.9 %copy-start.1 = (bf16[2,1024,1024]{2,1,0:T(8,128)(2,1)S(1)}, bf16[2,1024,1024]{2,1,0:T(8,128)(2,1)}, u32[]{:S(2)}) copy-start(bf16[2,1024,1024]{2,1,0:T(8,128)(2,1)} %param.8) | copy-start | bytes 12582916
  456.2 485.5 %all-reduce.13.cloned.1.call-start = ((), (), s32[]{:S(2)}) async-start(), calls=%async_computation.2 | async-start | bytes 2097152
  558.8 131.0 %copy-start.2 = (bf16[1024,256]{1,0:T(8,128)(2,1)S(1)}, bf16[1024,256]{1,0:T(8,128)(2,1)}, u32[]{:S(2)}) copy-start(bf16[1024,256]{1,0:T(8,128)(2,1)} %param.6) | copy-start | bytes 1572868
Sparse Core Ops, SparseCore 0:
  143.7 181.1 all-reduce.10
  456.4 40.6 all-reduce.8
  689.9 251.7 all-reduce.12
where the time goes:
time: 951 us; the launch traced here: 950 us
  blocking collectives  653 us (69%)
  waiting for transfers between devices  250 us (26%)
  matrix products  23.8 us (3%)
  between operations  14.5 us (2%)
    psum x1, blocking collectives, on_device(): total = lax.psum(local_total, 'seq')  259 us
    unnamed x5, waiting for transfers between devices  250 us
    pmax x1, blocking collectives, on_device(): peak = lax.pmax(jnp.max(logits, axis=0), 'seq')  132 us
    psum x1, blocking collectives, on_device(): shift = lax.psum(local_products, 'seq') / total  127 us
    all_gather x1, blocking collectives, on_device(): scaled = lax.all_gather(scaled_own, 'seq', axis=0, tiled=True)  50.3 us
    all_gather x1, blocking collectives, on_device(): lax.all_gather(own_out.astype(jnp.bfloat16), 'seq', axis=0, tiled=True)  47.2 us
  transfers between devices with their start and end apart: 3, of which 1 were waited for; matrix products, arithmetic and copies ran while one was open for 1% of the time, Pallas kernels for 0%

commit v1 on v0

v1 whole, which is shorter than its diff:
```python
import jax
import jax.numpy as jnp
from jax import lax
from jax.experimental import pallas as pl
from jax.experimental.pallas import tpu as pltpu
from jax.sharding import Mesh, PartitionSpec as P

BF = jnp.bfloat16
F32 = jnp.float32
AXES = ("x", "z", "y", "c")
ZY = ("z", "y")
STAT = 128
PARAMS = pltpu.CompilerParams(vmem_limit_bytes=40 * 1024 * 1024)


def dot(a, b, contract=((1,), (0,))):
    return lax.dot_general(a, b, (contract, ((), ())), preferred_element_type=F32)


def iota(shape, dim):
    return lax.broadcasted_iota(jnp.int32, shape, dim)


def call(body, outs, *args, flops=0, scratch=(), params=PARAMS):
    nbytes = sum(a.size * a.dtype.itemsize for a in args)
    nbytes += sum(o.size * o.dtype.itemsize for o in outs)
    return pl.pallas_call(
        body,
        out_shape=outs,
        in_specs=[pl.BlockSpec(memory_space=pltpu.VMEM)] * len(args),
        out_specs=[pl.BlockSpec(memory_space=pltpu.VMEM)] * len(outs),
        scratch_shapes=list(scratch),
        compiler_params=params,
        cost_estimate=pl.CostEstimate(flops=flops, bytes_accessed=nbytes, transcendentals=0),
    )(*args)


def split(value):
    high = value.astype(BF).astype(F32)
    return high, (value - high).astype(BF).astype(F32)


def stats(lane, first, second, third):
    return jnp.where(lane == 0, first, jnp.where(lane == 1, second, jnp.where(lane == 2, third, 0.0)))


def softmax_rows(logits):
    e = jnp.exp(logits - jnp.max(logits, axis=1, keepdims=True))
    return e / jnp.sum(e, axis=1, keepdims=True)


def reduce_tokens(tok_ref, cot_ref, par_ref, keep_ref, send_ref, logit_ref):
    core = lax.axis_index("c")
    tok = tok_ref[...]
    logits = dot(tok, par_ref[...])
    logit_ref[...] = logits
    n = logits.shape[1]
    refpoint = jnp.max(logits, axis=0, keepdims=True).astype(BF).astype(F32)
    dexp = jnp.exp(logits - refpoint).astype(BF)
    comb = softmax_rows(logits).astype(BF)
    numer = dot(dexp, tok, ((0,), (0,)))
    dslot = dot(comb, cot_ref[...], ((0,), (0,)))
    total = dot(dexp, jnp.ones((tok.shape[0], STAT), BF), ((0,), (0,)))
    diag = jnp.where(iota((n, n), 0) == iota((n, n), 1), refpoint, 0.0).astype(BF)
    point = dot(diag, jnp.ones((n, STAT), BF))
    high, low = split(total)
    side = stats(iota((n, STAT), 1), point, high, low).astype(BF)
    upper = jnp.concatenate([numer.astype(BF), side], axis=1)
    lower = jnp.concatenate([dslot.astype(BF), jnp.zeros((n, STAT), BF)], axis=1)
    rows = jnp.concatenate([upper, lower], axis=0)
    row, col = iota((n, 2 * n), 0), iota((n, 2 * n), 1)
    for ref, c in ((keep_ref, core), (send_ref, 1 - core)):
        want = (row // 8) * 8 + c * 4 + row % 4 + ((row // 4) % 2) * n
        ref[...] = dot((col == want).astype(BF), rows).astype(BF)


def merge_cores(a_ref, b_ref, out_ref):
    a, b = a_ref[...].astype(F32), b_ref[...].astype(F32)
    width = a.shape[1] - STAT
    ma, mb = a[:, width:width + 1], b[:, width:width + 1]
    top = jnp.maximum(ma, mb)
    sa, sb = jnp.exp(ma - top), jnp.exp(mb - top)
    out_ref[:, :width] = (sa * a[:, :width] + sb * b[:, :width]).astype(BF)
    ta = a[:, width + 1:width + 2] + a[:, width + 2:width + 3]
    tb = b[:, width + 1:width + 2] + b[:, width + 2:width + 3]
    high, low = split(sa * ta + sb * tb)
    out_ref[:, width:] = stats(iota((a.shape[0], STAT), 1), top, high, low).astype(BF)


def merge_shards(in_ref, pay_ref, full_ref, side_ref):
    value = in_ref[...].astype(F32)
    width = value.shape[2] - STAT
    point = value[:, :, width:width + 1]
    top = jnp.max(point, axis=0)
    scale = jnp.exp(point - top[None])
    total = jnp.sum(scale * (value[:, :, width + 1:width + 2] + value[:, :, width + 2:width + 3]), axis=0)
    acc = jnp.sum(scale * value[:, :, :width], axis=0)
    slots = acc.shape[0] // 2
    first = iota((2 * slots, 1), 0) < slots
    full = acc / jnp.where(first, total, 1.0)
    full_ref[...] = full
    both = jnp.concatenate([total[:slots], total[:slots]], axis=0)
    side_ref[...] = jnp.where(iota((2 * slots, STAT), 1) == 0, top, both)
    pay_ref[...] = jnp.broadcast_to(full.astype(BF)[None], pay_ref.shape)


def gelu_parts(u):
    cdf = 0.5 * (1.0 + lax.erf(u * 0.7071067811865476))
    pdf = 0.3989422804014327 * jnp.exp(-0.5 * u * u)
    return u * cdf, cdf + u * pdf


def experts(x_ref, win_ref, wout_ref, out_ref, f_ref, g_ref, o_acc, d_acc):
    e, h = pl.program_id(0), pl.program_id(1)
    rows = f_ref.shape[0]

    @pl.when((e == 0) & (h == 0))
    def _():
        row, col = iota((rows, 2 * rows), 0), iota((rows, 2 * rows), 1)
        want = (row // 4) * 8 + row % 4
        x = x_ref[...]
        f_ref[...] = dot((col == want).astype(BF), x).astype(BF)
        g_ref[...] = dot((col == want + 4).astype(BF), x).astype(BF)
        o_acc[...] = jnp.zeros_like(o_acc)
        d_acc[...] = jnp.zeros_like(d_acc)

    w1, w2 = win_ref[0], wout_ref[0]
    mine = (iota((rows, 1), 0) % 4) // 2 == e
    pre = dot(f_ref[...], w1)
    gelu, slope = gelu_parts(pre)
    act = jnp.where(mine, gelu, 0.0).astype(BF)
    o_acc[...] += dot(act, w2)
    dact = dot(g_ref[...], w2, ((1,), (1,)))
    dpre = jnp.where(mine, dact * slope, 0.0).astype(BF)
    d_acc[...] += dot(dpre, w1, ((1,), (1,)))

    @pl.when((e == pl.num_programs(0) - 1) & (h == pl.num_programs(1) - 1))
    def _():
        for v in range(rows // 4):
            out_ref[v, 0:4, :] = o_acc[4 * v:4 * v + 4, :]
            out_ref[v, 4:8, :] = d_acc[4 * v:4 * v + 4, :]


def finish_slots(in_ref, full_ref, side_ref, out_ref):
    value = jnp.sum(in_ref[...], axis=0)
    width = value.shape[1]
    slots = value.shape[0] // 2
    first = iota((2 * slots, 1), 0) < slots
    side = side_ref[...]
    body = jnp.where(first, value, value / side[:, 1:2]).astype(BF)
    wide = body.astype(F32)
    shift = jnp.sum(full_ref[:slots, :] * wide[slots:, :], axis=1, keepdims=True)
    shift = jnp.concatenate([shift, shift], axis=0)
    high, low = split(shift)
    st = stats(iota((2 * slots, STAT), 1), side[:, 0:1], high, low).astype(BF)
    block = jnp.concatenate([body, st], axis=1)
    out_ref[...] = jnp.broadcast_to(block[None], out_ref.shape)


def token_grads(logit_ref, tok_ref, cot_ref, own_ref, oth_ref,
                keep_ref, send_ref, dlog_ref, dexp_ref, comb_ref, so_ref, sc_ref):
    core = lax.axis_index("c")
    logits, tok = logit_ref[...], tok_ref[...]
    n = logits.shape[1]
    width = tok.shape[1]
    rows = jnp.concatenate([own_ref[...], oth_ref[...]], axis=0)
    slot, col = iota((n, 2 * n), 0), iota((n, 2 * n), 1)
    want = (slot // 8) * 8 + slot % 4 + jnp.where((slot // 4) % 2 == core, 0, n)
    first = dot((col == want).astype(BF), rows)
    second = dot((col == want + 4).astype(BF), rows[:, :width])
    slot_out, scaled = first[:, :width].astype(BF), second.astype(BF)
    so_ref[...] = slot_out
    sc_ref[...] = scaled
    side = first[:, width:].T
    point, shift = side[0:1, :], side[1:2, :] + side[2:3, :]
    comb = softmax_rows(logits)
    comb_ref[...] = comb.astype(BF)
    dexp = jnp.exp(logits - point).astype(BF)
    dexp_ref[...] = dexp
    dcomb = dot(cot_ref[...], slot_out, ((1,), (1,)))
    inner = dot(tok, scaled, ((1,), (1,)))
    dlog = comb * (dcomb - jnp.sum(comb * dcomb, axis=1, keepdims=True))
    dlog = (dlog + dexp.astype(F32) * (inner - shift)).astype(BF)
    dlog_ref[...] = dlog
    gp = dot(tok, dlog, ((0,), (0,))).reshape(width // 8, 8, n)
    low, high = gp[:, 0:4, :], gp[:, 4:8, :]
    keep_ref[...] = jnp.where(core == 0, low, high).astype(BF)
    send_ref[...] = jnp.where(core == 0, high, low).astype(BF)


def token_outputs(comb_ref, so_ref, dlog_ref, par_ref, dexp_ref, sc_ref, mixed_ref, grad_ref):
    mixed_ref[...] = dot(comb_ref[...], so_ref[...]).astype(BF)
    grad = dot(dlog_ref[...], par_ref[...], ((1,), (1,)))
    grad_ref[...] = (grad + dot(dexp_ref[...], sc_ref[...])).astype(BF)


def on_device(tokens, slot_parameters, w_in, w_out, grad_out):
    shape = jax.ShapeDtypeStruct
    tok, cot = tokens[0], grad_out[0]
    count, width = tok.shape
    n = slot_parameters.shape[1]
    videos = lax.axis_size("x")
    owners = lax.axis_size("z") * lax.axis_size("y")
    wide = width + STAT
    unit = 2 * count * width * n
    swap = [(0, 1), (1, 0)]

    keep, send, logits = call(
        reduce_tokens,
        [shape((n, wide), BF), shape((n, wide), BF), shape((count, n), F32)],
        tok, cot, slot_parameters, flops=5 * unit,
    )
    other = lax.ppermute(send, "c", swap)
    (merged,) = call(merge_cores, [shape((n, wide), BF)], keep, other)
    shards = lax.all_to_all(merged.reshape(owners, 8, wide), ZY, 0, 0, tiled=True)
    pay, full, side = call(
        merge_shards,
        [shape((videos, 8, width), BF), shape((8, width), F32), shape((8, STAT), F32)],
        shards,
    )
    stacked = lax.all_to_all(pay, "x", 0, 0, tiled=True)

    hidden = w_in.shape[2]
    chunk = 256
    rows = 4 * videos
    partial = pl.pallas_call(
        experts,
        grid=(w_in.shape[0], hidden // chunk),
        in_specs=[
            pl.BlockSpec((2 * rows, width), lambda e, h: (0, 0)),
            pl.BlockSpec((1, width, chunk), lambda e, h: (e, 0, h)),
            pl.BlockSpec((1, chunk, width), lambda e, h: (e, h, 0)),
        ],
        out_specs=pl.BlockSpec((videos, 8, width), lambda e, h: (0, 0, 0)),
        out_shape=shape((videos, 8, width), F32),
        scratch_shapes=[
            pltpu.VMEM((rows, width), BF), pltpu.VMEM((rows, width), BF),
            pltpu.VMEM((rows, width), F32), pltpu.VMEM((rows, width), F32),
        ],
        compiler_params=PARAMS,
        cost_estimate=pl.CostEstimate(flops=8 * rows * w_in.size, bytes_accessed=4 * w_in.size, transcendentals=0),
    )(stacked.reshape(2 * rows, width), w_in, w_out)
    parts = lax.all_to_all(partial, "x", 0, 0, tiled=True)
    (block,) = call(finish_slots, [shape((owners, 8, wide), BF)], parts, full, side)
    mine = lax.all_to_all(block, ZY, 0, 0, tiled=True).reshape(n, wide)
    theirs = lax.ppermute(mine, "c", swap)

    gp_keep, gp_send, dlog, dexp, comb, slot_out, scaled = call(
        token_grads,
        [shape((width // 8, 4, n), BF), shape((width // 8, 4, n), BF),
         shape((count, n), BF), shape((count, n), BF), shape((count, n), BF),
         shape((n, width), BF), shape((n, width), BF)],
        logits, tok, cot, mine, theirs, flops=5 * unit,
    )
    gp_other = lax.ppermute(gp_send, "c", swap)
    mixed, grad_tokens = call(
        token_outputs,
        [shape((count, width), BF), shape((count, width), BF)],
        comb, slot_out, dlog, slot_parameters, dexp, scaled, flops=3 * unit,
    )
    half = (gp_keep.astype(F32) + gp_other.astype(F32)).astype(BF)
    pieces = lax.all_to_all(half, ("x", "z", "y"), 0, 0, tiled=True)
    grad_params = jnp.sum(pieces.astype(F32), axis=0)
    return mixed[None], grad_tokens[None], grad_params


def solution(mesh):
    sizes = dict(mesh.shape)
    grid = Mesh(mesh.devices.reshape(sizes["batch"], sizes["seq"] // 8, 4, 2), AXES)
    seq = ("z", "y", "c")
    placed = (
        P("x", seq, None),
        P(),
        P(seq, None, "x"),
        P(seq, "x", None),
        P("x", seq, None),
    )
    return jax.shard_map(
        on_device,
        mesh=grid,
        in_specs=placed,
        out_specs=(P("x", seq, None), P("x", seq, None), P(AXES, None)),
        check_vma=False,
    )
```

time: 951 us -> 115 us (0.12)
  blocking collectives: 653 us -> 67.7 us
  waiting for transfers between devices: 250 us -> 15.8 us
  matrix products: 23.8 us -> 0 us
  Pallas kernels: 0 us -> 15.1 us
  between operations: 14.5 us -> 0.73 us
    psum x3 -> x0, blocking collectives: 400 us -> none  [the longest x1 259 us: on_device(): total = lax.psum(local_total, 'seq')]
    unnamed x5 -> x0, waiting for transfers between devices: 250 us -> none
    pmax x1 -> x0, blocking collectives: 132 us -> none  [on_device(): peak = lax.pmax(jnp.max(logits, axis=0), 'seq')]
    all_gather x4 -> x0, blocking collectives: 121 us -> none  [the longest x1 50.3 us: on_device(): scaled = lax.all_gather(scaled_own, 'seq', axis=0, tiled=True)]
    all_to_all x0 -> x4, blocking collectives: none -> 67.7 us  [the longest x1 30.6 us: on_device(): lax.all_to_all(merged.reshape(owners, 8, wide), ZY, 0, 0, tiled=True)]
    dot_general x12 -> x0, matrix products: 23.8 us -> none  [the longest x1 6.47 us: on_device(): jnp.einsum('vesh,edh->vesd', dpre, w_in, preferred_element_type=jnp.float32)]
    pallas_call x0 -> x7, Pallas kernels: none -> 15.1 us  [the longest x1 7.58 us: on_device(): pl.pallas_call(experts, grid=(w_in.shape[0], hidden // chunk), in_specs=[...]
    all_to_all x0 -> x1, waiting for transfers between devices: none -> 10.4 us  [on_device(): pieces = lax.all_to_all(half, ('x', 'z', 'y'), 0, 0, tiled=True)]
  transfers between devices with their start and end apart: 3 -> 4, of which waited for: 1 -> 4; matrix products, arithmetic and copies ran while one was open for 1% -> 0% of each run, Pallas kernels for 0% -> 2%
where the time goes in v1:
time: 115 us; the launch traced here: 113 us
  blocking collectives  67.7 us (59%)
  waiting for transfers between devices  15.8 us (14%)
  Pallas kernels  15.1 us (13%)
  starting transfers between devices  9 us (8%)
  local copies, waits for them, and re-layouts  3.51 us (3%)
  other arithmetic  1.6 us (1%)
    all_to_all x1, blocking collectives, on_device(): lax.all_to_all(merged.reshape(owners, 8, wide), ZY, 0, 0, tiled=True)  30.6 us
    all_to_all x1, blocking collectives, on_device(): mine = lax.all_to_all(block, ZY, 0, 0, tiled=True).reshape(n, wide)  20.4 us
    all_to_all x1, waiting for transfers between devices, on_device(): pieces = lax.all_to_all(half, ('x', 'z', 'y'), 0, 0, tiled=True)  10.4 us
    all_to_all x1, starting transfers between devices, on_device(): pieces = lax.all_to_all(half, ('x', 'z', 'y'), 0, 0, tiled=True)  8.68 us
    all_to_all x1, blocking collectives, on_device(): parts = lax.all_to_all(partial, 'x', 0, 0, tiled=True)  8.49 us
    all_to_all x1, blocking collectives, on_device(): stacked = lax.all_to_all(pay, 'x', 0, 0, tiled=True)  8.13 us
    pallas_call x1, Pallas kernels, on_device(): pl.pallas_call(experts, grid=(w_in.shape[0], hidden // chunk), in_specs=[...  7.58 us
    pallas_call x6, Pallas kernels, call(): pl.pallas_call(body, out_shape=outs, in_specs=[pl.BlockSpec(memory_space=...  7.51 us
  transfers between devices with their start and end apart: 4, of which 4 were waited for; matrix products, arithmetic and copies ran while one was open for 0% of the time, Pallas kernels for 2%

profile of v1, /device:TPU:6, one launch (start us, length us, event | category | flops | bytes accessed | tf_op | source)
XLA Modules:
  0.0 113.4 jit_solution(3574115912184265321)
XLA Ops:
  0.6 0.0 copy-start.2
  0.6 1.2 %copy-done.2 = bf16[1,512,1024]{2,1,0:T(8,128)(2,1)S(1)} copy-done((bf16[1,512,1024]{2,1,0:T(8,128)(2,1)S(1)}, bf16[1,512,1024]{2,1,0:T(8,128)(2,1)}, u32[]{:S(2)}) %copy-start.2) | copy-done | bytes 1048600
  1.9 0.0 copy-start.4
  1.9 1.2 %copy-done.4 = bf16[1,512,1024]{2,1,0:T(8,128)(2,1)S(1)} copy-done((bf16[1,512,1024]{2,1,0:T(8,128)(2,1)S(1)}, bf16[1,512,1024]{2,1,0:T(8,128)(2,1)}, u32[]{:S(2)}) %copy-start.4) | copy-done | bytes 1048600
  3.1 0.0 copy-start.6
  3.1 1.0 copy-done.6
  4.1 0.0 copy-start
  4.1 0.0 copy-start.1
  4.1 2.4 %shard_map.76 = (bf16[256,1152]{1,0:T(8,128)(2,1)S(1)}, bf16[256,1152]{1,0:T(8,128)(2,1)S(1)}, f32[512,256]{1,0:T(8,128)S(1)}) custom-call(bf16[512,1024]{1,0:T(8,128)(2,1)S(1)} %bitcast.11, bf16[512,1024]{1,0:T(8,128)(2,1)S(1)} %bitcast.13, bf16[1024,256]{1,0:T(8,128)(2,1)S(1)} %copy-done.6), custom_call_target="tpu_custom_call" | custom-call | flops 1342177280 | bytes 4325376 | tf_op jit(solution)/shard_map/pallas_call | solution.py:27
  6.6 0.1 collective-permute-start
  6.7 2.0 %collective-permute-done.b_ref = bf16[256,1152]{1,0:T(8,128)(2,1)S(1)} collective-permute-done((bf16[256,1152]{1,0:T(8,128)(2,1)S(1)}, bf16[256,1152]{1,0:T(8,128)(2,1)S(1)}, u32[]{:S(2)}, u32[]{:S(2)}) %collective-permute-start) | collective-permute-done | bytes 589856 | tf_op jit(solution)/shard_map/ppermute | solution.py:213
  8.7 0.5 shard_map.77
  9.2 30.6 %all_to_all.25.in_ref = bf16[32,8,1152]{2,1,0:T(8,128)(2,1)S(1)} all-to-all(bf16[32,8,1152]{2,1,0:T(8,128)(2,1)S(1)} %bitcast.7), channel_id=1, replica_groups=mesh['x'=4,'z'=8,'y'=4,'c'=2] {'z','y'}, dimensions={0} | all-to-all | bytes 1179648 | tf_op jit(solution)/shard_map/all_to_all | solution.py:215
  39.8 0.3 shard_map.78
  40.1 8.1 %all_to_all.26 = bf16[4,8,1024]{2,1,0:T(8,128)(2,1)S(1)} all-to-all(bf16[4,8,1024]{2,1,0:T(8,128)(2,1)S(1)} %get-tuple-element.21), channel_id=1, replica_groups=mesh['x'=4,'z'=8,'y'=4,'c'=2] {'x'}, dimensions={0} | all-to-all | bytes 131072 | tf_op jit(solution)/shard_map/all_to_all | solution.py:221
  48.2 0.0 copy-done
  48.2 0.0 copy-done.1
  48.2 0.0 copy-start.3
  48.2 0.0 copy-start.5
  48.2 7.6 %shard_map.79 = f32[4,8,1024]{2,1,0:T(8,128)S(1)} custom-call(bf16[32,1024]{1,0:T(8,128)(2,1)S(1)} %bitcast.10, bf16[2,1024,1024]{2,1,0:T(8,128)(2,1)S(1)} %copy-done, bf16[2,1024,1024]{2,1,0:T(8,128)(2,1)S(1)} %copy-done.1), custom_call_target="tpu_custom_call" | custom-call | flops 268435456 | bytes 8388608 | tf_op jit(solution)/shard_map/pallas_call | solution.py:226
  55.8 0.0 copy-start.7
  55.8 8.5 %all_to_all.27.in_ref = f32[4,8,1024]{2,1,0:T(8,128)S(1)} all-to-all(f32[4,8,1024]{2,1,0:T(8,128)S(1)} %shard_map.79), channel_id=1, replica_groups=mesh['x'=4,'z'=8,'y'=4,'c'=2] {'x'}, dimensions={0} | all-to-all | bytes 262144 | tf_op jit(solution)/shard_map/all_to_all | solution.py:243
  64.3 0.3 shard_map.80
  64.6 20.4 %all_to_all.28 = bf16[32,8,1152]{2,1,0:T(8,128)(2,1)S(1)} all-to-all(bf16[32,8,1152]{2,1,0:T(8,128)(2,1)S(1)} %shard_map.80), channel_id=1, replica_groups=mesh['x'=4,'z'=8,'y'=4,'c'=2] {'z','y'}, dimensions={0} | all-to-all | bytes 1179648 | tf_op jit(solution)/shard_map/all_to_all | solution.py:245
  85.0 0.0 collective-permute-start.1
  85.0 2.0 %collective-permute-done.1.oth_ref = bf16[256,1152]{1,0:T(8,128)(2,1)S(1)} collective-permute-done((bf16[256,1152]{1,0:T(8,128)(2,1)S(1)}, bf16[256,1152]{1,0:T(8,128)(2,1)S(1)}, u32[]{:S(2)}, u32[]{:S(2)}) %collective-permute-start.1) | collective-permute-done | bytes 589856 | tf_op jit(solution)/shard_map/ppermute | solution.py:246
  87.0 0.0 copy-done.3
  87.0 0.0 copy-done.5
  87.0 1.9 %shard_map.81 = (bf16[128,4,256]{2,1,0:T(4,128)(2,1)S(1)}, bf16[128,4,256]{2,1,0:T(4,128)(2,1)S(1)}, bf16[512,256]{1,0:T(8,128)(2,1)S(1)}, bf16[512,256]{1,0:T(8...) custom-call(f32[512,256]{1,0:T(8,128)S(1)} %get-tuple-element.18.logit_re, ...), custom_call_target="tpu_custom_call" | custom-call | flops 1342177280 | bytes 6160384 | tf_op jit(solution)/shard_map/pallas_call | solution.py:27
  88.9 0.2 collective-permute-start.2
  89.1 1.4 %collective-permute-done.2 = bf16[128,4,256]{2,1,0:T(4,128)(2,1)S(1)} collective-permute-done((bf16[128,4,256]{2,1,0:T(4,128)(2,1)S(1)}, bf16[128,4,256]{2,1,0:T(4,128)(2,1)S(1)}, u32[]{:S(2)}, u32[]{:S(2)}) %collective-permute-start.2) | collective-permute-done | bytes 262176 | tf_op jit(solution)/shard_map/ppermute | solution.py:255
  90.5 0.8 add_convert_fusion
  91.4 8.7 %all-to-all-start.4 = ((bf16[128,4,256]{2,1,0:T(4,128)(2,1)}), bf16[128,4,256]{2,1,0:T(4,128)(2,1)S(1)}, u32[]{:S(2)}, u32[]{:S(2)}) async-start(bf16[128,4,256]{2,1,0:T(4,128)(2,1)} %add_convert_fusion), calls=%async_computation.4 | async-start | bytes 524288 | tf_op jit(solution)/shard_map/all_to_all | solution.py:262
  100.1 0.0 copy-done.7
  100.1 2.2 %shard_map.82 = (bf16[512,1024]{1,0:T(8,128)(2,1)}, bf16[512,1024]{1,0:T(8,128)(2,1)}) custom-call(bf16[512,256]{1,0:T(8,128)(2,1)S(1)} %get-tuple-element.24.comb_ref, bf16[256,1024]{1,0:T(8,128)(2,1)S(1)} %get-tuple-element.25.so_ref, bf16[512,256]{1,0:T(8,128)(2,1)S(1)} %get-tuple-element.26.dlog_ref, bf16[1024,256]{1,0:T(8,128)(2,1)S(1)} %copy-done.7, ...), custom_call_target="tpu_custom_call" | custom-call | flops 805306368 | bytes 4456448 | tf_op jit(solution)/shard_map/pallas_call | solution.py:27
  102.2 10.4 %all-to-all-done.4 = bf16[128,4,256]{2,1,0:T(4,128)(2,1)S(1)} async-done(((bf16[128,4,256]{2,1,0:T(4,128)(2,1)}), bf16[128,4,256]{2,1,0:T(4,128)(2,1)S(1)}, u32[]{:S(2)}, u32[]{:S(2)}) %all-to-all-start.4) | async-done | bytes 262176 | tf_op jit(solution)/shard_map/all_to_all | solution.py:262
  112.7 0.8 convert_reduce_fusion
Async XLA Ops:
  0.6 1.2 %copy-start.2 = (bf16[1,512,1024]{2,1,0:T(8,128)(2,1)S(1)}, bf16[1,512,1024]{2,1,0:T(8,128)(2,1)}, u32[]{:S(2)}) copy-start(bf16[1,512,1024]{2,1,0:T(8,128)(2,1)} %param.5) | copy-start | bytes 3145732
  1.9 1.2 %copy-start.4 = (bf16[1,512,1024]{2,1,0:T(8,128)(2,1)S(1)}, bf16[1,512,1024]{2,1,0:T(8,128)(2,1)}, u32[]{:S(2)}) copy-start(bf16[1,512,1024]{2,1,0:T(8,128)(2,1)} %param.9) | copy-start | bytes 3145732
  3.1 1.0 copy-start.6
  4.1 44.1 %copy-start = (bf16[2,1024,1024]{2,1,0:T(8,128)(2,1)S(1)}, bf16[2,1024,1024]{2,1,0:T(8,128)(2,1)}, u32[]{:S(2)}) copy-start(bf16[2,1024,1024]{2,1,0:T(8,128)(2,1)} %win_ref.1) | copy-start | bytes 12582916
  4.1 44.1 %copy-start.1 = (bf16[2,1024,1024]{2,1,0:T(8,128)(2,1)S(1)}, bf16[2,1024,1024]{2,1,0:T(8,128)(2,1)}, u32[]{:S(2)}) copy-start(bf16[2,1024,1024]{2,1,0:T(8,128)(2,1)} %wout_ref.1) | copy-start | bytes 12582916
  6.6 2.1 %collective-permute-start = (bf16[256,1152]{1,0:T(8,128)(2,1)S(1)}, bf16[256,1152]{1,0:T(8,128)(2,1)S(1)}, u32[]{:S(2)}, u32[]{:S(2)}) collective-permute-start(bf16[256,1152]{1,0:T(8,128)(2,1)S(1)} %get-tuple-element.20), channel_id=1, source_target_pairs={{0,1},{1,0},{2,3},{3,2},{4,5},{5,4},{6,7},{7,6},{8,9},{9,8},{10,11... | collective-permute-start | bytes 1769480 | tf_op jit(solution)/shard_map/ppermute | solution.py:213
  48.2 38.8 %copy-start.3 = (bf16[1,512,1024]{2,1,0:T(8,128)(2,1)S(1)}, bf16[1,512,1024]{2,1,0:T(8,128)(2,1)}, u32[]{:S(2)}) copy-start(bf16[1,512,1024]{2,1,0:T(8,128)(2,1)} %param.5) | copy-start | bytes 3145732
  48.2 38.8 %copy-start.5 = (bf16[1,512,1024]{2,1,0:T(8,128)(2,1)S(1)}, bf16[1,512,1024]{2,1,0:T(8,128)(2,1)}, u32[]{:S(2)}) copy-start(bf16[1,512,1024]{2,1,0:T(8,128)(2,1)} %param.9) | copy-start | bytes 3145732
  55.8 44.2 %copy-start.7 = (bf16[1024,256]{1,0:T(8,128)(2,1)S(1)}, bf16[1024,256]{1,0:T(8,128)(2,1)}, u32[]{:S(2)}) copy-start(bf16[1024,256]{1,0:T(8,128)(2,1)} %par_ref.3) | copy-start | bytes 1572868
  85.0 2.0 %collective-permute-start.1 = (bf16[256,1152]{1,0:T(8,128)(2,1)S(1)}, bf16[256,1152]{1,0:T(8,128)(2,1)S(1)}, u32[]{:S(2)}, u32[]{:S(2)}) collective-permute-start(bf16[256,1152]{1,0:T(8,128)(2,1)S(1)} %bitcast.8), channel_id=1, source_target_pairs={{0,1},{1,0},{2,3},{3,2},{4,5},{5,4},{6,7},{7,6},{8,9},{9,8},{10,11... | collective-permute-start | bytes 1769480 | tf_op jit(solution)/shard_map/ppermute | solution.py:246
  88.9 1.6 %collective-permute-start.2 = (bf16[128,4,256]{2,1,0:T(4,128)(2,1)S(1)}, bf16[128,4,256]{2,1,0:T(4,128)(2,1)S(1)}, u32[]{:S(2)}, u32[]{:S(2)}) collective-permute-start(bf16[128,4,256]{2,1,0:T(4,128)(2,1)S(1)} %get-tuple-element.32), channel_id=1, source_target_pairs={{0,1},{1,0},{2,3},{3,2},{4,5},{5,4},{6,7},{7,6},{8,9},{9,8},{10,11... | collective-permute-start | bytes 786440 | tf_op jit(solution)/shard_map/ppermute | solution.py:255
  91.4 21.3 %all-to-all-start.4 = ((bf16[128,4,256]{2,1,0:T(4,128)(2,1)}), bf16[128,4,256]{2,1,0:T(4,128)(2,1)S(1)}, u32[]{:S(2)}, u32[]{:S(2)}) async-start(bf16[128,4,256]{2,1,0:T(4,128)(2,1)} %add_convert_fusion), calls=%async_computation.4 | async-start | bytes 524288 | tf_op jit(solution)/shard_map/all_to_all | solution.py:262

commit v2 on v1

v2 whole, which is shorter than its diff:
```python
import jax
import jax.numpy as jnp
from jax import lax
from jax.experimental import pallas as pl
from jax.experimental.pallas import tpu as pltpu
from jax.sharding import Mesh, PartitionSpec as P

BF = jnp.bfloat16
F32 = jnp.float32
AXES = ("x", "z", "y", "c")
ZY = ("z", "y")
PARTS = 4
STAT = 128
PARAMS = pltpu.CompilerParams(vmem_limit_bytes=24 * 1024 * 1024)


def dot(a, b, contract=((1,), (0,))):
    return lax.dot_general(a, b, (contract, ((), ())), preferred_element_type=F32)


def iota(shape, dim):
    return lax.broadcasted_iota(jnp.int32, shape, dim)


def call(body, outs, *args, flops=0, scratch=(), params=PARAMS):
    nbytes = sum(a.size * a.dtype.itemsize for a in args)
    nbytes += sum(o.size * o.dtype.itemsize for o in outs)
    return pl.pallas_call(
        body,
        out_shape=outs,
        in_specs=[pl.BlockSpec(memory_space=pltpu.VMEM)] * len(args),
        out_specs=[pl.BlockSpec(memory_space=pltpu.VMEM)] * len(outs),
        scratch_shapes=list(scratch),
        compiler_params=params,
        cost_estimate=pl.CostEstimate(flops=flops, bytes_accessed=nbytes, transcendentals=0),
    )(*args)


def split(value):
    high = value.astype(BF).astype(F32)
    return high, (value - high).astype(BF).astype(F32)


def stats(lane, first, second, third):
    return jnp.where(lane == 0, first, jnp.where(lane == 1, second, jnp.where(lane == 2, third, 0.0)))


def softmax_rows(logits):
    e = jnp.exp(logits - jnp.max(logits, axis=1, keepdims=True))
    return e / jnp.sum(e, axis=1, keepdims=True)


def swap_halves(value):
    return pltpu.roll(value, 4, 1)


def reduce_tokens(tok_hbm, cot_hbm, par_hbm, keep_ref, send_ref, logit_ref,
                  tok_ref, cot_ref, par_ref, comb_ref, sems):
    core = lax.axis_index("c")
    count, width = tok_ref.shape
    n = par_ref.shape[1]
    part = count // PARTS
    copies = [pltpu.make_async_copy(par_hbm, par_ref, sems.at[0])]
    for i in range(PARTS):
        rows = pl.ds(i * part, part)
        copies.append(pltpu.make_async_copy(tok_hbm.at[rows], tok_ref.at[rows], sems.at[1 + i]))
    copies.append(pltpu.make_async_copy(cot_hbm, cot_ref, sems.at[1 + PARTS]))
    for copy in copies:
        copy.start()
    copies[0].wait()
    par = par_ref[...]
    peak = None
    for i in range(PARTS):
        rows = pl.ds(i * part, part)
        copies[1 + i].wait()
        piece = dot(tok_ref[rows, :], par)
        logit_ref[rows, :] = piece
        comb_ref[rows, :] = softmax_rows(piece).astype(BF)
        high = jnp.max(piece, axis=0, keepdims=True)
        peak = high if peak is None else jnp.maximum(peak, high)
    refpoint = peak.astype(BF).astype(F32)
    dexp = jnp.exp(logit_ref[...] - refpoint).astype(BF)
    numer = dot(dexp, tok_ref[...], ((0,), (0,))).reshape(n // 8, 8, width)
    total = dot(dexp, jnp.ones((count, STAT), BF), ((0,), (0,)))
    diag = jnp.where(iota((n, n), 0) == iota((n, n), 1), refpoint, 0.0).astype(BF)
    point = dot(diag, jnp.ones((n, STAT), BF))
    high, low = split(total)
    side = stats(iota((n, STAT), 1), point, high, low).reshape(n // 8, 8, STAT)
    copies[1 + PARTS].wait()
    dslot = dot(comb_ref[...], cot_ref[...], ((0,), (0,))).reshape(n // 8, 8, width)
    upper = iota((1, 8, 1), 1) < 4
    zero = core == 0
    even = jnp.where(upper, numer, swap_halves(dslot)).astype(BF)
    odd = jnp.where(upper, swap_halves(numer), dslot).astype(BF)
    even_side = jnp.where(upper, side, 0.0).astype(BF)
    odd_side = jnp.where(upper, swap_halves(side), 0.0).astype(BF)
    keep_ref[:, :, :width] = jnp.where(zero, even, odd)
    send_ref[:, :, :width] = jnp.where(zero, odd, even)
    keep_ref[:, :, width:] = jnp.where(zero, even_side, odd_side)
    send_ref[:, :, width:] = jnp.where(zero, odd_side, even_side)


def merge_cores(a_ref, b_ref, out_ref):
    a, b = a_ref[...].astype(F32), b_ref[...].astype(F32)
    width = a.shape[2] - STAT
    ma, mb = a[:, :, width:width + 1], b[:, :, width:width + 1]
    top = jnp.maximum(ma, mb)
    sa, sb = jnp.exp(ma - top), jnp.exp(mb - top)
    out_ref[:, :, :width] = (sa * a[:, :, :width] + sb * b[:, :, :width]).astype(BF)
    ta = a[:, :, width + 1:width + 2] + a[:, :, width + 2:width + 3]
    tb = b[:, :, width + 1:width + 2] + b[:, :, width + 2:width + 3]
    high, low = split(sa * ta + sb * tb)
    lane = iota((a.shape[0], 8, STAT), 2)
    out_ref[:, :, width:] = stats(lane, top, high, low).astype(BF)


def merge_shards(in_ref, pay_ref, full_ref, side_ref):
    value = in_ref[...].astype(F32)
    width = value.shape[2] - STAT
    point = value[:, :, width:width + 1]
    top = jnp.max(point, axis=0)
    scale = jnp.exp(point - top[None])
    total = jnp.sum(scale * (value[:, :, width + 1:width + 2] + value[:, :, width + 2:width + 3]), axis=0)
    acc = jnp.sum(scale * value[:, :, :width], axis=0)
    slots = acc.shape[0] // 2
    first = iota((2 * slots, 1), 0) < slots
    full = acc / jnp.where(first, total, 1.0)
    full_ref[...] = full
    both = jnp.concatenate([total[:slots], total[:slots]], axis=0)
    side_ref[...] = jnp.where(iota((2 * slots, STAT), 1) == 0, top, both)
    pay_ref[...] = full.astype(BF)


def gelu_parts(u):
    cdf = 0.5 * (1.0 + lax.erf(u * 0.7071067811865476))
    pdf = 0.3989422804014327 * jnp.exp(-0.5 * u * u)
    return u * cdf, cdf + u * pdf


def experts(own_ref, a_ref, b_ref, c_ref, win_ref, wout_ref, *out_refs):
    blocks = [r[...].astype(F32) for r in (own_ref, a_ref, b_ref, c_ref)]
    fwd = jnp.concatenate([x[:4] for x in blocks], axis=0).astype(BF)
    bwd = jnp.concatenate([x[4:] for x in blocks], axis=0).astype(BF)
    rows = fwd.shape[0]
    out, back = 0.0, 0.0
    for e in range(win_ref.shape[0]):
        mine = (iota((rows, 1), 0) % 4) // 2 == e
        w1, w2 = win_ref[e], wout_ref[e]
        gelu, slope = gelu_parts(dot(fwd, w1))
        out += dot(jnp.where(mine, gelu, 0.0).astype(BF), w2)
        dact = dot(bwd, w2, ((1,), (1,)))
        back += dot(jnp.where(mine, dact * slope, 0.0).astype(BF), w1, ((1,), (1,)))
    for v, ref in enumerate(out_refs):
        ref[...] = jnp.concatenate([out[4 * v:4 * v + 4], back[4 * v:4 * v + 4]], axis=0)


def finish_slots(own_ref, a_ref, b_ref, c_ref, full_ref, side_ref, out_ref):
    value = (own_ref[...] + a_ref[...]) + (b_ref[...] + c_ref[...])
    width = value.shape[1]
    slots = value.shape[0] // 2
    first = iota((2 * slots, 1), 0) < slots
    side = side_ref[...]
    body = jnp.where(first, value, value / side[:, 1:2]).astype(BF)
    wide = body.astype(F32)
    shift = jnp.sum(full_ref[:slots, :] * wide[slots:, :], axis=1, keepdims=True)
    shift = jnp.concatenate([shift, shift], axis=0)
    high, low = split(shift)
    st = stats(iota((2 * slots, STAT), 1), side[:, 0:1], high, low).astype(BF)
    block = jnp.concatenate([body, st], axis=1)
    out_ref[...] = jnp.broadcast_to(block[None], out_ref.shape)


def token_grads(logit_ref, tok_ref, cot_ref, own_ref, oth_ref,
                keep_ref, send_ref, dlog_ref, dexp_ref, comb_ref, so_ref, sc_ref):
    core = lax.axis_index("c")
    logits, tok = logit_ref[...], tok_ref[...]
    n = logits.shape[1]
    width = tok.shape[1]
    zero = core == 0
    upper = iota((1, 8, 1), 1) < 4
    own, oth = own_ref[...].astype(F32), oth_ref[...].astype(F32)
    even, odd = jnp.where(zero, own, oth), jnp.where(zero, oth, own)
    first = jnp.where(upper, even, swap_halves(odd)).reshape(n, width + STAT)
    second = jnp.where(upper, swap_halves(even), odd).reshape(n, width + STAT)
    slot_out, scaled = first[:, :width].astype(BF), second[:, :width].astype(BF)
    so_ref[...] = slot_out
    sc_ref[...] = scaled
    side = first[:, width:].T
    point, shift = side[0:1, :], side[1:2, :] + side[2:3, :]
    comb = softmax_rows(logits)
    comb_ref[...] = comb.astype(BF)
    dexp = jnp.exp(logits - point).astype(BF)
    dexp_ref[...] = dexp
    dcomb = dot(cot_ref[...], slot_out, ((1,), (1,)))
    inner = dot(tok, scaled, ((1,), (1,)))
    dlog = comb * (dcomb - jnp.sum(comb * dcomb, axis=1, keepdims=True))
    dlog = (dlog + dexp.astype(F32) * (inner - shift)).astype(BF)
    dlog_ref[...] = dlog
    gp = dot(tok, dlog, ((0,), (0,))).reshape(width // 8, 8, n)
    left, right = gp[:, :, :n // 2], gp[:, :, n // 2:]
    even = jnp.where(upper, left, swap_halves(right)).astype(BF)
    odd = jnp.where(upper, swap_halves(left), right).astype(BF)
    keep_ref[...] = jnp.where(zero, even, odd)
    send_ref[...] = jnp.where(zero, odd, even)


def token_outputs(comb_ref, so_ref, dlog_ref, par_ref, dexp_ref, sc_ref, mixed_ref, grad_ref):
    mixed_ref[...] = dot(comb_ref[...], so_ref[...]).astype(BF)
    grad = dot(dlog_ref[...], par_ref[...], ((1,), (1,)))
    grad_ref[...] = (grad + dot(dexp_ref[...], sc_ref[...])).astype(BF)


def add_halves(a_ref, b_ref, out_ref):
    out_ref[...] = (a_ref[...].astype(F32) + b_ref[...].astype(F32)).astype(BF)


def sum_pieces(in_ref, out_ref):
    total = jnp.sum(in_ref[...].astype(F32), axis=0)
    half = total.shape[1]
    out_ref[:, :half] = total[:4]
    out_ref[:, half:] = total[4:]


def shifted(value, step, size):
    return lax.ppermute(value, "x", [(i, (i + step) % size) for i in range(size)])


def on_device(tokens, slot_parameters, w_in, w_out, grad_out):
    shape = jax.ShapeDtypeStruct
    tok, cot = tokens[0], grad_out[0]
    count, width = tok.shape
    n = slot_parameters.shape[1]
    videos = lax.axis_size("x")
    owners = lax.axis_size("z") * lax.axis_size("y")
    wide = width + STAT
    unit = 2 * count * width * n
    swap = [(0, 1), (1, 0)]

    vmem = pl.BlockSpec(memory_space=pltpu.VMEM)
    keep, send, logits = pl.pallas_call(
        reduce_tokens,
        out_shape=[shape((owners, 8, wide), BF), shape((owners, 8, wide), BF), shape((count, n), F32)],
        in_specs=[pl.BlockSpec(memory_space=pltpu.HBM)] * 3,
        out_specs=[vmem] * 3,
        scratch_shapes=[
            pltpu.VMEM((count, width), BF), pltpu.VMEM((count, width), BF),
            pltpu.VMEM((width, n), BF), pltpu.VMEM((count, n), BF),
            pltpu.SemaphoreType.DMA((PARTS + 2,)),
        ],
        compiler_params=PARAMS,
        cost_estimate=pl.CostEstimate(flops=4 * unit, bytes_accessed=4 << 20, transcendentals=0),
    )(*[pltpu.with_memory_space_constraint(a, pltpu.HBM) for a in (tok, cot, slot_parameters)])
    other = lax.ppermute(send, "c", swap)
    (merged,) = call(merge_cores, [shape((owners, 8, wide), BF)], keep, other, flops=40 * unit)
    shards = lax.all_to_all(merged, ZY, 0, 0, tiled=True)
    pay, full, side = call(
        merge_shards,
        [shape((8, width), BF), shape((8, width), F32), shape((8, STAT), F32)],
        shards,
    )
    behind = [shifted(pay, k, videos) for k in range(1, videos)]
    partial = call(
        experts, [shape((8, width), F32)] * videos, pay, *behind, w_in, w_out,
        flops=32 * videos * w_in.size,
    )
    parts = [shifted(partial[k], -k, videos) for k in range(1, videos)]
    (block,) = call(finish_slots, [shape((owners, 8, wide), BF)], partial[0], *parts, full, side)
    mine = lax.all_to_all(block, ZY, 0, 0, tiled=True)
    theirs = lax.ppermute(mine, "c", swap)

    gp_keep, gp_send, dlog, dexp, comb, slot_out, scaled = call(
        token_grads,
        [shape((width // 8, 8, n // 2), BF), shape((width // 8, 8, n // 2), BF),
         shape((count, n), BF), shape((count, n), BF), shape((count, n), BF),
         shape((n, width), BF), shape((n, width), BF)],
        logits, tok, cot, mine, theirs, flops=5 * unit,
    )
    gp_other = lax.ppermute(gp_send, "c", swap)
    mixed, grad_tokens = call(
        token_outputs,
        [shape((count, width), BF), shape((count, width), BF)],
        comb, slot_out, dlog, slot_parameters, dexp, scaled, flops=3 * unit,
    )
    (half,) = call(add_halves, [shape(gp_keep.shape, BF)], gp_keep, gp_other)
    pieces = lax.all_to_all(half, ("x", "z", "y"), 0, 0, tiled=True)
    (grad_params,) = call(sum_pieces, [shape((4, n), F32)], pieces)
    return mixed[None], grad_tokens[None], grad_params


def solution(mesh):
    sizes = dict(mesh.shape)
    grid = Mesh(mesh.devices.reshape(sizes["batch"], sizes["seq"] // 8, 4, 2), AXES)
    seq = ("z", "y", "c")
    placed = (
        P("x", seq, None),
        P(),
        P(seq, None, "x"),
        P(seq, "x", None),
        P("x", seq, None),
    )
    return jax.shard_map(
        on_device,
        mesh=grid,
        in_specs=placed,
        out_specs=(P("x", seq, None), P("x", seq, None), P(AXES, None)),
        check_vma=False,
    )
```

time: 115 us -> 107 us (0.930)
  blocking collectives: 67.7 us -> 51.2 us
  waiting for transfers between devices: 15.8 us -> 23.9 us
  starting transfers between devices: 9 us -> 16 us
  local copies, waits for them, and re-layouts: 3.51 us -> 0.02 us
  other arithmetic: 1.6 us -> 0 us
  Pallas kernels: 15.1 us -> 13.5 us
    all_to_all x4 -> x2, blocking collectives: 67.7 us -> 51.2 us  [the longest x1 30.9 us: on_device(): shards = lax.all_to_all(merged, ZY, 0, 0, tiled=True)]
    ppermute x0 -> x6, waiting for transfers between devices: none -> 8.04 us  [shifted(): lax.ppermute(value, 'x', [(i, (i + step) % size) for i in range(size)])]
    ppermute x0 -> x6, starting transfers between devices: none -> 6.23 us  [shifted(): lax.ppermute(value, 'x', [(i, (i + step) % size) for i in range(size)])]
    pallas_call x1, Pallas kernels: 7.58 us -> 4 us  [on_device(): pl.pallas_call(reduce_tokens, out_shape=[shape((owners, 8, wide), BF), sh...]
    unnamed x16 -> x10, local copies, waits for them, and re-layouts: 3.51 us -> 0.02 us
    pallas_call x6 -> x8, Pallas kernels: 7.51 us -> 9.5 us  [call(): pl.pallas_call(body, out_shape=outs, in_specs=[pl.BlockSpec(memory_space=...]
  transfers between devices with their start and end apart: 4 -> 10, of which waited for: 4 -> 10; matrix products, arithmetic and copies ran while one was open for 0% -> 0% of each run, Pallas kernels for 2% -> 2%
where the time goes in v2:
time: 107 us; the launch traced here: 105 us
  blocking collectives  51.2 us (48%)
  waiting for transfers between devices  23.9 us (22%)
  starting transfers between devices  16 us (15%)
  Pallas kernels  13.5 us (13%)
    all_to_all x1, blocking collectives, on_device(): shards = lax.all_to_all(merged, ZY, 0, 0, tiled=True)  30.9 us
    all_to_all x1, blocking collectives, on_device(): mine = lax.all_to_all(block, ZY, 0, 0, tiled=True)  20.3 us
    all_to_all x1, waiting for transfers between devices, on_device(): pieces = lax.all_to_all(half, ('x', 'z', 'y'), 0, 0, tiled=True)  10.4 us
    pallas_call x8, Pallas kernels, call(): pl.pallas_call(body, out_shape=outs, in_specs=[pl.BlockSpec(memory_space=...  9.5 us
    all_to_all x1, starting transfers between devices, on_device(): pieces = lax.all_to_all(half, ('x', 'z', 'y'), 0, 0, tiled=True)  9.49 us
    ppermute x6, waiting for transfers between devices, shifted(): lax.ppermute(value, 'x', [(i, (i + step) % size) for i in range(size)])  8.04 us
    ppermute x6, starting transfers between devices, shifted(): lax.ppermute(value, 'x', [(i, (i + step) % size) for i in range(size)])  6.23 us
    pallas_call x1, Pallas kernels, on_device(): pl.pallas_call(reduce_tokens, out_shape=[shape((owners, 8, wide), BF), sh...  4 us
  transfers between devices with their start and end apart: 10, of which 10 were waited for; matrix products, arithmetic and copies ran while one was open for 0% of the time, Pallas kernels for 2%

profile of v2, /device:TPU:6, one launch (start us, length us, event | category | flops | bytes accessed | tf_op | source)
XLA Modules:
  0.0 105.4 jit_solution(13246968248033038852)
XLA Ops:
  0.6 4.0 %shard_map.76 = (bf16[32,8,1152]{2,1,0:T(8,128)(2,1)S(1)}, bf16[32,8,1152]{2,1,0:T(8,128)(2,1)S(1)}, f32[512,256]{1,0:T(8,128)S(1)}) custom-call(bf16[512,1024]{1,0:T(8,128)(2,1)} %bitcast.4, bf16[512,1024]{1,0:T(8,128)(2,1)} %bitcast.6, bf16[1024,256]{1,0:T(8,128)(2,1)} %par_ref.1), custom_call_target="tpu_custom_call" | custom-call | flops 1073741824 | bytes 4194304 | tf_op jit(solution)/shard_map/pallas_call | solution.py:240
  4.6 0.1 collective-permute-start
  4.7 2.0 %collective-permute-done.b_ref = bf16[32,8,1152]{2,1,0:T(8,128)(2,1)S(1)} collective-permute-done((bf16[32,8,1152]{2,1,0:T(8,128)(2,1)S(1)}, bf16[32,8,1152]{2,1,0:T(8,128)(2,1)S(1)}, u32[]{:S(2)}, u32[]{:S(2)}) %collective-permute-start) | collective-permute-done | bytes 589856 | tf_op jit(solution)/shard_map/ppermute | solution.py:253
  6.7 0.0 copy-start
  6.7 0.0 copy-start.1
  6.7 0.5 shard_map.77
  7.3 30.9 %all_to_all.15.in_ref = bf16[32,8,1152]{2,1,0:T(8,128)(2,1)S(1)} all-to-all(bf16[32,8,1152]{2,1,0:T(8,128)(2,1)S(1)} %shard_map.77), channel_id=1, replica_groups=mesh['x'=4,'z'=8,'y'=4,'c'=2] {'z','y'}, dimensions={0} | all-to-all | bytes 1179648 | tf_op jit(solution)/shard_map/all_to_all | solution.py:255
  38.2 0.3 shard_map.78
  38.4 0.0 copy-start.2
  38.5 0.0 copy-start.3
  38.5 0.6 collective-permute-start.1
  39.0 2.4 %collective-permute-start.2 = (bf16[8,1024]{1,0:T(8,128)(2,1)S(1)}, bf16[8,1024]{1,0:T(8,128)(2,1)S(1)}, u32[]{:S(2)}, u32[]{:S(2)}) collective-permute-start(bf16[8,1024]{1,0:T(8,128)(2,1)S(1)} %get-tuple-element.25.own_ref), channel_id=1, source_target_pairs={{0,128},{64,192},{128,0},{192,64},{1,129},{65,193},{129,1},{193,65... | collective-permute-start | bytes 49160 | tf_op jit(solution)/shard_map/ppermute | solution.py:225
  41.4 0.0 collective-permute-start.3
  41.4 0.8 collective-permute-done.1.a_ref
  42.3 2.0 %collective-permute-done.2.b_ref = bf16[8,1024]{1,0:T(8,128)(2,1)S(1)} collective-permute-done((bf16[8,1024]{1,0:T(8,128)(2,1)S(1)}, bf16[8,1024]{1,0:T(8,128)(2,1)S(1)}, u32[]{:S(2)}, u32[]{:S(2)}) %collective-permute-start.2) | collective-permute-done | bytes 16416 | tf_op jit(solution)/shard_map/ppermute | solution.py:225
  44.3 2.1 %collective-permute-done.3.c_ref = bf16[8,1024]{1,0:T(8,128)(2,1)S(1)} collective-permute-done((bf16[8,1024]{1,0:T(8,128)(2,1)S(1)}, bf16[8,1024]{1,0:T(8,128)(2,1)S(1)}, u32[]{:S(2)}, u32[]{:S(2)}) %collective-permute-start.3) | collective-permute-done | bytes 16416 | tf_op jit(solution)/shard_map/ppermute | solution.py:225
  46.4 0.0 copy-done
  46.4 0.0 copy-done.1
  46.4 3.4 %shard_map.79 = (f32[8,1024]{1,0:T(8,128)S(1)}, f32[8,1024]{1,0:T(8,128)S(1)}, f32[8,1024]{1,0:T(8,128)S(1)}, f32[8,1024]{1,0:T(8,128)S(1)}) custom-call(bf16[8,1024]{1,0:T(8,128)(2,1)S(1)} %get-tuple-element.25.own_ref, bf16[8,1024]{1,0:T(8,128)(2,1)S(1)} %collective-permute-done.1.a_ref, bf16[8,1024]{1,0:T(8,128)(2,1)S(1)} %collective-permute-done.2.b_ref, ...), custom_call_target="tpu_custom_call" | custom-call | flops 268435456 | bytes 8585216 | tf_op jit(solution)/shard_map/pallas_call | solution.py:28
  49.8 0.0 copy-start.4
  49.8 0.0 collective-permute-start.4
  49.8 2.0 %collective-permute-start.5 = (f32[8,1024]{1,0:T(8,128)S(1)}, f32[8,1024]{1,0:T(8,128)S(1)}, u32[]{:S(2)}, u32[]{:S(2)}) collective-permute-start(f32[8,1024]{1,0:T(8,128)S(1)} %get-tuple-element.28), channel_id=1, source_target_pairs={{0,128},{64,192},{128,0},{192,64},{1,129},{65,193},{129,1},{193,65... | collective-permute-start | bytes 98312 | tf_op jit(solution)/shard_map/ppermute | solution.py:225
  51.9 1.2 %collective-permute-start.6 = (f32[8,1024]{1,0:T(8,128)S(1)}, f32[8,1024]{1,0:T(8,128)S(1)}, u32[]{:S(2)}, u32[]{:S(2)}) collective-permute-start(f32[8,1024]{1,0:T(8,128)S(1)} %get-tuple-element.29), channel_id=1, source_target_pairs={{0,64},{64,128},{128,192},{192,0},{1,65},{65,129},{129,193},{193,1... | collective-permute-start | bytes 98312 | tf_op jit(solution)/shard_map/ppermute | solution.py:225
  53.0 1.9 %collective-permute-done.4.a_ref = f32[8,1024]{1,0:T(8,128)S(1)} collective-permute-done((f32[8,1024]{1,0:T(8,128)S(1)}, f32[8,1024]{1,0:T(8,128)S(1)}, u32[]{:S(2)}, u32[]{:S(2)}) %collective-permute-start.4) | collective-permute-done | bytes 32800 | tf_op jit(solution)/shard_map/ppermute | solution.py:225
  54.9 0.4 collective-permute-done.5.b_ref
  55.3 0.8 collective-permute-done.6.c_ref
  56.1 0.3 shard_map.80
  56.4 20.3 %all_to_all.16.own_ref = bf16[32,8,1152]{2,1,0:T(8,128)(2,1)S(1)} all-to-all(bf16[32,8,1152]{2,1,0:T(8,128)(2,1)S(1)} %shard_map.80), channel_id=1, replica_groups=mesh['x'=4,'z'=8,'y'=4,'c'=2] {'z','y'}, dimensions={0} | all-to-all | bytes 1179648 | tf_op jit(solution)/shard_map/all_to_all | solution.py:268
  76.7 0.0 collective-permute-start.7
  76.7 2.0 %collective-permute-done.7.oth_ref = bf16[32,8,1152]{2,1,0:T(8,128)(2,1)S(1)} collective-permute-done((bf16[32,8,1152]{2,1,0:T(8,128)(2,1)S(1)}, bf16[32,8,1152]{2,1,0:T(8,128)(2,1)S(1)}, u32[]{:S(2)}, u32[]{:S(2)}) %collective-permute-start.7) | collective-permute-done | bytes 589856 | tf_op jit(solution)/shard_map/ppermute | solution.py:269
  78.7 0.0 copy-done.2
  78.7 0.0 copy-done.3
  78.7 1.4 %shard_map.81 = (bf16[128,8,128]{2,1,0:T(8,128)(2,1)S(1)}, bf16[128,8,128]{2,1,0:T(8,128)(2,1)S(1)}, bf16[512,256]{1,0:T(8,128)(2,1)S(1)}, bf16[512,256]{1,0:T(8...) custom-call(f32[512,256]{1,0:T(8,128)S(1)} %get-tuple-element.22.logit_re, ...), custom_call_target="tpu_custom_call" | custom-call | flops 1342177280 | bytes 6160384 | tf_op jit(solution)/shard_map/pallas_call | solution.py:28
  80.1 0.2 collective-permute-start.8
  80.4 1.4 %collective-permute-done.8.b_ref = bf16[128,8,128]{2,1,0:T(8,128)(2,1)S(1)} collective-permute-done((bf16[128,8,128]{2,1,0:T(8,128)(2,1)S(1)}, bf16[128,8,128]{2,1,0:T(8,128)(2,1)S(1)}, u32[]{:S(2)}, u32[]{:S(2)}) %collective-permute-start.8) | collective-permute-done | bytes 262176 | tf_op jit(solution)/shard_map/ppermute | solution.py:278
  81.8 0.8 shard_map.83
  82.5 9.5 %all-to-all-start.2 = ((bf16[128,8,128]{2,1,0:T(8,128)(2,1)}), bf16[128,8,128]{2,1,0:T(8,128)(2,1)S(1)}, u32[]{:S(2)}, u32[]{:S(2)}) async-start(bf16[128,8,128]{2,1,0:T(8,128)(2,1)} %shard_map.83), calls=%async_computation.2 | async-start | bytes 524288 | tf_op jit(solution)/shard_map/all_to_all | solution.py:285
  92.0 0.0 copy-done.4
  92.0 2.2 %shard_map.82 = (bf16[512,1024]{1,0:T(8,128)(2,1)}, bf16[512,1024]{1,0:T(8,128)(2,1)}) custom-call(bf16[512,256]{1,0:T(8,128)(2,1)S(1)} %get-tuple-element.32.comb_ref, bf16[256,1024]{1,0:T(8,128)(2,1)S(1)} %get-tuple-element.33.so_ref, bf16[512,256]{1,0:T(8,128)(2,1)S(1)} %get-tuple-element.34.dlog_ref, bf16[1024,256]{1,0:T(8,128)(2,1)S(1)} %copy-done.4, ...), custom_call_target="tpu_custom_call" | custom-call | flops 805306368 | bytes 4456448 | tf_op jit(solution)/shard_map/pallas_call | solution.py:28
  94.2 10.4 %all-to-all-done.2.in_ref = bf16[128,8,128]{2,1,0:T(8,128)(2,1)S(1)} async-done(((bf16[128,8,128]{2,1,0:T(8,128)(2,1)}), bf16[128,8,128]{2,1,0:T(8,128)(2,1)S(1)}, u32[]{:S(2)}, u32[]{:S(2)}) %all-to-all-start.2) | async-done | bytes 262176 | tf_op jit(solution)/shard_map/all_to_all | solution.py:285
  104.6 0.7 shard_map.84
Async XLA Ops:
  4.6 2.1 %collective-permute-start = (bf16[32,8,1152]{2,1,0:T(8,128)(2,1)S(1)}, bf16[32,8,1152]{2,1,0:T(8,128)(2,1)S(1)}, u32[]{:S(2)}, u32[]{:S(2)}) collective-permute-start(bf16[32,8,1152]{2,1,0:T(8,128)(2,1)S(1)} %get-tuple-element.24), channel_id=1, source_target_pairs={{0,1},{1,0},{2,3},{3,2},{4,5},{5,4},{6,7},{7,6},{8,9},{9,8},{10,11... | collective-permute-start | bytes 1769480 | tf_op jit(solution)/shard_map/ppermute | solution.py:253
  6.7 39.7 %copy-start = (bf16[2,1024,1024]{2,1,0:T(8,128)(2,1)S(1)}, bf16[2,1024,1024]{2,1,0:T(8,128)(2,1)}, u32[]{:S(2)}) copy-start(bf16[2,1024,1024]{2,1,0:T(8,128)(2,1)} %win_ref.1) | copy-start | bytes 12582916
  6.7 39.7 %copy-start.1 = (bf16[2,1024,1024]{2,1,0:T(8,128)(2,1)S(1)}, bf16[2,1024,1024]{2,1,0:T(8,128)(2,1)}, u32[]{:S(2)}) copy-start(bf16[2,1024,1024]{2,1,0:T(8,128)(2,1)} %wout_ref.1) | copy-start | bytes 12582916
  38.4 40.3 %copy-start.2 = (bf16[1,512,1024]{2,1,0:T(8,128)(2,1)S(1)}, bf16[1,512,1024]{2,1,0:T(8,128)(2,1)}, u32[]{:S(2)}) copy-start(bf16[1,512,1024]{2,1,0:T(8,128)(2,1)} %param.5) | copy-start | bytes 3145732
  38.5 40.3 %copy-start.3 = (bf16[1,512,1024]{2,1,0:T(8,128)(2,1)S(1)}, bf16[1,512,1024]{2,1,0:T(8,128)(2,1)}, u32[]{:S(2)}) copy-start(bf16[1,512,1024]{2,1,0:T(8,128)(2,1)} %param.9) | copy-start | bytes 3145732
  38.5 3.8 %collective-permute-start.1 = (bf16[8,1024]{1,0:T(8,128)(2,1)S(1)}, bf16[8,1024]{1,0:T(8,128)(2,1)S(1)}, u32[]{:S(2)}, u32[]{:S(2)}) collective-permute-start(bf16[8,1024]{1,0:T(8,128)(2,1)S(1)} %get-tuple-element.25.own_ref), channel_id=1, source_target_pairs={{0,64},{64,128},{128,192},{192,0},{1,65},{65,129},{129,193},{193,1... | collective-permute-start | bytes 49160 | tf_op jit(solution)/shard_map/ppermute | solution.py:225
  39.0 5.2 %collective-permute-start.2 = (bf16[8,1024]{1,0:T(8,128)(2,1)S(1)}, bf16[8,1024]{1,0:T(8,128)(2,1)S(1)}, u32[]{:S(2)}, u32[]{:S(2)}) collective-permute-start(bf16[8,1024]{1,0:T(8,128)(2,1)S(1)} %get-tuple-element.25.own_ref), channel_id=1, source_target_pairs={{0,128},{64,192},{128,0},{192,64},{1,129},{65,193},{129,1},{193,65... | collective-permute-start | bytes 49160 | tf_op jit(solution)/shard_map/ppermute | solution.py:225
  41.4 4.9 %collective-permute-start.3 = (bf16[8,1024]{1,0:T(8,128)(2,1)S(1)}, bf16[8,1024]{1,0:T(8,128)(2,1)S(1)}, u32[]{:S(2)}, u32[]{:S(2)}) collective-permute-start(bf16[8,1024]{1,0:T(8,128)(2,1)S(1)} %get-tuple-element.25.own_ref), channel_id=1, source_target_pairs={{0,192},{64,0},{128,64},{192,128},{1,193},{65,1},{129,65},{193,129... | collective-permute-start | bytes 49160 | tf_op jit(solution)/shard_map/ppermute | solution.py:225
  49.8 42.3 %copy-start.4 = (bf16[1024,256]{1,0:T(8,128)(2,1)S(1)}, bf16[1024,256]{1,0:T(8,128)(2,1)}, u32[]{:S(2)}) copy-start(bf16[1024,256]{1,0:T(8,128)(2,1)} %par_ref.1) | copy-start | bytes 1572868
  49.8 5.1 %collective-permute-start.4 = (f32[8,1024]{1,0:T(8,128)S(1)}, f32[8,1024]{1,0:T(8,128)S(1)}, u32[]{:S(2)}, u32[]{:S(2)}) collective-permute-start(f32[8,1024]{1,0:T(8,128)S(1)} %get-tuple-element.27), channel_id=1, source_target_pairs={{0,192},{64,0},{128,64},{192,128},{1,193},{65,1},{129,65},{193,129... | collective-permute-start | bytes 98312 | tf_op jit(solution)/shard_map/ppermute | solution.py:225
  49.8 5.5 %collective-permute-start.5 = (f32[8,1024]{1,0:T(8,128)S(1)}, f32[8,1024]{1,0:T(8,128)S(1)}, u32[]{:S(2)}, u32[]{:S(2)}) collective-permute-start(f32[8,1024]{1,0:T(8,128)S(1)} %get-tuple-element.28), channel_id=1, source_target_pairs={{0,128},{64,192},{128,0},{192,64},{1,129},{65,193},{129,1},{193,65... | collective-permute-start | bytes 98312 | tf_op jit(solution)/shard_map/ppermute | solution.py:225
  51.9 4.3 %collective-permute-start.6 = (f32[8,1024]{1,0:T(8,128)S(1)}, f32[8,1024]{1,0:T(8,128)S(1)}, u32[]{:S(2)}, u32[]{:S(2)}) collective-permute-start(f32[8,1024]{1,0:T(8,128)S(1)} %get-tuple-element.29), channel_id=1, source_target_pairs={{0,64},{64,128},{128,192},{192,0},{1,65},{65,129},{129,193},{193,1... | collective-permute-start | bytes 98312 | tf_op jit(solution)/shard_map/ppermute | solution.py:225
  76.7 2.0 %collective-permute-start.7 = (bf16[32,8,1152]{2,1,0:T(8,128)(2,1)S(1)}, bf16[32,8,1152]{2,1,0:T(8,128)(2,1)S(1)}, u32[]{:S(2)}, u32[]{:S(2)}) collective-permute-start(bf16[32,8,1152]{2,1,0:T(8,128)(2,1)S(1)} %all_to_all.16.own_ref), channel_id=1, source_target_pairs={{0,1},{1,0},{2,3},{3,2},{4,5},{5,4},{6,7},{7,6},{8,9},{9,8},{10,11... | collective-permute-start | bytes 1769480 | tf_op jit(solution)/shard_map/ppermute | solution.py:269
  80.1 1.6 %collective-permute-start.8 = (bf16[128,8,128]{2,1,0:T(8,128)(2,1)S(1)}, bf16[128,8,128]{2,1,0:T(8,128)(2,1)S(1)}, u32[]{:S(2)}, u32[]{:S(2)}) collective-permute-start(bf16[128,8,128]{2,1,0:T(8,128)(2,1)S(1)} %get-tuple-element.40), channel_id=1, source_target_pairs={{0,1},{1,0},{2,3},{3,2},{4,5},{5,4},{6,7},{7,6},{8,9},{9,8},{10,11... | collective-permute-start | bytes 786440 | tf_op jit(solution)/shard_map/ppermute | solution.py:278
  82.5 22.1 %all-to-all-start.2 = ((bf16[128,8,128]{2,1,0:T(8,128)(2,1)}), bf16[128,8,128]{2,1,0:T(8,128)(2,1)S(1)}, u32[]{:S(2)}, u32[]{:S(2)}) async-start(bf16[128,8,128]{2,1,0:T(8,128)(2,1)} %shard_map.83), calls=%async_computation.2 | async-start | bytes 524288 | tf_op jit(solution)/shard_map/all_to_all | solution.py:285

commit v3 on v2

--- a/solution.py
+++ b/solution.py
@@ -1,3 +1,5 @@
+import math
+
 import jax
 import jax.numpy as jnp
 from jax import lax
@@ -9,7 +11,7 @@
 F32 = jnp.float32
 AXES = ("x", "z", "y", "c")
 ZY = ("z", "y")
-PARTS = 4
+PARTS = 2
 STAT = 128
 PARAMS = pltpu.CompilerParams(vmem_limit_bytes=24 * 1024 * 1024)
 
@@ -24,7 +26,7 @@
 
 def call(body, outs, *args, flops=0, scratch=(), params=PARAMS):
     nbytes = sum(a.size * a.dtype.itemsize for a in args)
-    nbytes += sum(o.size * o.dtype.itemsize for o in outs)
+    nbytes += sum(math.prod(o.shape) * 4 for o in outs)
     return pl.pallas_call(
         body,
         out_shape=outs,
@@ -94,34 +96,47 @@
     odd = jnp.where(upper, swap_halves(numer), dslot).astype(BF)
     even_side = jnp.where(upper, side, 0.0).astype(BF)
     odd_side = jnp.where(upper, swap_halves(side), 0.0).astype(BF)
-    keep_ref[:, :, :width] = jnp.where(zero, even, odd)
-    send_ref[:, :, :width] = jnp.where(zero, odd, even)
-    keep_ref[:, :, width:] = jnp.where(zero, even_side, odd_side)
-    send_ref[:, :, width:] = jnp.where(zero, odd_side, even_side)
+    even = jnp.concatenate([even, even_side], axis=2)
+    odd = jnp.concatenate([odd, odd_side], axis=2)
+    for ref, value in ((keep_ref, jnp.where(zero, even, odd)), (send_ref, jnp.where(zero, odd, even))):
+        value = value.reshape(n // 8 // ref.shape[0], *ref.shape[:1], 8, width + STAT)
+        for y in range(ref.shape[0]):
+            ref[y] = value[:, y]
+
+
+def merge(parts):
+    width = parts[0].shape[-1] - STAT
+    points = [p[..., width:width + 1] for p in parts]
+    top = points[0]
+    for point in points[1:]:
+        top = jnp.maximum(top, point)
+    body, total = 0.0, 0.0
+    for part, point in zip(parts, points):
+        scale = jnp.exp(point - top)
+        body += scale * part[..., :width]
+        total += scale * (part[..., width + 1:width + 2] + part[..., width + 2:width + 3])
+    return body, top, total
+
+
+def store_merged(parts, out_ref):
+    body, top, total = merge(parts)
+    width = body.shape[-1]
+    high, low = split(total)
+    out_ref[..., :width] = body.astype(BF)
+    lane = iota(body.shape[:-1] + (STAT,), body.ndim - 1)
+    out_ref[..., width:] = stats(lane, top, high, low).astype(BF)
 
 
 def merge_cores(a_ref, b_ref, out_ref):
-    a, b = a_ref[...].astype(F32), b_ref[...].astype(F32)
-    width = a.shape[2] - STAT
-    ma, mb = a[:, :, width:width + 1], b[:, :, width:width + 1]
-    top = jnp.maximum(ma, mb)
-    sa, sb = jnp.exp(ma - top), jnp.exp(mb - top)
-    out_ref[:, :, :width] = (sa * a[:, :, :width] + sb * b[:, :, :width]).astype(BF)
-    ta = a[:, :, width + 1:width + 2] + a[:, :, width + 2:width + 3]
-    tb = b[:, :, width + 1:width + 2] + b[:, :, width + 2:width + 3]
-    high, low = split(sa * ta + sb * tb)
-    lane = iota((a.shape[0], 8, STAT), 2)
-    out_ref[:, :, width:] = stats(lane, top, high, low).astype(BF)
+    store_merged([a_ref[...].astype(F32), b_ref[...].astype(F32)], out_ref)
+
+
+def merge_columns(in_ref, out_ref):
+    store_merged([in_ref[i].astype(F32) for i in range(in_ref.shape[0])], out_ref)
 
 
 def merge_shards(in_ref, pay_ref, full_ref, side_ref):
-    value = in_ref[...].astype(F32)
-    width = value.shape[2] - STAT
-    point = value[:, :, width:width + 1]
-    top = jnp.max(point, axis=0)
-    scale = jnp.exp(point - top[None])
-    total = jnp.sum(scale * (value[:, :, width + 1:width + 2] + value[:, :, width + 2:width + 3]), axis=0)
-    acc = jnp.sum(scale * value[:, :, :width], axis=0)
+    acc, top, total = merge([in_ref[i].astype(F32) for i in range(in_ref.shape[0])])
     slots = acc.shape[0] // 2
     first = iota((2 * slots, 1), 0) < slots
     full = acc / jnp.where(first, total, 1.0)
@@ -151,11 +166,12 @@
         dact = dot(bwd, w2, ((1,), (1,)))
         back += dot(jnp.where(mine, dact * slope, 0.0).astype(BF), w1, ((1,), (1,)))
     for v, ref in enumerate(out_refs):
-        ref[...] = jnp.concatenate([out[4 * v:4 * v + 4], back[4 * v:4 * v + 4]], axis=0)
+        ref[...] = jnp.concatenate([out[4 * v:4 * v + 4], back[4 * v:4 * v + 4]], axis=0).astype(BF)
 
 
 def finish_slots(own_ref, a_ref, b_ref, c_ref, full_ref, side_ref, out_ref):
-    value = (own_ref[...] + a_ref[...]) + (b_ref[...] + c_ref[...])
+    own, a, b, c = [r[...].astype(F32) for r in (own_ref, a_ref, b_ref, c_ref)]
+    value = (own + a) + (b + c)
     width = value.shape[1]
     slots = value.shape[0] // 2
     first = iota((2 * slots, 1), 0) < slots
@@ -200,8 +216,8 @@
     left, right = gp[:, :, :n // 2], gp[:, :, n // 2:]
     even = jnp.where(upper, left, swap_halves(right)).astype(BF)
     odd = jnp.where(upper, swap_halves(left), right).astype(BF)
-    keep_ref[...] = jnp.where(zero, even, odd)
-    send_ref[...] = jnp.where(zero, odd, even)
+    keep_ref[...] = jnp.where(zero, even, odd).reshape(keep_ref.shape)
+    send_ref[...] = jnp.where(zero, odd, even).reshape(send_ref.shape)
 
 
 def token_outputs(comb_ref, so_ref, dlog_ref, par_ref, dexp_ref, sc_ref, mixed_ref, grad_ref):
@@ -210,13 +226,23 @@
     grad_ref[...] = (grad + dot(dexp_ref[...], sc_ref[...])).astype(BF)
 
 
-def add_halves(a_ref, b_ref, out_ref):
-    out_ref[...] = (a_ref[...].astype(F32) + b_ref[...].astype(F32)).astype(BF)
+def add_halves(a_ref, b_ref, *out_refs):
+    here = lax.axis_index("x")
+    for k, ref in enumerate(out_refs):
+        to = lax.rem(here + k, len(out_refs))
+        ref[...] = (a_ref[to].astype(F32) + b_ref[to].astype(F32)).astype(BF)
+
+
+def add_rows(own_ref, a_ref, b_ref, c_ref, after_ref, out_ref):
+    del after_ref
+    pairs = [r[...].astype(F32) for r in (own_ref, a_ref, b_ref, c_ref)]
+    out_ref[...] = ((pairs[0] + pairs[1]) + (pairs[2] + pairs[3])).astype(BF)
 
 
 def sum_pieces(in_ref, out_ref):
-    total = jnp.sum(in_ref[...].astype(F32), axis=0)
-    half = total.shape[1]
+    value = in_ref[...].astype(F32)
+    count, rows, half = value.shape
+    total = jnp.sum(jnp.sum(value.reshape(count // 8, 8, rows, half), axis=0), axis=0)
     out_ref[:, :half] = total[:4]
     out_ref[:, half:] = total[4:]
 
@@ -231,7 +257,8 @@
     count, width = tok.shape
     n = slot_parameters.shape[1]
     videos = lax.axis_size("x")
-    owners = lax.axis_size("z") * lax.axis_size("y")
+    depth, rows_y = lax.axis_size("z"), lax.axis_size("y")
+    owners = depth * rows_y
     wide = width + STAT
     unit = 2 * count * width * n
     swap = [(0, 1), (1, 0)]
@@ -239,7 +266,7 @@
     vmem = pl.BlockSpec(memory_space=pltpu.VMEM)
     keep, send, logits = pl.pallas_call(
         reduce_tokens,
-        out_shape=[shape((owners, 8, wide), BF), shape((owners, 8, wide), BF), shape((count, n), F32)],
+        out_shape=[shape((rows_y, depth, 8, wide), BF), shape((rows_y, depth, 8, wide), BF), shape((count, n), F32)],
         in_specs=[pl.BlockSpec(memory_space=pltpu.HBM)] * 3,
         out_specs=[vmem] * 3,
         scratch_shapes=[
@@ -251,8 +278,10 @@
         cost_estimate=pl.CostEstimate(flops=4 * unit, bytes_accessed=4 << 20, transcendentals=0),
     )(*[pltpu.with_memory_space_constraint(a, pltpu.HBM) for a in (tok, cot, slot_parameters)])
     other = lax.ppermute(send, "c", swap)
-    (merged,) = call(merge_cores, [shape((owners, 8, wide), BF)], keep, other, flops=40 * unit)
-    shards = lax.all_to_all(merged, ZY, 0, 0, tiled=True)
+    (merged,) = call(merge_cores, [shape(keep.shape, BF)], keep, other, flops=40 * unit)
+    columns = lax.all_to_all(merged, "y", 0, 0, tiled=True)
+    (merged,) = call(merge_columns, [shape((depth, 8, wide), BF)], columns)
+    shards = lax.all_to_all(merged, "z", 0, 0, tiled=True)
     pay, full, side = call(
         merge_shards,
         [shape((8, width), BF), shape((8, width), F32), shape((8, STAT), F32)],
@@ -260,7 +289,7 @@
     )
     behind = [shifted(pay, k, videos) for k in range(1, videos)]
     partial = call(
-        experts, [shape((8, width), F32)] * videos, pay, *behind, w_in, w_out,
+        experts, [shape((8, width), BF)] * videos, pay, *behind, w_in, w_out,
         flops=32 * videos * w_in.size,
     )
     parts = [shifted(partial[k], -k, videos) for k in range(1, videos)]
@@ -270,7 +299,7 @@
 
     gp_keep, gp_send, dlog, dexp, comb, slot_out, scaled = call(
         token_grads,
-        [shape((width // 8, 8, n // 2), BF), shape((width // 8, 8, n // 2), BF),
+        [shape((videos, owners, 8, n // 2), BF), shape((videos, owners, 8, n // 2), BF),
          shape((count, n), BF), shape((count, n), BF), shape((count, n), BF),
          shape((n, width), BF), shape((n, width), BF)],
         logits, tok, cot, mine, theirs, flops=5 * unit,
@@ -281,8 +310,16 @@
         [shape((count, width), BF), shape((count, width), BF)],
         comb, slot_out, dlog, slot_parameters, dexp, scaled, flops=3 * unit,
     )
-    (half,) = call(add_halves, [shape(gp_keep.shape, BF)], gp_keep, gp_other)
-    pieces = lax.all_to_all(half, ("x", "z", "y"), 0, 0, tiled=True)
+    quarters = call(add_halves, [shape(gp_keep.shape[1:], BF)] * videos, gp_keep, gp_other)
+    arrived = [shifted(quarters[k], k, videos) for k in range(1, videos)]
+    half = pl.pallas_call(
+        add_rows,
+        out_shape=shape(gp_keep.shape[1:], BF),
+        in_specs=[vmem] * videos + [pl.BlockSpec(memory_space=pltpu.HBM)],
+        out_specs=vmem,
+        compiler_params=PARAMS,
+    )(quarters[0], *arrived, pltpu.with_memory_space_constraint(mixed, pltpu.HBM))
+    pieces = lax.all_to_all(half, ZY, 0, 0, tiled=True)
     (grad_params,) = call(sum_pieces, [shape((4, n), F32)], pieces)
     return mixed[None], grad_tokens[None], grad_params
 

time: 107 us -> 104 us (0.972)
  blocking collectives: 51.2 us -> 64.1 us
  waiting for transfers between devices: 23.9 us -> 13.7 us
  starting transfers between devices: 16 us -> 11.6 us
    all_to_all x1 -> x3, blocking collectives: 30.9 us -> 46.6 us  [the longest x1 17.5 us: on_device(): shards = lax.all_to_all(merged, 'z', 0, 0, tiled=True)]
    all_to_all x1 -> x0, waiting for transfers between devices: 10.4 us -> none  [on_device(): pieces = lax.all_to_all(half, ('x', 'z', 'y'), 0, 0, tiled=True)]
    all_to_all x1 -> x0, starting transfers between devices: 9.49 us -> none  [on_device(): pieces = lax.all_to_all(half, ('x', 'z', 'y'), 0, 0, tiled=True)]
    ppermute x6 -> x9, starting transfers between devices: 6.23 us -> 11.2 us  [shifted(): lax.ppermute(value, 'x', [(i, (i + step) % size) for i in range(size)])]
    all_to_all x1, blocking collectives: 20.3 us -> 17.5 us  [on_device(): mine = lax.all_to_all(block, ZY, 0, 0, tiled=True)]
    pallas_call x1 -> x2, Pallas kernels: 4 us -> 3.47 us  [the longest x1 3.44 us: on_device(): pl.pallas_call(reduce_tokens, out_shape=[shape((rows_y, depth, 8, wide),...]
    pallas_call x8 -> x9, Pallas kernels: 9.5 us -> 9.01 us  [call(): pl.pallas_call(body, out_shape=outs, in_specs=[pl.BlockSpec(memory_space=...]
    ppermute x6 -> x9, waiting for transfers between devices: 8.04 us -> 8.27 us  [shifted(): lax.ppermute(value, 'x', [(i, (i + step) % size) for i in range(size)])]
  transfers between devices with their start and end apart: 10 -> 12, of which waited for: 10 -> 11; matrix products, arithmetic and copies ran while one was open for 0% -> 0% of each run, Pallas kernels for 2% -> 2%
where the time goes in v3:
time: 104 us; the launch traced here: 103 us
  blocking collectives  64.1 us (62%)
  waiting for transfers between devices  13.7 us (13%)
  Pallas kernels  12.5 us (12%)
  starting transfers between devices  11.6 us (11%)
    all_to_all x1, blocking collectives, on_device(): mine = lax.all_to_all(block, ZY, 0, 0, tiled=True)  17.5 us
    all_to_all x1, blocking collectives, on_device(): shards = lax.all_to_all(merged, 'z', 0, 0, tiled=True)  17.5 us
    all_to_all x1, blocking collectives, on_device(): columns = lax.all_to_all(merged, 'y', 0, 0, tiled=True)  15 us
    all_to_all x1, blocking collectives, on_device(): pieces = lax.all_to_all(half, ZY, 0, 0, tiled=True)  14.1 us
    ppermute x9, starting transfers between devices, shifted(): lax.ppermute(value, 'x', [(i, (i + step) % size) for i in range(size)])  11.2 us
    pallas_call x9, Pallas kernels, call(): pl.pallas_call(body, out_shape=outs, in_specs=[pl.BlockSpec(memory_space=...  9.01 us
    ppermute x9, waiting for transfers between devices, shifted(): lax.ppermute(value, 'x', [(i, (i + step) % size) for i in range(size)])  8.27 us
    pallas_call x1, Pallas kernels, on_device(): pl.pallas_call(reduce_tokens, out_shape=[shape((rows_y, depth, 8, wide),...  3.44 us
  transfers between devices with their start and end apart: 12, of which 11 were waited for; matrix products, arithmetic and copies ran while one was open for 0% of the time, Pallas kernels for 2%

profile of v3, /device:TPU:6, one launch (start us, length us, event | category | flops | bytes accessed | tf_op | source)
XLA Modules:
  0.0 102.6 jit_solution(3309639449751578128)
XLA Ops:
  0.6 3.4 %shard_map.76 = (bf16[4,8,8,1152]{3,2,1,0:T(8,128)(2,1)S(1)}, bf16[4,8,8,1152]{3,2,1,0:T(8,128)(2,1)S(1)}, f32[512,256]{1,0:T(8,128)S(1)}) custom-call(bf16[512,1024]{1,0:T(8,128)(2,1)} %bitcast.4, bf16[512,1024]{1,0:T(8,128)(2,1)} %bitcast.6, bf16[1024,256]{1,0:T(8,128)(2,1)} %par_ref.1), custom_call_target="tpu_custom_call" | custom-call | flops 1073741824 | bytes 4194304 | tf_op jit(solution)/shard_map/pallas_call | solution.py:267
  4.1 0.1 collective-permute-start
  4.2 2.0 %collective-permute-done.b_ref = bf16[4,8,8,1152]{3,2,1,0:T(8,128)(2,1)S(1)} collective-permute-done((bf16[4,8,8,1152]{3,2,1,0:T(8,128)(2,1)S(1)}, bf16[4,8,8,1152]{3,2,1,0:T(8,128)(2,1)S(1)}, u32[]{:S(2)}, u32[]{:S(2)}) %collective-permute-start) | collective-permute-done | bytes 589856 | tf_op jit(solution)/shard_map/ppermute | solution.py:280
  6.2 0.0 copy-start
  6.2 0.0 copy-start.1
  6.2 0.6 shard_map.77
  6.8 15.0 %all_to_all.20.in_ref = bf16[4,8,8,1152]{3,2,1,0:T(8,128)(2,1)S(1)} all-to-all(bf16[4,8,8,1152]{3,2,1,0:T(8,128)(2,1)S(1)} %shard_map.77), channel_id=1, replica_groups=mesh['x'=4,'z'=8,'y'=4,'c'=2] {'y'}, dimensions={0} | all-to-all | bytes 1179648 | tf_op jit(solution)/shard_map/all_to_all | solution.py:282
  21.8 0.3 shard_map.78
  22.1 17.5 %all_to_all.21.in_ref = bf16[8,8,1152]{2,1,0:T(8,128)(2,1)S(1)} all-to-all(bf16[8,8,1152]{2,1,0:T(8,128)(2,1)S(1)} %shard_map.78), channel_id=1, replica_groups=mesh['x'=4,'z'=8,'y'=4,'c'=2] {'z'}, dimensions={0} | all-to-all | bytes 294912 | tf_op jit(solution)/shard_map/all_to_all | solution.py:284
  39.6 0.2 shard_map.79
  39.9 0.0 copy-start.2
  39.9 0.0 copy-start.3
  39.9 0.6 collective-permute-start.1
  40.4 2.4 %collective-permute-start.2 = (bf16[8,1024]{1,0:T(8,128)(2,1)S(1)}, bf16[8,1024]{1,0:T(8,128)(2,1)S(1)}, u32[]{:S(2)}, u32[]{:S(2)}) collective-permute-start(bf16[8,1024]{1,0:T(8,128)(2,1)S(1)} %get-tuple-element.29.own_ref), channel_id=1, source_target_pairs={{0,128},{64,192},{128,0},{192,64},{1,129},{65,193},{129,1},{193,65... | collective-permute-start | bytes 49160 | tf_op jit(solution)/shard_map/ppermute | solution.py:251
  42.9 0.0 collective-permute-start.3
  42.9 0.8 collective-permute-done.1.a_ref
  43.7 2.0 %collective-permute-done.2.b_ref = bf16[8,1024]{1,0:T(8,128)(2,1)S(1)} collective-permute-done((bf16[8,1024]{1,0:T(8,128)(2,1)S(1)}, bf16[8,1024]{1,0:T(8,128)(2,1)S(1)}, u32[]{:S(2)}, u32[]{:S(2)}) %collective-permute-start.2) | collective-permute-done | bytes 16416 | tf_op jit(solution)/shard_map/ppermute | solution.py:251
  45.7 2.1 %collective-permute-done.3.c_ref = bf16[8,1024]{1,0:T(8,128)(2,1)S(1)} collective-permute-done((bf16[8,1024]{1,0:T(8,128)(2,1)S(1)}, bf16[8,1024]{1,0:T(8,128)(2,1)S(1)}, u32[]{:S(2)}, u32[]{:S(2)}) %collective-permute-start.3) | collective-permute-done | bytes 16416 | tf_op jit(solution)/shard_map/ppermute | solution.py:251
  47.8 0.0 copy-done
  47.8 0.0 copy-done.1
  47.8 3.4 %shard_map.80 = (bf16[8,1024]{1,0:T(8,128)(2,1)S(1)}, bf16[8,1024]{1,0:T(8,128)(2,1)S(1)}, bf16[8,1024]{1,0:T(8,128)(2,1)S(1)}, bf16[8,1024]{1,0:T(8,128)(2,1)S(1)}) custom-call(bf16[8,1024]{1,0:T(8,128)(2,1)S(1)} %get-tuple-element.29.own_ref, bf16[8,1024]{1,0:T(8,128)(2,1)S(1)} %collective-permute-done.1.a_ref, ...), custom_call_target="tpu_custom_call" | custom-call | flops 268435456 | bytes 8585216 | tf_op jit(solution)/shard_map/pallas_call | solution.py:30
  51.2 0.0 copy-start.4
  51.2 0.1 collective-permute-start.4
  51.3 2.0 %collective-permute-start.5 = (bf16[8,1024]{1,0:T(8,128)(2,1)S(1)}, bf16[8,1024]{1,0:T(8,128)(2,1)S(1)}, u32[]{:S(2)}, u32[]{:S(2)}) collective-permute-start(bf16[8,1024]{1,0:T(8,128)(2,1)S(1)} %get-tuple-element.32), channel_id=1, source_target_pairs={{0,128},{64,192},{128,0},{192,64},{1,129},{65,193},{129,1},{193,65... | collective-permute-start | bytes 49160 | tf_op jit(solution)/shard_map/ppermute | solution.py:251
  53.3 1.2 %collective-permute-start.6 = (bf16[8,1024]{1,0:T(8,128)(2,1)S(1)}, bf16[8,1024]{1,0:T(8,128)(2,1)S(1)}, u32[]{:S(2)}, u32[]{:S(2)}) collective-permute-start(bf16[8,1024]{1,0:T(8,128)(2,1)S(1)} %get-tuple-element.33), channel_id=1, source_target_pairs={{0,64},{64,128},{128,192},{192,0},{1,65},{65,129},{129,193},{193,1... | collective-permute-start | bytes 49160 | tf_op jit(solution)/shard_map/ppermute | solution.py:251
  54.5 1.7 %collective-permute-done.4.a_ref = bf16[8,1024]{1,0:T(8,128)(2,1)S(1)} collective-permute-done((bf16[8,1024]{1,0:T(8,128)(2,1)S(1)}, bf16[8,1024]{1,0:T(8,128)(2,1)S(1)}, u32[]{:S(2)}, u32[]{:S(2)}) %collective-permute-start.4) | collective-permute-done | bytes 16416 | tf_op jit(solution)/shard_map/ppermute | solution.py:251
  56.2 0.4 collective-permute-done.5.b_ref
  56.6 0.6 collective-permute-done.6.c_ref
  57.3 0.3 shard_map.81
  57.5 17.5 %all_to_all.22.own_ref = bf16[32,8,1152]{2,1,0:T(8,128)(2,1)S(1)} all-to-all(bf16[32,8,1152]{2,1,0:T(8,128)(2,1)S(1)} %shard_map.81), channel_id=1, replica_groups=mesh['x'=4,'z'=8,'y'=4,'c'=2] {'z','y'}, dimensions={0} | all-to-all | bytes 1179648 | tf_op jit(solution)/shard_map/all_to_all | solution.py:297
  75.1 0.0 collective-permute-start.7
  75.1 2.0 %collective-permute-done.7.oth_ref = bf16[32,8,1152]{2,1,0:T(8,128)(2,1)S(1)} collective-permute-done((bf16[32,8,1152]{2,1,0:T(8,128)(2,1)S(1)}, bf16[32,8,1152]{2,1,0:T(8,128)(2,1)S(1)}, u32[]{:S(2)}, u32[]{:S(2)}) %collective-permute-start.7) | collective-permute-done | bytes 589856 | tf_op jit(solution)/shard_map/ppermute | solution.py:298
  77.1 0.0 copy-done.2
  77.1 0.0 copy-done.3
  77.1 1.4 %shard_map.82 = (bf16[4,32,8,128]{3,2,1,0:T(8,128)(2,1)S(1)}, bf16[4,32,8,128]{3,2,1,0:T(8,128)(2,1)S(1)}, bf16[512,256]{1,0:T(8,128)(2,1)S(1)}, bf16[512,256]{1...) custom-call(f32[512,256]{1,0:T(8,128)S(1)} %get-tuple-element.26.log, ...), custom_call_target="tpu_custom_call" | custom-call | flops 1342177280 | bytes 8519680 | tf_op jit(solution)/shard_map/pallas_call | solution.py:30
  78.5 0.2 collective-permute-start.8
  78.7 1.4 %collective-permute-done.8.b_ref = bf16[4,32,8,128]{3,2,1,0:T(8,128)(2,1)S(1)} collective-permute-done((bf16[4,32,8,128]{3,2,1,0:T(8,128)(2,1)S(1)}, bf16[4,32,8,128]{3,2,1,0:T(8,128)(2,1)S(1)}, u32[]{:S(2)}, u32[]{:S(2)}) %collective-permute-start.8) | collective-permute-done | bytes 262176 | tf_op jit(solution)/shard_map/ppermute | solution.py:307
  80.1 0.1 shard_map.84
  80.2 1.7 %collective-permute-start.10 = (bf16[32,8,128]{2,1,0:T(8,128)(2,1)S(1)}, bf16[32,8,128]{2,1,0:T(8,128)(2,1)S(1)}, u32[]{:S(2)}, u32[]{:S(2)}) collective-permute-start(bf16[32,8,128]{2,1,0:T(8,128)(2,1)S(1)} %get-tuple-element.47), channel_id=1, source_target_pairs={{0,128},{64,192},{128,0},{192,64},{1,129},{65,193},{129,1},{193,65... | collective-permute-start | bytes 196616 | tf_op jit(solution)/shard_map/ppermute | solution.py:251
  81.9 1.7 %collective-permute-start.11 = (bf16[32,8,128]{2,1,0:T(8,128)(2,1)S(1)}, bf16[32,8,128]{2,1,0:T(8,128)(2,1)S(1)}, u32[]{:S(2)}, u32[]{:S(2)}) collective-permute-start(bf16[32,8,128]{2,1,0:T(8,128)(2,1)S(1)} %get-tuple-element.48), channel_id=1, source_target_pairs={{0,192},{64,0},{128,64},{192,128},{1,193},{65,1},{129,65},{193,129... | collective-permute-start | bytes 196616 | tf_op jit(solution)/shard_map/ppermute | solution.py:251
  83.6 1.5 %collective-permute-start.9 = (bf16[32,8,128]{2,1,0:T(8,128)(2,1)S(1)}, bf16[32,8,128]{2,1,0:T(8,128)(2,1)S(1)}, u32[]{:S(2)}, u32[]{:S(2)}) collective-permute-start(bf16[32,8,128]{2,1,0:T(8,128)(2,1)S(1)} %get-tuple-element.46), channel_id=1, source_target_pairs={{0,64},{64,128},{128,192},{192,0},{1,65},{65,129},{129,193},{193,1... | collective-permute-start | bytes 196616 | tf_op jit(solution)/shard_map/ppermute | solution.py:251
  85.1 0.0 copy-done.4
  85.1 2.2 %shard_map.83 = (bf16[512,1024]{1,0:T(8,128)(2,1)}, bf16[512,1024]{1,0:T(8,128)(2,1)}) custom-call(bf16[512,256]{1,0:T(8,128)(2,1)S(1)} %get-tuple-element.36.comb_ref, bf16[256,1024]{1,0:T(8,128)(2,1)S(1)} %get-tuple-element.37.so_ref, bf16[512,256]{1,0:T(8,128)(2,1)S(1)} %get-tuple-element.38.dlog_ref, bf16[1024,256]{1,0:T(8,128)(2,1)S(1)} %copy-done.4, ...), custom_call_target="tpu_custom_call" | custom-call | flops 805306368 | bytes 6553600 | tf_op jit(solution)/shard_map/pallas_call | solution.py:30
  87.3 0.0 collective-permute-done.10.b_ref
  87.3 0.1 collective-permute-done.11.c_ref
  87.4 0.4 collective-permute-done.9.a_ref
  87.9 14.1 %all_to_all.23.in_ref = bf16[32,8,128]{2,1,0:T(8,128)(2,1)S(1)} all-to-all(bf16[32,8,128]{2,1,0:T(8,128)(2,1)S(1)} %shard_map.85), channel_id=1, replica_groups=mesh['x'=4,'z'=8,'y'=4,'c'=2] {'z','y'}, dimensions={0} | all-to-all | bytes 131072 | tf_op jit(solution)/shard_map/all_to_all | solution.py:322
  102.0 0.6 shard_map.86
  (1 shorter events, 0.0 us)
Async XLA Ops:
  4.1 2.1 %collective-permute-start = (bf16[4,8,8,1152]{3,2,1,0:T(8,128)(2,1)S(1)}, bf16[4,8,8,1152]{3,2,1,0:T(8,128)(2,1)S(1)}, u32[]{:S(2)}, u32[]{:S(2)}) collective-permute-start(bf16[4,8,8,1152]{3,2,1,0:T(8,128)(2,1)S(1)} %get-tuple-element.28), channel_id=1, source_target_pairs={{0,1},{1,0},{2,3},{3,2},{4,5},{5,4},{6,7},{7,6},{8,9},{9,8},{10,11... | collective-permute-start | bytes 1769480 | tf_op jit(solution)/shard_map/ppermute | solution.py:280
  6.2 41.6 %copy-start = (bf16[2,1024,1024]{2,1,0:T(8,128)(2,1)S(1)}, bf16[2,1024,1024]{2,1,0:T(8,128)(2,1)}, u32[]{:S(2)}) copy-start(bf16[2,1024,1024]{2,1,0:T(8,128)(2,1)} %win_ref.1) | copy-start | bytes 12582916
  6.2 41.6 %copy-start.1 = (bf16[2,1024,1024]{2,1,0:T(8,128)(2,1)S(1)}, bf16[2,1024,1024]{2,1,0:T(8,128)(2,1)}, u32[]{:S(2)}) copy-start(bf16[2,1024,1024]{2,1,0:T(8,128)(2,1)} %wout_ref.1) | copy-start | bytes 12582916
  39.9 37.2 %copy-start.2 = (bf16[1,512,1024]{2,1,0:T(8,128)(2,1)S(1)}, bf16[1,512,1024]{2,1,0:T(8,128)(2,1)}, u32[]{:S(2)}) copy-start(bf16[1,512,1024]{2,1,0:T(8,128)(2,1)} %param.5) | copy-start | bytes 3145732
  39.9 37.2 %copy-start.3 = (bf16[1,512,1024]{2,1,0:T(8,128)(2,1)S(1)}, bf16[1,512,1024]{2,1,0:T(8,128)(2,1)}, u32[]{:S(2)}) copy-start(bf16[1,512,1024]{2,1,0:T(8,128)(2,1)} %param.9) | copy-start | bytes 3145732
  39.9 3.8 %collective-permute-start.1 = (bf16[8,1024]{1,0:T(8,128)(2,1)S(1)}, bf16[8,1024]{1,0:T(8,128)(2,1)S(1)}, u32[]{:S(2)}, u32[]{:S(2)}) collective-permute-start(bf16[8,1024]{1,0:T(8,128)(2,1)S(1)} %get-tuple-element.29.own_ref), channel_id=1, source_target_pairs={{0,64},{64,128},{128,192},{192,0},{1,65},{65,129},{129,193},{193,1... | collective-permute-start | bytes 49160 | tf_op jit(solution)/shard_map/ppermute | solution.py:251
  40.4 5.2 %collective-permute-start.2 = (bf16[8,1024]{1,0:T(8,128)(2,1)S(1)}, bf16[8,1024]{1,0:T(8,128)(2,1)S(1)}, u32[]{:S(2)}, u32[]{:S(2)}) collective-permute-start(bf16[8,1024]{1,0:T(8,128)(2,1)S(1)} %get-tuple-element.29.own_ref), channel_id=1, source_target_pairs={{0,128},{64,192},{128,0},{192,64},{1,129},{65,193},{129,1},{193,65... | collective-permute-start | bytes 49160 | tf_op jit(solution)/shard_map/ppermute | solution.py:251
  42.9 4.9 %collective-permute-start.3 = (bf16[8,1024]{1,0:T(8,128)(2,1)S(1)}, bf16[8,1024]{1,0:T(8,128)(2,1)S(1)}, u32[]{:S(2)}, u32[]{:S(2)}) collective-permute-start(bf16[8,1024]{1,0:T(8,128)(2,1)S(1)} %get-tuple-element.29.own_ref), channel_id=1, source_target_pairs={{0,192},{64,0},{128,64},{192,128},{1,193},{65,1},{129,65},{193,129... | collective-permute-start | bytes 49160 | tf_op jit(solution)/shard_map/ppermute | solution.py:251
  51.2 33.9 %copy-start.4 = (bf16[1024,256]{1,0:T(8,128)(2,1)S(1)}, bf16[1024,256]{1,0:T(8,128)(2,1)}, u32[]{:S(2)}) copy-start(bf16[1024,256]{1,0:T(8,128)(2,1)} %par_ref.1) | copy-start | bytes 1572868
  51.2 5.0 %collective-permute-start.4 = (bf16[8,1024]{1,0:T(8,128)(2,1)S(1)}, bf16[8,1024]{1,0:T(8,128)(2,1)S(1)}, u32[]{:S(2)}, u32[]{:S(2)}) collective-permute-start(bf16[8,1024]{1,0:T(8,128)(2,1)S(1)} %get-tuple-element.31), channel_id=1, source_target_pairs={{0,192},{64,0},{128,64},{192,128},{1,193},{65,1},{129,65},{193,129... | collective-permute-start | bytes 49160 | tf_op jit(solution)/shard_map/ppermute | solution.py:251
  51.3 5.3 %collective-permute-start.5 = (bf16[8,1024]{1,0:T(8,128)(2,1)S(1)}, bf16[8,1024]{1,0:T(8,128)(2,1)S(1)}, u32[]{:S(2)}, u32[]{:S(2)}) collective-permute-start(bf16[8,1024]{1,0:T(8,128)(2,1)S(1)} %get-tuple-element.32), channel_id=1, source_target_pairs={{0,128},{64,192},{128,0},{192,64},{1,129},{65,193},{129,1},{193,65... | collective-permute-start | bytes 49160 | tf_op jit(solution)/shard_map/ppermute | solution.py:251
  53.3 3.9 %collective-permute-start.6 = (bf16[8,1024]{1,0:T(8,128)(2,1)S(1)}, bf16[8,1024]{1,0:T(8,128)(2,1)S(1)}, u32[]{:S(2)}, u32[]{:S(2)}) collective-permute-start(bf16[8,1024]{1,0:T(8,128)(2,1)S(1)} %get-tuple-element.33), channel_id=1, source_target_pairs={{0,64},{64,128},{128,192},{192,0},{1,65},{65,129},{129,193},{193,1... | collective-permute-start | bytes 49160 | tf_op jit(solution)/shard_map/ppermute | solution.py:251
  75.1 2.0 %collective-permute-start.7 = (bf16[32,8,1152]{2,1,0:T(8,128)(2,1)S(1)}, bf16[32,8,1152]{2,1,0:T(8,128)(2,1)S(1)}, u32[]{:S(2)}, u32[]{:S(2)}) collective-permute-start(bf16[32,8,1152]{2,1,0:T(8,128)(2,1)S(1)} %all_to_all.22.own_ref), channel_id=1, source_target_pairs={{0,1},{1,0},{2,3},{3,2},{4,5},{5,4},{6,7},{7,6},{8,9},{9,8},{10,11... | collective-permute-start | bytes 1769480 | tf_op jit(solution)/shard_map/ppermute | solution.py:298
  78.5 1.6 %collective-permute-start.8 = (bf16[4,32,8,128]{3,2,1,0:T(8,128)(2,1)S(1)}, bf16[4,32,8,128]{3,2,1,0:T(8,128)(2,1)S(1)}, u32[]{:S(2)}, u32[]{:S(2)}) collective-permute-start(bf16[4,32,8,128]{3,2,1,0:T(8,128)(2,1)S(1)} %get-tuple-element.44), channel_id=1, source_target_pairs={{0,1},{1,0},{2,3},{3,2},{4,5},{5,4},{6,7},{7,6},{8,9},{9,8},{10,11... | collective-permute-start | bytes 786440 | tf_op jit(solution)/shard_map/ppermute | solution.py:307
  80.2 7.1 %collective-permute-start.10 = (bf16[32,8,128]{2,1,0:T(8,128)(2,1)S(1)}, bf16[32,8,128]{2,1,0:T(8,128)(2,1)S(1)}, u32[]{:S(2)}, u32[]{:S(2)}) collective-permute-start(bf16[32,8,128]{2,1,0:T(8,128)(2,1)S(1)} %get-tuple-element.47), channel_id=1, source_target_pairs={{0,128},{64,192},{128,0},{192,64},{1,129},{65,193},{129,1},{193,65... | collective-permute-start | bytes 196616 | tf_op jit(solution)/shard_map/ppermute | solution.py:251
  81.9 5.5 %collective-permute-start.11 = (bf16[32,8,128]{2,1,0:T(8,128)(2,1)S(1)}, bf16[32,8,128]{2,1,0:T(8,128)(2,1)S(1)}, u32[]{:S(2)}, u32[]{:S(2)}) collective-permute-start(bf16[32,8,128]{2,1,0:T(8,128)(2,1)S(1)} %get-tuple-element.48), channel_id=1, source_target_pairs={{0,192},{64,0},{128,64},{192,128},{1,193},{65,1},{129,65},{193,129... | collective-permute-start | bytes 196616 | tf_op jit(solution)/shard_map/ppermute | solution.py:251
  83.6 4.3 %collective-permute-start.9 = (bf16[32,8,128]{2,1,0:T(8,128)(2,1)S(1)}, bf16[32,8,128]{2,1,0:T(8,128)(2,1)S(1)}, u32[]{:S(2)}, u32[]{:S(2)}) collective-permute-start(bf16[32,8,128]{2,1,0:T(8,128)(2,1)S(1)} %get-tuple-element.46), channel_id=1, source_target_pairs={{0,64},{64,128},{128,192},{192,0},{1,65},{65,129},{129,193},{193,1... | collective-permute-start | bytes 196616 | tf_op jit(solution)/shard_map/ppermute | solution.py:251

commit v4 on v3

--- a/solution.py
+++ b/solution.py
@@ -127,12 +127,15 @@
     out_ref[..., width:] = stats(lane, top, high, low).astype(BF)
 
 
-def merge_cores(a_ref, b_ref, out_ref):
-    store_merged([a_ref[...].astype(F32), b_ref[...].astype(F32)], out_ref)
-
-
-def merge_columns(in_ref, out_ref):
-    store_merged([in_ref[i].astype(F32) for i in range(in_ref.shape[0])], out_ref)
+def merge_cores(a_ref, b_ref, *out_refs):
+    here = lax.axis_index("y")
+    for k, ref in enumerate(out_refs):
+        to = lax.rem(here + k, len(out_refs))
+        store_merged([a_ref[to].astype(F32), b_ref[to].astype(F32)], ref)
+
+
+def merge_columns(a_ref, b_ref, c_ref, d_ref, out_ref):
+    store_merged([r[...].astype(F32) for r in (a_ref, b_ref, c_ref, d_ref)], out_ref)
 
 
 def merge_shards(in_ref, pay_ref, full_ref, side_ref):
@@ -247,8 +250,8 @@
     out_ref[:, half:] = total[4:]
 
 
-def shifted(value, step, size):
-    return lax.ppermute(value, "x", [(i, (i + step) % size) for i in range(size)])
+def shifted(value, step, size, axis="x"):
+    return lax.ppermute(value, axis, [(i, (i + step) % size) for i in range(size)])
 
 
 def on_device(tokens, slot_parameters, w_in, w_out, grad_out):
@@ -278,9 +281,9 @@
         cost_estimate=pl.CostEstimate(flops=4 * unit, bytes_accessed=4 << 20, transcendentals=0),
     )(*[pltpu.with_memory_space_constraint(a, pltpu.HBM) for a in (tok, cot, slot_parameters)])
     other = lax.ppermute(send, "c", swap)
-    (merged,) = call(merge_cores, [shape(keep.shape, BF)], keep, other, flops=40 * unit)
-    columns = lax.all_to_all(merged, "y", 0, 0, tiled=True)
-    (merged,) = call(merge_columns, [shape((depth, 8, wide), BF)], columns)
+    blocks = call(merge_cores, [shape((depth, 8, wide), BF)] * rows_y, keep, other, flops=40 * unit)
+    columns = [shifted(blocks[k], k, rows_y, "y") for k in range(1, rows_y)]
+    (merged,) = call(merge_columns, [shape((depth, 8, wide), BF)], blocks[0], *columns)
     shards = lax.all_to_all(merged, "z", 0, 0, tiled=True)
     pay, full, side = call(
         merge_shards,

time: 104 us -> 102 us (0.981); the launches traced: 103 us -> 102 us
  blocking collectives: 64.1 us -> 50.2 us
  waiting for transfers between devices: 13.7 us -> 22.1 us
  starting transfers between devices: 11.6 us -> 16.5 us
    all_to_all x1 -> x0, blocking collectives: 15 us -> none  [on_device(): columns = lax.all_to_all(merged, 'y', 0, 0, tiled=True)]
    ppermute x9 -> x12, waiting for transfers between devices: 8.27 us -> 16.7 us  [shifted(): lax.ppermute(value, axis, [(i, (i + step) % size) for i in range(size)])]
    ppermute x9 -> x12, starting transfers between devices: 11.2 us -> 16.2 us  [shifted(): lax.ppermute(value, axis, [(i, (i + step) % size) for i in range(size)])]
    all_to_all x1, blocking collectives: 17.5 us -> 18.6 us  [on_device(): mine = lax.all_to_all(block, ZY, 0, 0, tiled=True)]
  transfers between devices with their start and end apart: 12 -> 15, of which waited for: 11 -> 13; matrix products, arithmetic and copies ran while one was open for 0% -> 0% of each run, Pallas kernels for 2% -> 2%
where the time goes in v4:
time: 102 us
  blocking collectives  50.2 us (49%)
  waiting for transfers between devices  22.1 us (22%)
  starting transfers between devices  16.5 us (16%)
  Pallas kernels  12.6 us (12%)
    all_to_all x1, blocking collectives, on_device(): mine = lax.all_to_all(block, ZY, 0, 0, tiled=True)  18.6 us
    all_to_all x1, blocking collectives, on_device(): shards = lax.all_to_all(merged, 'z', 0, 0, tiled=True)  17.5 us
    ppermute x12, waiting for transfers between devices, shifted(): lax.ppermute(value, axis, [(i, (i + step) % size) for i in range(size)])  16.7 us
    ppermute x12, starting transfers between devices, shifted(): lax.ppermute(value, axis, [(i, (i + step) % size) for i in range(size)])  16.2 us
    all_to_all x1, blocking collectives, on_device(): pieces = lax.all_to_all(half, ZY, 0, 0, tiled=True)  14.1 us
    pallas_call x9, Pallas kernels, call(): pl.pallas_call(body, out_shape=outs, in_specs=[pl.BlockSpec(memory_space=...  9.15 us
    pallas_call x1, Pallas kernels, on_device(): pl.pallas_call(reduce_tokens, out_shape=[shape((rows_y, depth, 8, wide),...  3.44 us
  transfers between devices with their start and end apart: 15, of which 13 were waited for; matrix products, arithmetic and copies ran while one was open for 0% of the time, Pallas kernels for 2%

profile of v4, /device:TPU:6, one launch (start us, length us, event | category | flops | bytes accessed | tf_op | source)
XLA Modules:
  0.0 102.2 jit_solution(11710267644211777980)
XLA Ops:
  0.6 3.4 %shard_map.76 = (bf16[4,8,8,1152]{3,2,1,0:T(8,128)(2,1)S(1)}, bf16[4,8,8,1152]{3,2,1,0:T(8,128)(2,1)S(1)}, f32[512,256]{1,0:T(8,128)S(1)}) custom-call(bf16[512,1024]{1,0:T(8,128)(2,1)} %bitcast.4, bf16[512,1024]{1,0:T(8,128)(2,1)} %bitcast.6, bf16[1024,256]{1,0:T(8,128)(2,1)} %par_ref.1), custom_call_target="tpu_custom_call" | custom-call | flops 1073741824 | bytes 4194304 | tf_op jit(solution)/shard_map/pallas_call | solution.py:270
  4.1 0.1 collective-permute-start
  4.2 2.0 %collective-permute-done.b_ref = bf16[4,8,8,1152]{3,2,1,0:T(8,128)(2,1)S(1)} collective-permute-done((bf16[4,8,8,1152]{3,2,1,0:T(8,128)(2,1)S(1)}, bf16[4,8,8,1152]{3,2,1,0:T(8,128)(2,1)S(1)}, u32[]{:S(2)}, u32[]{:S(2)}) %collective-permute-start) | collective-permute-done | bytes 589856 | tf_op jit(solution)/shard_map/ppermute | solution.py:283
  6.2 0.0 copy-start
  6.2 0.0 copy-start.1
  6.2 0.7 shard_map.77
  6.9 1.7 %collective-permute-start.1 = (bf16[8,8,1152]{2,1,0:T(8,128)(2,1)S(1)}, bf16[8,8,1152]{2,1,0:T(8,128)(2,1)S(1)}, u32[]{:S(2)}, u32[]{:S(2)}) collective-permute-start(bf16[8,8,1152]{2,1,0:T(8,128)(2,1)S(1)} %get-tuple-element.34), channel_id=1, source_target_pairs={{0,2},{2,4},{4,6},{6,0},{1,3},{3,5},{5,7},{7,1},{8,10},{10,12},{12... | collective-permute-start | bytes 442376 | tf_op jit(solution)/shard_map/ppermute | solution.py:254
  8.6 2.9 %collective-permute-start.2 = (bf16[8,8,1152]{2,1,0:T(8,128)(2,1)S(1)}, bf16[8,8,1152]{2,1,0:T(8,128)(2,1)S(1)}, u32[]{:S(2)}, u32[]{:S(2)}) collective-permute-start(bf16[8,8,1152]{2,1,0:T(8,128)(2,1)S(1)} %get-tuple-element.35), channel_id=1, source_target_pairs={{0,4},{2,6},{4,0},{6,2},{1,5},{3,7},{5,1},{7,3},{8,12},{10,14},{12... | collective-permute-start | bytes 442376 | tf_op jit(solution)/shard_map/ppermute | solution.py:254
  11.5 1.3 %collective-permute-start.3 = (bf16[8,8,1152]{2,1,0:T(8,128)(2,1)S(1)}, bf16[8,8,1152]{2,1,0:T(8,128)(2,1)S(1)}, u32[]{:S(2)}, u32[]{:S(2)}) collective-permute-start(bf16[8,8,1152]{2,1,0:T(8,128)(2,1)S(1)} %get-tuple-element.36), channel_id=1, source_target_pairs={{0,6},{2,0},{4,2},{6,4},{1,7},{3,1},{5,3},{7,5},{8,14},{10,8},{12,... | collective-permute-start | bytes 442376 | tf_op jit(solution)/shard_map/ppermute | solution.py:254
  12.8 1.3 %collective-permute-done.1.b_ref = bf16[8,8,1152]{2,1,0:T(8,128)(2,1)S(1)} collective-permute-done((bf16[8,8,1152]{2,1,0:T(8,128)(2,1)S(1)}, bf16[8,8,1152]{2,1,0:T(8,128)(2,1)S(1)}, u32[]{:S(2)}, u32[]{:S(2)}) %collective-permute-start.1) | collective-permute-done | bytes 147488 | tf_op jit(solution)/shard_map/ppermute | solution.py:254
  14.2 4.3 %collective-permute-done.2.c_ref = bf16[8,8,1152]{2,1,0:T(8,128)(2,1)S(1)} collective-permute-done((bf16[8,8,1152]{2,1,0:T(8,128)(2,1)S(1)}, bf16[8,8,1152]{2,1,0:T(8,128)(2,1)S(1)}, u32[]{:S(2)}, u32[]{:S(2)}) %collective-permute-start.2) | collective-permute-done | bytes 147488 | tf_op jit(solution)/shard_map/ppermute | solution.py:254
  18.5 0.0 collective-permute-done.3.d_ref
  18.5 0.3 shard_map.78
  18.8 17.5 %all_to_all.15.in_ref = bf16[8,8,1152]{2,1,0:T(8,128)(2,1)S(1)} all-to-all(bf16[8,8,1152]{2,1,0:T(8,128)(2,1)S(1)} %shard_map.78), channel_id=1, replica_groups=mesh['x'=4,'z'=8,'y'=4,'c'=2] {'z'}, dimensions={0} | all-to-all | bytes 294912 | tf_op jit(solution)/shard_map/all_to_all | solution.py:287
  36.3 0.2 shard_map.79
  36.6 0.0 copy-start.2
  36.6 0.0 copy-start.3
  36.6 0.6 collective-permute-start.4
  37.2 2.4 %collective-permute-start.5 = (bf16[8,1024]{1,0:T(8,128)(2,1)S(1)}, bf16[8,1024]{1,0:T(8,128)(2,1)S(1)}, u32[]{:S(2)}, u32[]{:S(2)}) collective-permute-start(bf16[8,1024]{1,0:T(8,128)(2,1)S(1)} %get-tuple-element.37.own_ref), channel_id=1, source_target_pairs={{0,128},{64,192},{128,0},{192,64},{1,129},{65,193},{129,1},{193,65... | collective-permute-start | bytes 49160 | tf_op jit(solution)/shard_map/ppermute | solution.py:254
  39.6 0.0 collective-permute-start.6
  39.6 0.8 collective-permute-done.4.a_ref
  40.4 2.0 %collective-permute-done.5.b_ref = bf16[8,1024]{1,0:T(8,128)(2,1)S(1)} collective-permute-done((bf16[8,1024]{1,0:T(8,128)(2,1)S(1)}, bf16[8,1024]{1,0:T(8,128)(2,1)S(1)}, u32[]{:S(2)}, u32[]{:S(2)}) %collective-permute-start.5) | collective-permute-done | bytes 16416 | tf_op jit(solution)/shard_map/ppermute | solution.py:254
  42.4 2.1 %collective-permute-done.6.c_ref = bf16[8,1024]{1,0:T(8,128)(2,1)S(1)} collective-permute-done((bf16[8,1024]{1,0:T(8,128)(2,1)S(1)}, bf16[8,1024]{1,0:T(8,128)(2,1)S(1)}, u32[]{:S(2)}, u32[]{:S(2)}) %collective-permute-start.6) | collective-permute-done | bytes 16416 | tf_op jit(solution)/shard_map/ppermute | solution.py:254
  44.5 0.0 copy-done
  44.5 0.0 copy-done.1
  44.5 3.4 %shard_map.80 = (bf16[8,1024]{1,0:T(8,128)(2,1)S(1)}, bf16[8,1024]{1,0:T(8,128)(2,1)S(1)}, bf16[8,1024]{1,0:T(8,128)(2,1)S(1)}, bf16[8,1024]{1,0:T(8,128)(2,1)S(1)}) custom-call(bf16[8,1024]{1,0:T(8,128)(2,1)S(1)} %get-tuple-element.37.own_ref, bf16[8,1024]{1,0:T(8,128)(2,1)S(1)} %collective-permute-done.4.a_ref, ...), custom_call_target="tpu_custom_call" | custom-call | flops 268435456 | bytes 8585216 | tf_op jit(solution)/shard_map/pallas_call | solution.py:30
  47.9 0.0 copy-start.4
  47.9 0.1 collective-permute-start.7
  48.0 2.0 %collective-permute-start.8 = (bf16[8,1024]{1,0:T(8,128)(2,1)S(1)}, bf16[8,1024]{1,0:T(8,128)(2,1)S(1)}, u32[]{:S(2)}, u32[]{:S(2)}) collective-permute-start(bf16[8,1024]{1,0:T(8,128)(2,1)S(1)} %get-tuple-element.40), channel_id=1, source_target_pairs={{0,128},{64,192},{128,0},{192,64},{1,129},{65,193},{129,1},{193,65... | collective-permute-start | bytes 49160 | tf_op jit(solution)/shard_map/ppermute | solution.py:254
  50.0 1.2 %collective-permute-start.9 = (bf16[8,1024]{1,0:T(8,128)(2,1)S(1)}, bf16[8,1024]{1,0:T(8,128)(2,1)S(1)}, u32[]{:S(2)}, u32[]{:S(2)}) collective-permute-start(bf16[8,1024]{1,0:T(8,128)(2,1)S(1)} %get-tuple-element.41), channel_id=1, source_target_pairs={{0,64},{64,128},{128,192},{192,0},{1,65},{65,129},{129,193},{193,1... | collective-permute-start | bytes 49160 | tf_op jit(solution)/shard_map/ppermute | solution.py:254
  51.2 1.7 %collective-permute-done.7.a_ref = bf16[8,1024]{1,0:T(8,128)(2,1)S(1)} collective-permute-done((bf16[8,1024]{1,0:T(8,128)(2,1)S(1)}, bf16[8,1024]{1,0:T(8,128)(2,1)S(1)}, u32[]{:S(2)}, u32[]{:S(2)}) %collective-permute-start.7) | collective-permute-done | bytes 16416 | tf_op jit(solution)/shard_map/ppermute | solution.py:254
  52.9 0.4 collective-permute-done.8.b_ref
  53.3 0.6 collective-permute-done.9.c_ref
  54.0 0.3 shard_map.81
  54.2 18.6 %all_to_all.16.own_ref = bf16[32,8,1152]{2,1,0:T(8,128)(2,1)S(1)} all-to-all(bf16[32,8,1152]{2,1,0:T(8,128)(2,1)S(1)} %shard_map.81), channel_id=1, replica_groups=mesh['x'=4,'z'=8,'y'=4,'c'=2] {'z','y'}, dimensions={0} | all-to-all | bytes 1179648 | tf_op jit(solution)/shard_map/all_to_all | solution.py:300
  72.9 0.0 collective-permute-start.10
  72.9 2.0 %collective-permute-done.10.oth_ref = bf16[32,8,1152]{2,1,0:T(8,128)(2,1)S(1)} collective-permute-done((bf16[32,8,1152]{2,1,0:T(8,128)(2,1)S(1)}, bf16[32,8,1152]{2,1,0:T(8,128)(2,1)S(1)}, u32[]{:S(2)}, u32[]{:S(2)}) %collective-permute-start.10) | collective-permute-done | bytes 589856 | tf_op jit(solution)/shard_map/ppermute | solution.py:301
  74.9 0.0 copy-done.2
  74.9 0.0 copy-done.3
  74.9 1.4 %shard_map.82 = (bf16[4,32,8,128]{3,2,1,0:T(8,128)(2,1)S(1)}, bf16[4,32,8,128]{3,2,1,0:T(8,128)(2,1)S(1)}, bf16[512,256]{1,0:T(8,128)(2,1)S(1)}, bf16[512,256]{1...) custom-call(f32[512,256]{1,0:T(8,128)S(1)} %get-tuple-element.30.log, ...), custom_call_target="tpu_custom_call" | custom-call | flops 1342177280 | bytes 8519680 | tf_op jit(solution)/shard_map/pallas_call | solution.py:30
  76.3 0.2 collective-permute-start.11
  76.5 1.4 %collective-permute-done.11.b_ref = bf16[4,32,8,128]{3,2,1,0:T(8,128)(2,1)S(1)} collective-permute-done((bf16[4,32,8,128]{3,2,1,0:T(8,128)(2,1)S(1)}, bf16[4,32,8,128]{3,2,1,0:T(8,128)(2,1)S(1)}, u32[]{:S(2)}, u32[]{:S(2)}) %collective-permute-start.11) | collective-permute-done | bytes 262176 | tf_op jit(solution)/shard_map/ppermute | solution.py:310
  77.9 0.1 shard_map.84
  78.0 2.6 %collective-permute-start.12 = (bf16[32,8,128]{2,1,0:T(8,128)(2,1)S(1)}, bf16[32,8,128]{2,1,0:T(8,128)(2,1)S(1)}, u32[]{:S(2)}, u32[]{:S(2)}) collective-permute-start(bf16[32,8,128]{2,1,0:T(8,128)(2,1)S(1)} %get-tuple-element.54), channel_id=1, source_target_pairs={{0,64},{64,128},{128,192},{192,0},{1,65},{65,129},{129,193},{193,1... | collective-permute-start | bytes 196616 | tf_op jit(solution)/shard_map/ppermute | solution.py:254
  80.5 1.4 %collective-permute-start.13 = (bf16[32,8,128]{2,1,0:T(8,128)(2,1)S(1)}, bf16[32,8,128]{2,1,0:T(8,128)(2,1)S(1)}, u32[]{:S(2)}, u32[]{:S(2)}) collective-permute-start(bf16[32,8,128]{2,1,0:T(8,128)(2,1)S(1)} %get-tuple-element.55), channel_id=1, source_target_pairs={{0,128},{64,192},{128,0},{192,64},{1,129},{65,193},{129,1},{193,65... | collective-permute-start | bytes 196616 | tf_op jit(solution)/shard_map/ppermute | solution.py:254
  81.9 0.0 collective-permute-start.14
  82.0 0.0 copy-done.4
  82.0 2.2 %shard_map.83 = (bf16[512,1024]{1,0:T(8,128)(2,1)}, bf16[512,1024]{1,0:T(8,128)(2,1)}) custom-call(bf16[512,256]{1,0:T(8,128)(2,1)S(1)} %get-tuple-element.44.comb_ref, bf16[256,1024]{1,0:T(8,128)(2,1)S(1)} %get-tuple-element.45.so_ref, bf16[512,256]{1,0:T(8,128)(2,1)S(1)} %get-tuple-element.46.dlog_ref, bf16[1024,256]{1,0:T(8,128)(2,1)S(1)} %copy-done.4, ...), custom_call_target="tpu_custom_call" | custom-call | flops 805306368 | bytes 6553600 | tf_op jit(solution)/shard_map/pallas_call | solution.py:30
  84.1 0.0 collective-permute-done.12.a_ref
  84.1 2.6 %collective-permute-done.13.b_ref = bf16[32,8,128]{2,1,0:T(8,128)(2,1)S(1)} collective-permute-done((bf16[32,8,128]{2,1,0:T(8,128)(2,1)S(1)}, bf16[32,8,128]{2,1,0:T(8,128)(2,1)S(1)}, u32[]{:S(2)}, u32[]{:S(2)}) %collective-permute-start.13) | collective-permute-done | bytes 65568 | tf_op jit(solution)/shard_map/ppermute | solution.py:254
  86.7 0.7 collective-permute-done.14.c_ref
  87.5 14.1 %all_to_all.17.in_ref = bf16[32,8,128]{2,1,0:T(8,128)(2,1)S(1)} all-to-all(bf16[32,8,128]{2,1,0:T(8,128)(2,1)S(1)} %shard_map.85), channel_id=1, replica_groups=mesh['x'=4,'z'=8,'y'=4,'c'=2] {'z','y'}, dimensions={0} | all-to-all | bytes 131072 | tf_op jit(solution)/shard_map/all_to_all | solution.py:325
  101.6 0.6 shard_map.86
  (1 shorter events, 0.0 us)
Async XLA Ops:
  4.1 2.1 %collective-permute-start = (bf16[4,8,8,1152]{3,2,1,0:T(8,128)(2,1)S(1)}, bf16[4,8,8,1152]{3,2,1,0:T(8,128)(2,1)S(1)}, u32[]{:S(2)}, u32[]{:S(2)}) collective-permute-start(bf16[4,8,8,1152]{3,2,1,0:T(8,128)(2,1)S(1)} %get-tuple-element.32), channel_id=1, source_target_pairs={{0,1},{1,0},{2,3},{3,2},{4,5},{5,4},{6,7},{7,6},{8,9},{9,8},{10,11... | collective-permute-start | bytes 1769480 | tf_op jit(solution)/shard_map/ppermute | solution.py:283
  6.2 38.4 %copy-start = (bf16[2,1024,1024]{2,1,0:T(8,128)(2,1)S(1)}, bf16[2,1024,1024]{2,1,0:T(8,128)(2,1)}, u32[]{:S(2)}) copy-start(bf16[2,1024,1024]{2,1,0:T(8,128)(2,1)} %win_ref.1) | copy-start | bytes 12582916
  6.2 38.4 %copy-start.1 = (bf16[2,1024,1024]{2,1,0:T(8,128)(2,1)S(1)}, bf16[2,1024,1024]{2,1,0:T(8,128)(2,1)}, u32[]{:S(2)}) copy-start(bf16[2,1024,1024]{2,1,0:T(8,128)(2,1)} %wout_ref.1) | copy-start | bytes 12582916
  6.9 7.2 %collective-permute-start.1 = (bf16[8,8,1152]{2,1,0:T(8,128)(2,1)S(1)}, bf16[8,8,1152]{2,1,0:T(8,128)(2,1)S(1)}, u32[]{:S(2)}, u32[]{:S(2)}) collective-permute-start(bf16[8,8,1152]{2,1,0:T(8,128)(2,1)S(1)} %get-tuple-element.34), channel_id=1, source_target_pairs={{0,2},{2,4},{4,6},{6,0},{1,3},{3,5},{5,7},{7,1},{8,10},{10,12},{12... | collective-permute-start | bytes 442376 | tf_op jit(solution)/shard_map/ppermute | solution.py:254
  8.6 9.9 %collective-permute-start.2 = (bf16[8,8,1152]{2,1,0:T(8,128)(2,1)S(1)}, bf16[8,8,1152]{2,1,0:T(8,128)(2,1)S(1)}, u32[]{:S(2)}, u32[]{:S(2)}) collective-permute-start(bf16[8,8,1152]{2,1,0:T(8,128)(2,1)S(1)} %get-tuple-element.35), channel_id=1, source_target_pairs={{0,4},{2,6},{4,0},{6,2},{1,5},{3,7},{5,1},{7,3},{8,12},{10,14},{12... | collective-permute-start | bytes 442376 | tf_op jit(solution)/shard_map/ppermute | solution.py:254
  11.5 7.0 %collective-permute-start.3 = (bf16[8,8,1152]{2,1,0:T(8,128)(2,1)S(1)}, bf16[8,8,1152]{2,1,0:T(8,128)(2,1)S(1)}, u32[]{:S(2)}, u32[]{:S(2)}) collective-permute-start(bf16[8,8,1152]{2,1,0:T(8,128)(2,1)S(1)} %get-tuple-element.36), channel_id=1, source_target_pairs={{0,6},{2,0},{4,2},{6,4},{1,7},{3,1},{5,3},{7,5},{8,14},{10,8},{12,... | collective-permute-start | bytes 442376 | tf_op jit(solution)/shard_map/ppermute | solution.py:254
  36.6 38.3 %copy-start.2 = (bf16[1,512,1024]{2,1,0:T(8,128)(2,1)S(1)}, bf16[1,512,1024]{2,1,0:T(8,128)(2,1)}, u32[]{:S(2)}) copy-start(bf16[1,512,1024]{2,1,0:T(8,128)(2,1)} %param.5) | copy-start | bytes 3145732
  36.6 38.3 %copy-start.3 = (bf16[1,512,1024]{2,1,0:T(8,128)(2,1)S(1)}, bf16[1,512,1024]{2,1,0:T(8,128)(2,1)}, u32[]{:S(2)}) copy-start(bf16[1,512,1024]{2,1,0:T(8,128)(2,1)} %param.9) | copy-start | bytes 3145732
  36.6 3.8 %collective-permute-start.4 = (bf16[8,1024]{1,0:T(8,128)(2,1)S(1)}, bf16[8,1024]{1,0:T(8,128)(2,1)S(1)}, u32[]{:S(2)}, u32[]{:S(2)}) collective-permute-start(bf16[8,1024]{1,0:T(8,128)(2,1)S(1)} %get-tuple-element.37.own_ref), channel_id=1, source_target_pairs={{0,64},{64,128},{128,192},{192,0},{1,65},{65,129},{129,193},{193,1... | collective-permute-start | bytes 49160 | tf_op jit(solution)/shard_map/ppermute | solution.py:254
  37.2 5.2 %collective-permute-start.5 = (bf16[8,1024]{1,0:T(8,128)(2,1)S(1)}, bf16[8,1024]{1,0:T(8,128)(2,1)S(1)}, u32[]{:S(2)}, u32[]{:S(2)}) collective-permute-start(bf16[8,1024]{1,0:T(8,128)(2,1)S(1)} %get-tuple-element.37.own_ref), channel_id=1, source_target_pairs={{0,128},{64,192},{128,0},{192,64},{1,129},{65,193},{129,1},{193,65... | collective-permute-start | bytes 49160 | tf_op jit(solution)/shard_map/ppermute | solution.py:254
  39.6 4.9 %collective-permute-start.6 = (bf16[8,1024]{1,0:T(8,128)(2,1)S(1)}, bf16[8,1024]{1,0:T(8,128)(2,1)S(1)}, u32[]{:S(2)}, u32[]{:S(2)}) collective-permute-start(bf16[8,1024]{1,0:T(8,128)(2,1)S(1)} %get-tuple-element.37.own_ref), channel_id=1, source_target_pairs={{0,192},{64,0},{128,64},{192,128},{1,193},{65,1},{129,65},{193,129... | collective-permute-start | bytes 49160 | tf_op jit(solution)/shard_map/ppermute | solution.py:254
  47.9 34.0 %copy-start.4 = (bf16[1024,256]{1,0:T(8,128)(2,1)S(1)}, bf16[1024,256]{1,0:T(8,128)(2,1)}, u32[]{:S(2)}) copy-start(bf16[1024,256]{1,0:T(8,128)(2,1)} %par_ref.1) | copy-start | bytes 1572868
  47.9 5.0 %collective-permute-start.7 = (bf16[8,1024]{1,0:T(8,128)(2,1)S(1)}, bf16[8,1024]{1,0:T(8,128)(2,1)S(1)}, u32[]{:S(2)}, u32[]{:S(2)}) collective-permute-start(bf16[8,1024]{1,0:T(8,128)(2,1)S(1)} %get-tuple-element.39), channel_id=1, source_target_pairs={{0,192},{64,0},{128,64},{192,128},{1,193},{65,1},{129,65},{193,129... | collective-permute-start | bytes 49160 | tf_op jit(solution)/shard_map/ppermute | solution.py:254
  48.0 5.3 %collective-permute-start.8 = (bf16[8,1024]{1,0:T(8,128)(2,1)S(1)}, bf16[8,1024]{1,0:T(8,128)(2,1)S(1)}, u32[]{:S(2)}, u32[]{:S(2)}) collective-permute-start(bf16[8,1024]{1,0:T(8,128)(2,1)S(1)} %get-tuple-element.40), channel_id=1, source_target_pairs={{0,128},{64,192},{128,0},{192,64},{1,129},{65,193},{129,1},{193,65... | collective-permute-start | bytes 49160 | tf_op jit(solution)/shard_map/ppermute | solution.py:254
  50.0 3.9 %collective-permute-start.9 = (bf16[8,1024]{1,0:T(8,128)(2,1)S(1)}, bf16[8,1024]{1,0:T(8,128)(2,1)S(1)}, u32[]{:S(2)}, u32[]{:S(2)}) collective-permute-start(bf16[8,1024]{1,0:T(8,128)(2,1)S(1)} %get-tuple-element.41), channel_id=1, source_target_pairs={{0,64},{64,128},{128,192},{192,0},{1,65},{65,129},{129,193},{193,1... | collective-permute-start | bytes 49160 | tf_op jit(solution)/shard_map/ppermute | solution.py:254
  72.9 2.0 %collective-permute-start.10 = (bf16[32,8,1152]{2,1,0:T(8,128)(2,1)S(1)}, bf16[32,8,1152]{2,1,0:T(8,128)(2,1)S(1)}, u32[]{:S(2)}, u32[]{:S(2)}) collective-permute-start(bf16[32,8,1152]{2,1,0:T(8,128)(2,1)S(1)} %all_to_all.16.own_ref), channel_id=1, source_target_pairs={{0,1},{1,0},{2,3},{3,2},{4,5},{5,4},{6,7},{7,6},{8,9},{9,8},{10,11... | collective-permute-start | bytes 1769480 | tf_op jit(solution)/shard_map/ppermute | solution.py:301
  76.3 1.6 %collective-permute-start.11 = (bf16[4,32,8,128]{3,2,1,0:T(8,128)(2,1)S(1)}, bf16[4,32,8,128]{3,2,1,0:T(8,128)(2,1)S(1)}, u32[]{:S(2)}, u32[]{:S(2)}) collective-permute-start(bf16[4,32,8,128]{3,2,1,0:T(8,128)(2,1)S(1)} %get-tuple-element.52), channel_id=1, source_target_pairs={{0,1},{1,0},{2,3},{3,2},{4,5},{5,4},{6,7},{7,6},{8,9},{9,8},{10,11... | collective-permute-start | bytes 786440 | tf_op jit(solution)/shard_map/ppermute | solution.py:310
  78.0 6.2 %collective-permute-start.12 = (bf16[32,8,128]{2,1,0:T(8,128)(2,1)S(1)}, bf16[32,8,128]{2,1,0:T(8,128)(2,1)S(1)}, u32[]{:S(2)}, u32[]{:S(2)}) collective-permute-start(bf16[32,8,128]{2,1,0:T(8,128)(2,1)S(1)} %get-tuple-element.54), channel_id=1, source_target_pairs={{0,64},{64,128},{128,192},{192,0},{1,65},{65,129},{129,193},{193,1... | collective-permute-start | bytes 196616 | tf_op jit(solution)/shard_map/ppermute | solution.py:254
  80.5 6.2 %collective-permute-start.13 = (bf16[32,8,128]{2,1,0:T(8,128)(2,1)S(1)}, bf16[32,8,128]{2,1,0:T(8,128)(2,1)S(1)}, u32[]{:S(2)}, u32[]{:S(2)}) collective-permute-start(bf16[32,8,128]{2,1,0:T(8,128)(2,1)S(1)} %get-tuple-element.55), channel_id=1, source_target_pairs={{0,128},{64,192},{128,0},{192,64},{1,129},{65,193},{129,1},{193,65... | collective-permute-start | bytes 196616 | tf_op jit(solution)/shard_map/ppermute | solution.py:254
  81.9 5.5 %collective-permute-start.14 = (bf16[32,8,128]{2,1,0:T(8,128)(2,1)S(1)}, bf16[32,8,128]{2,1,0:T(8,128)(2,1)S(1)}, u32[]{:S(2)}, u32[]{:S(2)}) collective-permute-start(bf16[32,8,128]{2,1,0:T(8,128)(2,1)S(1)} %get-tuple-element.56), channel_id=1, source_target_pairs={{0,192},{64,0},{128,64},{192,128},{1,193},{65,1},{129,65},{193,129... | collective-permute-start | bytes 196616 | tf_op jit(solution)/shard_map/ppermute | solution.py:254

commit v5 on v3

--- a/solution.py
+++ b/solution.py
@@ -56,8 +56,8 @@
     return pltpu.roll(value, 4, 1)
 
 
-def reduce_tokens(tok_hbm, cot_hbm, par_hbm, keep_ref, send_ref, logit_ref,
-                  tok_ref, cot_ref, par_ref, comb_ref, sems):
+def reduce_tokens(tok_hbm, cot_hbm, par_hbm, *refs):
+    *refs, logit_ref, tok_ref, cot_ref, par_ref, comb_ref, all_ref, sems = refs
     core = lax.axis_index("c")
     count, width = tok_ref.shape
     n = par_ref.shape[1]
@@ -87,63 +87,99 @@
     diag = jnp.where(iota((n, n), 0) == iota((n, n), 1), refpoint, 0.0).astype(BF)
     point = dot(diag, jnp.ones((n, STAT), BF))
     high, low = split(total)
-    side = stats(iota((n, STAT), 1), point, high, low).reshape(n // 8, 8, STAT)
     copies[1 + PARTS].wait()
     dslot = dot(comb_ref[...], cot_ref[...], ((0,), (0,))).reshape(n // 8, 8, width)
     upper = iota((1, 8, 1), 1) < 4
     zero = core == 0
     even = jnp.where(upper, numer, swap_halves(dslot)).astype(BF)
     odd = jnp.where(upper, swap_halves(numer), dslot).astype(BF)
-    even_side = jnp.where(upper, side, 0.0).astype(BF)
-    odd_side = jnp.where(upper, swap_halves(side), 0.0).astype(BF)
-    even = jnp.concatenate([even, even_side], axis=2)
-    odd = jnp.concatenate([odd, odd_side], axis=2)
-    for ref, value in ((keep_ref, jnp.where(zero, even, odd)), (send_ref, jnp.where(zero, odd, even))):
-        value = value.reshape(n // 8 // ref.shape[0], *ref.shape[:1], 8, width + STAT)
-        for y in range(ref.shape[0]):
-            ref[y] = value[:, y]
-
-
-def merge(parts):
-    width = parts[0].shape[-1] - STAT
-    points = [p[..., width:width + 1] for p in parts]
-    top = points[0]
-    for point in points[1:]:
-        top = jnp.maximum(top, point)
-    body, total = 0.0, 0.0
-    for part, point in zip(parts, points):
-        scale = jnp.exp(point - top)
-        body += scale * part[..., :width]
-        total += scale * (part[..., width + 1:width + 2] + part[..., width + 2:width + 3])
-    return body, top, total
-
-
-def store_merged(parts, out_ref):
-    body, top, total = merge(parts)
-    width = body.shape[-1]
+    sides = [value.reshape(n // 8, 8, STAT) for value in (point, high, low)]
+    even_sides = [jnp.where(upper, value, 0.0) for value in sides]
+    odd_sides = [jnp.where(upper, swap_halves(value), 0.0) for value in sides]
+    columns = all_ref.shape[1]
+    depth = n // 8 // columns
+    keep = jnp.where(zero, even, odd)
+    send = jnp.where(zero, odd, even)
+    keep_sides = [jnp.where(zero, e, o) for e, o in zip(even_sides, odd_sides)]
+    send_sides = [jnp.where(zero, o, e) for e, o in zip(even_sides, odd_sides)]
+    lane = iota((8, STAT), 1)
+    for which, (value, marks) in enumerate(((keep, keep_sides), (send, send_sides))):
+        for y in range(columns):
+            for z in range(depth):
+                for j in range(width // STAT):
+                    all_ref[which, y, z * (width // STAT) + j] = value[z * columns + y, :, j * STAT:(j + 1) * STAT]
+            tile = jnp.zeros((8, STAT), F32)
+            for i, mark in enumerate(marks):
+                for z in range(depth):
+                    tile = jnp.where(lane == i * depth + z, mark[z * columns + y], tile)
+            all_ref[which, y, depth * (width // STAT)] = tile.astype(BF)
+    here = lax.axis_index("y")
+    for k in range(columns):
+        to = lax.rem(here + k, columns)
+        refs[k][...] = all_ref[0, to]
+        refs[columns + k][...] = all_ref[1, to]
+
+
+def merge_tiles(parts):
+    count = parts[0].shape[0] - 1
+    groups = 8
+    marks = [p[count].astype(F32) for p in parts]
+    top = marks[0]
+    for mark in marks[1:]:
+        top = jnp.maximum(top, mark)
+    scales = [jnp.exp(mark - top) for mark in marks]
+    total = 0.0
+    for scale, mark in zip(scales, marks):
+        total += scale * (pltpu.roll(mark, STAT - groups, 1) + pltpu.roll(mark, STAT - 2 * groups, 1))
+    size = count // groups
+    bodies = []
+    for z in range(groups):
+        body = 0.0
+        for scale, part in zip(scales, parts):
+            body += scale[:, z:z + 1][None] * part[z * size:(z + 1) * size].astype(F32)
+        bodies.append(body.astype(BF))
     high, low = split(total)
-    out_ref[..., :width] = body.astype(BF)
-    lane = iota(body.shape[:-1] + (STAT,), body.ndim - 1)
-    out_ref[..., width:] = stats(lane, top, high, low).astype(BF)
+    return bodies, top, high, low
 
 
 def merge_cores(a_ref, b_ref, out_ref):
-    store_merged([a_ref[...].astype(F32), b_ref[...].astype(F32)], out_ref)
-
-
-def merge_columns(in_ref, out_ref):
-    store_merged([in_ref[i].astype(F32) for i in range(in_ref.shape[0])], out_ref)
+    bodies, top, high, low = merge_tiles([a_ref, b_ref])
+    size = bodies[0].shape[0]
+    for z, body in enumerate(bodies):
+        out_ref[z * size:(z + 1) * size] = body
+    lane = iota(top.shape, 1)
+    mark = jnp.where(lane < 16, pltpu.roll(high, 8, 1), jnp.where(lane < 24, pltpu.roll(low, 16, 1), 0.0))
+    out_ref[len(bodies) * size] = jnp.where(lane < 8, top, mark).astype(BF)
+
+
+def merge_columns(a_ref, b_ref, c_ref, d_ref, out_ref):
+    bodies, top, high, low = merge_tiles([a_ref, b_ref, c_ref, d_ref])
+    size = bodies[0].shape[0]
+    lane = iota(top.shape, 1)
+    for z, body in enumerate(bodies):
+        out_ref[z, :size] = body
+        out_ref[z, size] = stats(lane, top[:, z:z + 1], high[:, z:z + 1], low[:, z:z + 1]).astype(BF)
 
 
 def merge_shards(in_ref, pay_ref, full_ref, side_ref):
-    acc, top, total = merge([in_ref[i].astype(F32) for i in range(in_ref.shape[0])])
-    slots = acc.shape[0] // 2
+    size = in_ref.shape[1] - 1
+    marks = [in_ref[i, size].astype(F32) for i in range(in_ref.shape[0])]
+    top = marks[0][:, 0:1]
+    for mark in marks[1:]:
+        top = jnp.maximum(top, mark[:, 0:1])
+    acc, total = 0.0, 0.0
+    for i, mark in enumerate(marks):
+        scale = jnp.exp(mark[:, 0:1] - top)
+        acc += scale[None] * in_ref[i, :size].astype(F32)
+        total += scale * (mark[:, 1:2] + mark[:, 2:3])
+    slots = total.shape[0] // 2
     first = iota((2 * slots, 1), 0) < slots
-    full = acc / jnp.where(first, total, 1.0)
-    full_ref[...] = full
+    full = acc / jnp.where(first, total, 1.0)[None]
+    for j in range(size):
+        full_ref[:, j * STAT:(j + 1) * STAT] = full[j]
+        pay_ref[:, j * STAT:(j + 1) * STAT] = full[j].astype(BF)
     both = jnp.concatenate([total[:slots], total[:slots]], axis=0)
     side_ref[...] = jnp.where(iota((2 * slots, STAT), 1) == 0, top, both)
-    pay_ref[...] = full.astype(BF)
 
 
 def gelu_parts(u):
@@ -186,8 +222,8 @@
     out_ref[...] = jnp.broadcast_to(block[None], out_ref.shape)
 
 
-def token_grads(logit_ref, tok_ref, cot_ref, own_ref, oth_ref,
-                keep_ref, send_ref, dlog_ref, dexp_ref, comb_ref, so_ref, sc_ref):
+def token_grads(logit_ref, tok_ref, cot_ref, own_ref, oth_ref, *refs):
+    *out_refs, dlog_ref, dexp_ref, comb_ref, so_ref, sc_ref, all_ref = refs
     core = lax.axis_index("c")
     logits, tok = logit_ref[...], tok_ref[...]
     n = logits.shape[1]
@@ -216,8 +252,13 @@
     left, right = gp[:, :, :n // 2], gp[:, :, n // 2:]
     even = jnp.where(upper, left, swap_halves(right)).astype(BF)
     odd = jnp.where(upper, swap_halves(left), right).astype(BF)
-    keep_ref[...] = jnp.where(zero, even, odd).reshape(keep_ref.shape)
-    send_ref[...] = jnp.where(zero, odd, even).reshape(send_ref.shape)
+    all_ref[0] = jnp.where(zero, even, odd).reshape(all_ref.shape[1:])
+    all_ref[1] = jnp.where(zero, odd, even).reshape(all_ref.shape[1:])
+    here, steps = lax.axis_index("x"), all_ref.shape[1]
+    for k in range(steps):
+        to = lax.rem(here + k, steps)
+        out_refs[k][...] = all_ref[0, to]
+        out_refs[steps + k][...] = all_ref[1, to]
 
 
 def token_outputs(comb_ref, so_ref, dlog_ref, par_ref, dexp_ref, sc_ref, mixed_ref, grad_ref):
@@ -226,11 +267,8 @@
     grad_ref[...] = (grad + dot(dexp_ref[...], sc_ref[...])).astype(BF)
 
 
-def add_halves(a_ref, b_ref, *out_refs):
-    here = lax.axis_index("x")
-    for k, ref in enumerate(out_refs):
-        to = lax.rem(here + k, len(out_refs))
-        ref[...] = (a_ref[to].astype(F32) + b_ref[to].astype(F32)).astype(BF)
+def add_halves(a_ref, b_ref, out_ref):
+    out_ref[...] = (a_ref[...].astype(F32) + b_ref[...].astype(F32)).astype(BF)
 
 
 def add_rows(own_ref, a_ref, b_ref, c_ref, after_ref, out_ref):
@@ -247,8 +285,8 @@
     out_ref[:, half:] = total[4:]
 
 
-def shifted(value, step, size):
-    return lax.ppermute(value, "x", [(i, (i + step) % size) for i in range(size)])
+def shifted(value, step, size, axis="x"):
+    return lax.ppermute(value, axis, [(i, (i + step) % size) for i in range(size)])
 
 
 def on_device(tokens, slot_parameters, w_in, w_out, grad_out):
@@ -264,23 +302,31 @@
     swap = [(0, 1), (1, 0)]
 
     vmem = pl.BlockSpec(memory_space=pltpu.VMEM)
-    keep, send, logits = pl.pallas_call(
+    tiles = (depth * (width // STAT) + 1, 8, STAT)
+    *blocks, logits = pl.pallas_call(
         reduce_tokens,
-        out_shape=[shape((rows_y, depth, 8, wide), BF), shape((rows_y, depth, 8, wide), BF), shape((count, n), F32)],
+        out_shape=[shape(tiles, BF)] * (2 * rows_y) + [shape((count, n), F32)],
         in_specs=[pl.BlockSpec(memory_space=pltpu.HBM)] * 3,
-        out_specs=[vmem] * 3,
+        out_specs=[vmem] * (2 * rows_y + 1),
         scratch_shapes=[
             pltpu.VMEM((count, width), BF), pltpu.VMEM((count, width), BF),
             pltpu.VMEM((width, n), BF), pltpu.VMEM((count, n), BF),
+            pltpu.VMEM((2, rows_y) + tiles, BF),
             pltpu.SemaphoreType.DMA((PARTS + 2,)),
         ],
         compiler_params=PARAMS,
         cost_estimate=pl.CostEstimate(flops=4 * unit, bytes_accessed=4 << 20, transcendentals=0),
     )(*[pltpu.with_memory_space_constraint(a, pltpu.HBM) for a in (tok, cot, slot_parameters)])
-    other = lax.ppermute(send, "c", swap)
-    (merged,) = call(merge_cores, [shape(keep.shape, BF)], keep, other, flops=40 * unit)
-    columns = lax.all_to_all(merged, "y", 0, 0, tiled=True)
-    (merged,) = call(merge_columns, [shape((depth, 8, wide), BF)], columns)
+    order = sorted(range(rows_y), key=lambda k: -min(k, rows_y - k))
+    others = {k: lax.ppermute(blocks[rows_y + k], "c", swap) for k in order}
+    shares = {}
+    for k in order:
+        (share,) = call(merge_cores, [shape(tiles, BF)], blocks[k], others[k], flops=10 * unit)
+        shares[k] = shifted(share, k, rows_y, "y") if k else share
+    (merged,) = call(
+        merge_columns, [shape((depth, width // STAT + 1, 8, STAT), BF)],
+        *[shares[k] for k in range(rows_y)],
+    )
     shards = lax.all_to_all(merged, "z", 0, 0, tiled=True)
     pay, full, side = call(
         merge_shards,
@@ -297,28 +343,33 @@
     mine = lax.all_to_all(block, ZY, 0, 0, tiled=True)
     theirs = lax.ppermute(mine, "c", swap)
 
-    gp_keep, gp_send, dlog, dexp, comb, slot_out, scaled = call(
+    quarter = shape((owners, 8, n // 2), BF)
+    *quarters, dlog, dexp, comb, slot_out, scaled = call(
         token_grads,
-        [shape((videos, owners, 8, n // 2), BF), shape((videos, owners, 8, n // 2), BF),
-         shape((count, n), BF), shape((count, n), BF), shape((count, n), BF),
-         shape((n, width), BF), shape((n, width), BF)],
+        [quarter] * (2 * videos)
+        + [shape((count, n), BF), shape((count, n), BF), shape((count, n), BF),
+           shape((n, width), BF), shape((n, width), BF)],
         logits, tok, cot, mine, theirs, flops=5 * unit,
-    )
-    gp_other = lax.ppermute(gp_send, "c", swap)
+        scratch=[pltpu.VMEM((2, videos) + quarter.shape, BF)],
+    )
+    order = sorted(range(videos), key=lambda k: -min(k, videos - k))
+    others = {k: lax.ppermute(quarters[videos + k], "c", swap) for k in order}
+    shares = {}
+    for k in order:
+        (share,) = call(add_halves, [quarter], quarters[k], others[k])
+        shares[k] = shifted(share, k, videos) if k else share
     mixed, grad_tokens = call(
         token_outputs,
         [shape((count, width), BF), shape((count, width), BF)],
         comb, slot_out, dlog, slot_parameters, dexp, scaled, flops=3 * unit,
     )
-    quarters = call(add_halves, [shape(gp_keep.shape[1:], BF)] * videos, gp_keep, gp_other)
-    arrived = [shifted(quarters[k], k, videos) for k in range(1, videos)]
     half = pl.pallas_call(
         add_rows,
-        out_shape=shape(gp_keep.shape[1:], BF),
+        out_shape=quarter,
         in_specs=[vmem] * videos + [pl.BlockSpec(memory_space=pltpu.HBM)],
         out_specs=vmem,
         compiler_params=PARAMS,
-    )(quarters[0], *arrived, pltpu.with_memory_space_constraint(mixed, pltpu.HBM))
+    )(*[shares[k] for k in range(videos)], pltpu.with_memory_space_constraint(mixed, pltpu.HBM))
     pieces = lax.all_to_all(half, ZY, 0, 0, tiled=True)
     (grad_params,) = call(sum_pieces, [shape((4, n), F32)], pieces)
     return mixed[None], grad_tokens[None], grad_params

time: 104 us -> 100 us (0.962); the launches traced: 103 us -> 100 us
  blocking collectives: 64.1 us -> 50.6 us
  starting transfers between devices: 11.6 us -> 20.3 us
  waiting for transfers between devices: 13.7 us -> 15.6 us
    all_to_all x1 -> x0, blocking collectives: 15 us -> none  [on_device(): columns = lax.all_to_all(merged, 'y', 0, 0, tiled=True)]
    ppermute x11 -> x20, starting transfers between devices: 11.5 us -> 20.3 us  [the longest x12 18.1 us: shifted(): lax.ppermute(value, axis, [(i, (i + step) % size) for i in range(size)])]
    ppermute x11 -> x20, waiting for transfers between devices: 11.7 us -> 13.6 us  [the longest x12 13 us: shifted(): lax.ppermute(value, axis, [(i, (i + step) % size) for i in range(size)])]
    all_to_all x1, blocking collectives: 17.5 us -> 18.8 us  [on_device(): mine = lax.all_to_all(block, ZY, 0, 0, tiled=True)]
    pallas_call x9 -> x15, Pallas kernels: 9.01 us -> 8.99 us  [call(): pl.pallas_call(body, out_shape=outs, in_specs=[pl.BlockSpec(memory_space=...]
  transfers between devices with their start and end apart: 12 -> 21, of which waited for: 11 -> 12; matrix products, arithmetic and copies ran while one was open for 0% -> 0% of each run, Pallas kernels for 2% -> 3%
where the time goes in v5:
time: 100 us
  blocking collectives  50.6 us (51%)
  starting transfers between devices  20.3 us (20%)
  waiting for transfers between devices  15.6 us (16%)
  Pallas kernels  12.6 us (13%)
    all_to_all x1, blocking collectives, on_device(): mine = lax.all_to_all(block, ZY, 0, 0, tiled=True)  18.8 us
    ppermute x12, starting transfers between devices, shifted(): lax.ppermute(value, axis, [(i, (i + step) % size) for i in range(size)])  18.1 us
    all_to_all x1, blocking collectives, on_device(): shards = lax.all_to_all(merged, 'z', 0, 0, tiled=True)  17.5 us
    all_to_all x1, blocking collectives, on_device(): pieces = lax.all_to_all(half, ZY, 0, 0, tiled=True)  14.3 us
    ppermute x12, waiting for transfers between devices, shifted(): lax.ppermute(value, axis, [(i, (i + step) % size) for i in range(size)])  13 us
    pallas_call x15, Pallas kernels, call(): pl.pallas_call(body, out_shape=outs, in_specs=[pl.BlockSpec(memory_space=...  8.99 us
    pallas_call x1, Pallas kernels, on_device(): pl.pallas_call(reduce_tokens, out_shape=[shape(tiles, BF)] * (2 * rows_y)...  3.61 us
    ppermute x1, waiting for transfers between devices, on_device(): theirs = lax.ppermute(mine, 'c', swap)  2 us
  transfers between devices with their start and end apart: 21, of which 12 were waited for; matrix products, arithmetic and copies ran while one was open for 0% of the time, Pallas kernels for 3%

profile of v5, /device:TPU:6, one launch (start us, length us, event | category | flops | bytes accessed | tf_op | source)
XLA Modules:
  0.0 100.0 jit_solution(116375388306699432)
XLA Ops:
  0.6 3.6 %shard_map.76 = (bf16[65,8,128]{2,1,0:T(8,128)(2,1)S(1)}, bf16[65,8,128]{2,1,0:T(8,128)(2,1)S(1)}, bf16[65,8,128]{2,1,0:T(8,128)(2,1)S(1)}, bf16[65,8,128]{2,1,0...) custom-call(bf16[512,1024]{1,0:T(8,128)(2,1)} %bitcast.4, ...), custom_call_target="tpu_custom_call" | custom-call | flops 1073741824 | bytes 4194304 | tf_op jit(solution)/shard_map/pallas_call | solution.py:306
  4.2 0.1 collective-permute-start.1
  4.3 0.5 collective-permute-start
  4.8 0.1 collective-permute-start.3
  4.9 0.4 collective-permute-start.5
  5.4 0.3 collective-permute-done.1.b_ref
  5.7 0.1 shard_map.78
  5.8 1.7 %collective-permute-start.2 = (bf16[65,8,128]{2,1,0:T(8,128)(2,1)S(1)}, bf16[65,8,128]{2,1,0:T(8,128)(2,1)S(1)}, u32[]{:S(2)}, u32[]{:S(2)}) collective-permute-start(bf16[65,8,128]{2,1,0:T(8,128)(2,1)S(1)} %shard_map.78), channel_id=1, source_target_pairs={{0,2},{2,4},{4,6},{6,0},{1,3},{3,5},{5,7},{7,1},{8,10},{10,12},{12... | collective-permute-start | bytes 399368 | tf_op jit(solution)/shard_map/ppermute | solution.py:289
  7.5 0.0 collective-permute-done.3.b_ref
  7.5 0.1 shard_map.79
  7.6 3.0 %collective-permute-start.4 = (bf16[65,8,128]{2,1,0:T(8,128)(2,1)S(1)}, bf16[65,8,128]{2,1,0:T(8,128)(2,1)S(1)}, u32[]{:S(2)}, u32[]{:S(2)}) collective-permute-start(bf16[65,8,128]{2,1,0:T(8,128)(2,1)S(1)} %shard_map.79), channel_id=1, source_target_pairs={{0,4},{2,6},{4,0},{6,2},{1,5},{3,7},{5,1},{7,3},{8,12},{10,14},{12... | collective-permute-start | bytes 399368 | tf_op jit(solution)/shard_map/ppermute | solution.py:289
  10.6 0.0 collective-permute-done.5.b_ref
  10.6 0.1 shard_map.80
  10.8 1.4 %collective-permute-start.6 = (bf16[65,8,128]{2,1,0:T(8,128)(2,1)S(1)}, bf16[65,8,128]{2,1,0:T(8,128)(2,1)S(1)}, u32[]{:S(2)}, u32[]{:S(2)}) collective-permute-start(bf16[65,8,128]{2,1,0:T(8,128)(2,1)S(1)} %shard_map.80), channel_id=1, source_target_pairs={{0,6},{2,0},{4,2},{6,4},{1,7},{3,1},{5,3},{7,5},{8,14},{10,8},{12,... | collective-permute-start | bytes 399368 | tf_op jit(solution)/shard_map/ppermute | solution.py:289
  12.2 0.0 collective-permute-done.b_ref
  12.2 0.1 shard_map.77.a_ref
  12.3 0.5 collective-permute-done.2.b_ref
  12.8 4.0 %collective-permute-done.4.c_ref = bf16[65,8,128]{2,1,0:T(8,128)(2,1)S(1)} collective-permute-done((bf16[65,8,128]{2,1,0:T(8,128)(2,1)S(1)}, bf16[65,8,128]{2,1,0:T(8,128)(2,1)S(1)}, u32[]{:S(2)}, u32[]{:S(2)}) %collective-permute-start.4) | collective-permute-done | bytes 133152 | tf_op jit(solution)/shard_map/ppermute | solution.py:289
  16.8 0.0 collective-permute-done.6.d_ref
  16.8 0.2 shard_map.81
  17.0 17.5 %all_to_all.15.in_ref = bf16[8,9,8,128]{3,2,1,0:T(8,128)(2,1)S(1)} all-to-all(bf16[8,9,8,128]{3,2,1,0:T(8,128)(2,1)S(1)} %shard_map.81), channel_id=1, replica_groups=mesh['x'=4,'z'=8,'y'=4,'c'=2] {'z'}, dimensions={0} | all-to-all | bytes 294912 | tf_op jit(solution)/shard_map/all_to_all | solution.py:330
  34.5 0.2 shard_map.82
  34.8 0.0 copy-start.2
  34.8 0.0 copy-start.3
  34.8 0.9 collective-permute-start.9
  35.7 1.1 %collective-permute-start.8 = (bf16[8,1024]{1,0:T(8,128)(2,1)S(1)}, bf16[8,1024]{1,0:T(8,128)(2,1)S(1)}, u32[]{:S(2)}, u32[]{:S(2)}) collective-permute-start(bf16[8,1024]{1,0:T(8,128)(2,1)S(1)} %get-tuple-element.43.own_ref), channel_id=1, source_target_pairs={{0,128},{64,192},{128,0},{192,64},{1,129},{65,193},{129,1},{193,65... | collective-permute-start | bytes 49160 | tf_op jit(solution)/shard_map/ppermute | solution.py:289
  36.8 2.1 %collective-permute-start.7 = (bf16[8,1024]{1,0:T(8,128)(2,1)S(1)}, bf16[8,1024]{1,0:T(8,128)(2,1)S(1)}, u32[]{:S(2)}, u32[]{:S(2)}) collective-permute-start(bf16[8,1024]{1,0:T(8,128)(2,1)S(1)} %get-tuple-element.43.own_ref), channel_id=1, source_target_pairs={{0,64},{64,128},{128,192},{192,0},{1,65},{65,129},{129,193},{193,1... | collective-permute-start | bytes 49160 | tf_op jit(solution)/shard_map/ppermute | solution.py:289
  38.9 0.9 collective-permute-done.9.c_ref
  39.8 1.1 %collective-permute-done.8.b_ref = bf16[8,1024]{1,0:T(8,128)(2,1)S(1)} collective-permute-done((bf16[8,1024]{1,0:T(8,128)(2,1)S(1)}, bf16[8,1024]{1,0:T(8,128)(2,1)S(1)}, u32[]{:S(2)}, u32[]{:S(2)}) %collective-permute-start.8) | collective-permute-done | bytes 16416 | tf_op jit(solution)/shard_map/ppermute | solution.py:289
  41.0 0.0 collective-permute-done.7.a_ref
  41.0 0.0 copy-done
  41.0 0.0 copy-done.1
  41.0 3.4 %shard_map.83 = (bf16[8,1024]{1,0:T(8,128)(2,1)S(1)}, bf16[8,1024]{1,0:T(8,128)(2,1)S(1)}, bf16[8,1024]{1,0:T(8,128)(2,1)S(1)}, bf16[8,1024]{1,0:T(8,128)(2,1)S(1)}) custom-call(bf16[8,1024]{1,0:T(8,128)(2,1)S(1)} %get-tuple-element.43.own_ref, bf16[8,1024]{1,0:T(8,128)(2,1)S(1)} %collective-permute-done.7.a_ref, ...), custom_call_target="tpu_custom_call" | custom-call | flops 268435456 | bytes 8585216 | tf_op jit(solution)/shard_map/pallas_call | solution.py:30
  44.4 1.8 %collective-permute-start.10 = (bf16[8,1024]{1,0:T(8,128)(2,1)S(1)}, bf16[8,1024]{1,0:T(8,128)(2,1)S(1)}, u32[]{:S(2)}, u32[]{:S(2)}) collective-permute-start(bf16[8,1024]{1,0:T(8,128)(2,1)S(1)} %get-tuple-element.45), channel_id=1, source_target_pairs={{0,192},{64,0},{128,64},{192,128},{1,193},{65,1},{129,65},{193,129... | collective-permute-start | bytes 49160 | tf_op jit(solution)/shard_map/ppermute | solution.py:289
  46.2 2.6 %collective-permute-start.11 = (bf16[8,1024]{1,0:T(8,128)(2,1)S(1)}, bf16[8,1024]{1,0:T(8,128)(2,1)S(1)}, u32[]{:S(2)}, u32[]{:S(2)}) collective-permute-start(bf16[8,1024]{1,0:T(8,128)(2,1)S(1)} %get-tuple-element.46), channel_id=1, source_target_pairs={{0,128},{64,192},{128,0},{192,64},{1,129},{65,193},{129,1},{193,65... | collective-permute-start | bytes 49160 | tf_op jit(solution)/shard_map/ppermute | solution.py:289
  48.8 0.3 collective-permute-start.12
  49.1 0.2 collective-permute-done.10.a_ref
  49.4 2.0 %collective-permute-done.11.b_ref = bf16[8,1024]{1,0:T(8,128)(2,1)S(1)} collective-permute-done((bf16[8,1024]{1,0:T(8,128)(2,1)S(1)}, bf16[8,1024]{1,0:T(8,128)(2,1)S(1)}, u32[]{:S(2)}, u32[]{:S(2)}) %collective-permute-start.11) | collective-permute-done | bytes 16416 | tf_op jit(solution)/shard_map/ppermute | solution.py:289
  51.4 1.1 %collective-permute-done.12.c_ref = bf16[8,1024]{1,0:T(8,128)(2,1)S(1)} collective-permute-done((bf16[8,1024]{1,0:T(8,128)(2,1)S(1)}, bf16[8,1024]{1,0:T(8,128)(2,1)S(1)}, u32[]{:S(2)}, u32[]{:S(2)}) %collective-permute-start.12) | collective-permute-done | bytes 16416 | tf_op jit(solution)/shard_map/ppermute | solution.py:289
  52.5 0.3 shard_map.84
  52.8 18.8 %all_to_all.16.own_ref = bf16[32,8,1152]{2,1,0:T(8,128)(2,1)S(1)} all-to-all(bf16[32,8,1152]{2,1,0:T(8,128)(2,1)S(1)} %shard_map.84), channel_id=1, replica_groups=mesh['x'=4,'z'=8,'y'=4,'c'=2] {'z','y'}, dimensions={0} | all-to-all | bytes 1179648 | tf_op jit(solution)/shard_map/all_to_all | solution.py:343
  71.6 0.0 collective-permute-start.13
  71.6 2.0 %collective-permute-done.13.oth_ref = bf16[32,8,1152]{2,1,0:T(8,128)(2,1)S(1)} collective-permute-done((bf16[32,8,1152]{2,1,0:T(8,128)(2,1)S(1)}, bf16[32,8,1152]{2,1,0:T(8,128)(2,1)S(1)}, u32[]{:S(2)}, u32[]{:S(2)}) %collective-permute-start.13) | collective-permute-done | bytes 589856 | tf_op jit(solution)/shard_map/ppermute | solution.py:344
  73.6 0.0 copy-done.2
  73.6 0.0 copy-done.3
  73.6 1.5 %shard_map.85 = (bf16[32,8,128]{2,1,0:T(8,128)(2,1)S(1)}, bf16[32,8,128]{2,1,0:T(8,128)(2,1)S(1)}, bf16[32,8,128]{2,1,0:T(8,128)(2,1)S(1)}, bf16[32,8,128]{2,1,0...) custom-call(f32[512,256]{1,0:T(8,128)S(1)} %get-tuple-element.34.log, ...), custom_call_target="tpu_custom_call" | custom-call | flops 1342177280 | bytes 8519680 | tf_op jit(solution)/shard_map/pallas_call | solution.py:30
  75.1 0.2 collective-permute-start.15
  75.4 0.4 collective-permute-start.17
  75.7 0.1 collective-permute-start.19
  75.9 0.4 collective-permute-start.14
  76.3 0.2 collective-permute-done.15.b_ref
  76.5 1.6 %collective-permute-start.16 = (bf16[32,8,128]{2,1,0:T(8,128)(2,1)S(1)}, bf16[32,8,128]{2,1,0:T(8,128)(2,1)S(1)}, u32[]{:S(2)}, u32[]{:S(2)}) collective-permute-start(bf16[32,8,128]{2,1,0:T(8,128)(2,1)S(1)} %shard_map.88), channel_id=1, source_target_pairs={{0,64},{64,128},{128,192},{192,0},{1,65},{65,129},{129,193},{193,1... | collective-permute-start | bytes 196616 | tf_op jit(solution)/shard_map/ppermute | solution.py:289
  78.1 0.0 collective-permute-done.17.b_ref
  78.2 0.4 collective-permute-start.18
  78.5 0.0 collective-permute-done.19.b_ref
  78.6 1.2 %collective-permute-start.20 = (bf16[32,8,128]{2,1,0:T(8,128)(2,1)S(1)}, bf16[32,8,128]{2,1,0:T(8,128)(2,1)S(1)}, u32[]{:S(2)}, u32[]{:S(2)}) collective-permute-start(bf16[32,8,128]{2,1,0:T(8,128)(2,1)S(1)} %shard_map.90), channel_id=1, source_target_pairs={{0,192},{64,0},{128,64},{192,128},{1,193},{65,1},{129,65},{193,129... | collective-permute-start | bytes 196616 | tf_op jit(solution)/shard_map/ppermute | solution.py:289
  79.8 0.0 copy-done.4
  79.8 2.2 %shard_map.86 = (bf16[512,1024]{1,0:T(8,128)(2,1)}, bf16[512,1024]{1,0:T(8,128)(2,1)}) custom-call(bf16[512,256]{1,0:T(8,128)(2,1)S(1)} %get-tuple-element.50.comb_ref, bf16[256,1024]{1,0:T(8,128)(2,1)S(1)} %get-tuple-element.51.so_ref, bf16[512,256]{1,0:T(8,128)(2,1)S(1)} %get-tuple-element.52.dlog_ref, bf16[1024,256]{1,0:T(8,128)(2,1)S(1)} %copy-done.4, ...), custom_call_target="tpu_custom_call" | custom-call | flops 805306368 | bytes 6553600 | tf_op jit(solution)/shard_map/pallas_call | solution.py:30
  81.9 0.0 collective-permute-done.14.b_ref
  82.0 0.0 collective-permute-done.16.a_ref
  82.0 2.6 %collective-permute-done.18.b_ref = bf16[32,8,128]{2,1,0:T(8,128)(2,1)S(1)} collective-permute-done((bf16[32,8,128]{2,1,0:T(8,128)(2,1)S(1)}, bf16[32,8,128]{2,1,0:T(8,128)(2,1)S(1)}, u32[]{:S(2)}, u32[]{:S(2)}) %collective-permute-start.18) | collective-permute-done | bytes 65568 | tf_op jit(solution)/shard_map/ppermute | solution.py:289
  84.5 0.5 collective-permute-done.20.c_ref
  85.1 14.3 %all_to_all.17.in_ref = bf16[32,8,128]{2,1,0:T(8,128)(2,1)S(1)} all-to-all(bf16[32,8,128]{2,1,0:T(8,128)(2,1)S(1)} %shard_map.91), channel_id=1, replica_groups=mesh['x'=4,'z'=8,'y'=4,'c'=2] {'z','y'}, dimensions={0} | all-to-all | bytes 131072 | tf_op jit(solution)/shard_map/all_to_all | solution.py:373
  99.4 0.6 shard_map.92
  (8 shorter events, 0.1 us)
Async XLA Ops:
  4.2 1.4 %collective-permute-start.1 = (bf16[65,8,128]{2,1,0:T(8,128)(2,1)S(1)}, bf16[65,8,128]{2,1,0:T(8,128)(2,1)S(1)}, u32[]{:S(2)}, u32[]{:S(2)}) collective-permute-start(bf16[65,8,128]{2,1,0:T(8,128)(2,1)S(1)} %get-tuple-element.38), channel_id=1, source_target_pairs={{0,1},{1,0},{2,3},{3,2},{4,5},{5,4},{6,7},{7,6},{8,9},{9,8},{10,11... | collective-permute-start | bytes 399368 | tf_op jit(solution)/shard_map/ppermute | solution.py:321
  4.3 7.8 %collective-permute-start = (bf16[65,8,128]{2,1,0:T(8,128)(2,1)S(1)}, bf16[65,8,128]{2,1,0:T(8,128)(2,1)S(1)}, u32[]{:S(2)}, u32[]{:S(2)}) collective-permute-start(bf16[65,8,128]{2,1,0:T(8,128)(2,1)S(1)} %get-tuple-element.36), channel_id=1, source_target_pairs={{0,1},{1,0},{2,3},{3,2},{4,5},{5,4},{6,7},{7,6},{8,9},{9,8},{10,11... | collective-permute-start | bytes 399368 | tf_op jit(solution)/shard_map/ppermute | solution.py:321
  4.8 2.6 %collective-permute-start.3 = (bf16[65,8,128]{2,1,0:T(8,128)(2,1)S(1)}, bf16[65,8,128]{2,1,0:T(8,128)(2,1)S(1)}, u32[]{:S(2)}, u32[]{:S(2)}) collective-permute-start(bf16[65,8,128]{2,1,0:T(8,128)(2,1)S(1)} %get-tuple-element.40), channel_id=1, source_target_pairs={{0,1},{1,0},{2,3},{3,2},{4,5},{5,4},{6,7},{7,6},{8,9},{9,8},{10,11... | collective-permute-start | bytes 399368 | tf_op jit(solution)/shard_map/ppermute | solution.py:321
  4.9 5.7 %collective-permute-start.5 = (bf16[65,8,128]{2,1,0:T(8,128)(2,1)S(1)}, bf16[65,8,128]{2,1,0:T(8,128)(2,1)S(1)}, u32[]{:S(2)}, u32[]{:S(2)}) collective-permute-start(bf16[65,8,128]{2,1,0:T(8,128)(2,1)S(1)} %get-tuple-element.42), channel_id=1, source_target_pairs={{0,1},{1,0},{2,3},{3,2},{4,5},{5,4},{6,7},{7,6},{8,9},{9,8},{10,11... | collective-permute-start | bytes 399368 | tf_op jit(solution)/shard_map/ppermute | solution.py:321
  5.8 7.0 %collective-permute-start.2 = (bf16[65,8,128]{2,1,0:T(8,128)(2,1)S(1)}, bf16[65,8,128]{2,1,0:T(8,128)(2,1)S(1)}, u32[]{:S(2)}, u32[]{:S(2)}) collective-permute-start(bf16[65,8,128]{2,1,0:T(8,128)(2,1)S(1)} %shard_map.78), channel_id=1, source_target_pairs={{0,2},{2,4},{4,6},{6,0},{1,3},{3,5},{5,7},{7,1},{8,10},{10,12},{12... | collective-permute-start | bytes 399368 | tf_op jit(solution)/shard_map/ppermute | solution.py:289
  7.6 9.2 %collective-permute-start.4 = (bf16[65,8,128]{2,1,0:T(8,128)(2,1)S(1)}, bf16[65,8,128]{2,1,0:T(8,128)(2,1)S(1)}, u32[]{:S(2)}, u32[]{:S(2)}) collective-permute-start(bf16[65,8,128]{2,1,0:T(8,128)(2,1)S(1)} %shard_map.79), channel_id=1, source_target_pairs={{0,4},{2,6},{4,0},{6,2},{1,5},{3,7},{5,1},{7,3},{8,12},{10,14},{12... | collective-permute-start | bytes 399368 | tf_op jit(solution)/shard_map/ppermute | solution.py:289
  10.8 6.0 %collective-permute-start.6 = (bf16[65,8,128]{2,1,0:T(8,128)(2,1)S(1)}, bf16[65,8,128]{2,1,0:T(8,128)(2,1)S(1)}, u32[]{:S(2)}, u32[]{:S(2)}) collective-permute-start(bf16[65,8,128]{2,1,0:T(8,128)(2,1)S(1)} %shard_map.80), channel_id=1, source_target_pairs={{0,6},{2,0},{4,2},{6,4},{1,7},{3,1},{5,3},{7,5},{8,14},{10,8},{12,... | collective-permute-start | bytes 399368 | tf_op jit(solution)/shard_map/ppermute | solution.py:289
  12.2 28.8 %copy-start = (bf16[2,1024,1024]{2,1,0:T(8,128)(2,1)S(1)}, bf16[2,1024,1024]{2,1,0:T(8,128)(2,1)}, u32[]{:S(2)}) copy-start(bf16[2,1024,1024]{2,1,0:T(8,128)(2,1)} %win_ref.1) | copy-start | bytes 12582916
  12.2 28.8 %copy-start.1 = (bf16[2,1024,1024]{2,1,0:T(8,128)(2,1)S(1)}, bf16[2,1024,1024]{2,1,0:T(8,128)(2,1)}, u32[]{:S(2)}) copy-start(bf16[2,1024,1024]{2,1,0:T(8,128)(2,1)} %wout_ref.1) | copy-start | bytes 12582916
  34.8 38.9 %copy-start.2 = (bf16[1,512,1024]{2,1,0:T(8,128)(2,1)S(1)}, bf16[1,512,1024]{2,1,0:T(8,128)(2,1)}, u32[]{:S(2)}) copy-start(bf16[1,512,1024]{2,1,0:T(8,128)(2,1)} %param.5) | copy-start | bytes 3145732
  34.8 38.9 %copy-start.3 = (bf16[1,512,1024]{2,1,0:T(8,128)(2,1)S(1)}, bf16[1,512,1024]{2,1,0:T(8,128)(2,1)}, u32[]{:S(2)}) copy-start(bf16[1,512,1024]{2,1,0:T(8,128)(2,1)} %param.9) | copy-start | bytes 3145732
  34.8 5.0 %collective-permute-start.9 = (bf16[8,1024]{1,0:T(8,128)(2,1)S(1)}, bf16[8,1024]{1,0:T(8,128)(2,1)S(1)}, u32[]{:S(2)}, u32[]{:S(2)}) collective-permute-start(bf16[8,1024]{1,0:T(8,128)(2,1)S(1)} %get-tuple-element.43.own_ref), channel_id=1, source_target_pairs={{0,192},{64,0},{128,64},{192,128},{1,193},{65,1},{129,65},{193,129... | collective-permute-start | bytes 49160 | tf_op jit(solution)/shard_map/ppermute | solution.py:289
  35.7 5.2 %collective-permute-start.8 = (bf16[8,1024]{1,0:T(8,128)(2,1)S(1)}, bf16[8,1024]{1,0:T(8,128)(2,1)S(1)}, u32[]{:S(2)}, u32[]{:S(2)}) collective-permute-start(bf16[8,1024]{1,0:T(8,128)(2,1)S(1)} %get-tuple-element.43.own_ref), channel_id=1, source_target_pairs={{0,128},{64,192},{128,0},{192,64},{1,129},{65,193},{129,1},{193,65... | collective-permute-start | bytes 49160 | tf_op jit(solution)/shard_map/ppermute | solution.py:289
  36.8 4.1 %collective-permute-start.7 = (bf16[8,1024]{1,0:T(8,128)(2,1)S(1)}, bf16[8,1024]{1,0:T(8,128)(2,1)S(1)}, u32[]{:S(2)}, u32[]{:S(2)}) collective-permute-start(bf16[8,1024]{1,0:T(8,128)(2,1)S(1)} %get-tuple-element.43.own_ref), channel_id=1, source_target_pairs={{0,64},{64,128},{128,192},{192,0},{1,65},{65,129},{129,193},{193,1... | collective-permute-start | bytes 49160 | tf_op jit(solution)/shard_map/ppermute | solution.py:289
  44.4 35.4 %copy-start.4 = (bf16[1024,256]{1,0:T(8,128)(2,1)S(1)}, bf16[1024,256]{1,0:T(8,128)(2,1)}, u32[]{:S(2)}) copy-start(bf16[1024,256]{1,0:T(8,128)(2,1)} %par_ref.1) | copy-start | bytes 1572868
  44.4 5.0 %collective-permute-start.10 = (bf16[8,1024]{1,0:T(8,128)(2,1)S(1)}, bf16[8,1024]{1,0:T(8,128)(2,1)S(1)}, u32[]{:S(2)}, u32[]{:S(2)}) collective-permute-start(bf16[8,1024]{1,0:T(8,128)(2,1)S(1)} %get-tuple-element.45), channel_id=1, source_target_pairs={{0,192},{64,0},{128,64},{192,128},{1,193},{65,1},{129,65},{193,129... | collective-permute-start | bytes 49160 | tf_op jit(solution)/shard_map/ppermute | solution.py:289
  46.2 5.2 %collective-permute-start.11 = (bf16[8,1024]{1,0:T(8,128)(2,1)S(1)}, bf16[8,1024]{1,0:T(8,128)(2,1)S(1)}, u32[]{:S(2)}, u32[]{:S(2)}) collective-permute-start(bf16[8,1024]{1,0:T(8,128)(2,1)S(1)} %get-tuple-element.46), channel_id=1, source_target_pairs={{0,128},{64,192},{128,0},{192,64},{1,129},{65,193},{129,1},{193,65... | collective-permute-start | bytes 49160 | tf_op jit(solution)/shard_map/ppermute | solution.py:289
  48.8 3.7 %collective-permute-start.12 = (bf16[8,1024]{1,0:T(8,128)(2,1)S(1)}, bf16[8,1024]{1,0:T(8,128)(2,1)S(1)}, u32[]{:S(2)}, u32[]{:S(2)}) collective-permute-start(bf16[8,1024]{1,0:T(8,128)(2,1)S(1)} %get-tuple-element.47), channel_id=1, source_target_pairs={{0,64},{64,128},{128,192},{192,0},{1,65},{65,129},{129,193},{193,1... | collective-permute-start | bytes 49160 | tf_op jit(solution)/shard_map/ppermute | solution.py:289
  71.6 2.0 %collective-permute-start.13 = (bf16[32,8,1152]{2,1,0:T(8,128)(2,1)S(1)}, bf16[32,8,1152]{2,1,0:T(8,128)(2,1)S(1)}, u32[]{:S(2)}, u32[]{:S(2)}) collective-permute-start(bf16[32,8,1152]{2,1,0:T(8,128)(2,1)S(1)} %all_to_all.16.own_ref), channel_id=1, source_target_pairs={{0,1},{1,0},{2,3},{3,2},{4,5},{5,4},{6,7},{7,6},{8,9},{9,8},{10,11... | collective-permute-start | bytes 1769480 | tf_op jit(solution)/shard_map/ppermute | solution.py:344
  75.1 1.3 %collective-permute-start.15 = (bf16[32,8,128]{2,1,0:T(8,128)(2,1)S(1)}, bf16[32,8,128]{2,1,0:T(8,128)(2,1)S(1)}, u32[]{:S(2)}, u32[]{:S(2)}) collective-permute-start(bf16[32,8,128]{2,1,0:T(8,128)(2,1)S(1)} %get-tuple-element.60), channel_id=1, source_target_pairs={{0,1},{1,0},{2,3},{3,2},{4,5},{5,4},{6,7},{7,6},{8,9},{9,8},{10,11... | collective-permute-start | bytes 196616 | tf_op jit(solution)/shard_map/ppermute | solution.py:356
  75.4 2.8 %collective-permute-start.17 = (bf16[32,8,128]{2,1,0:T(8,128)(2,1)S(1)}, bf16[32,8,128]{2,1,0:T(8,128)(2,1)S(1)}, u32[]{:S(2)}, u32[]{:S(2)}) collective-permute-start(bf16[32,8,128]{2,1,0:T(8,128)(2,1)S(1)} %get-tuple-element.62), channel_id=1, source_target_pairs={{0,1},{1,0},{2,3},{3,2},{4,5},{5,4},{6,7},{7,6},{8,9},{9,8},{10,11... | collective-permute-start | bytes 196616 | tf_op jit(solution)/shard_map/ppermute | solution.py:356
  75.7 2.8 %collective-permute-start.19 = (bf16[32,8,128]{2,1,0:T(8,128)(2,1)S(1)}, bf16[32,8,128]{2,1,0:T(8,128)(2,1)S(1)}, u32[]{:S(2)}, u32[]{:S(2)}) collective-permute-start(bf16[32,8,128]{2,1,0:T(8,128)(2,1)S(1)} %get-tuple-element.64), channel_id=1, source_target_pairs={{0,1},{1,0},{2,3},{3,2},{4,5},{5,4},{6,7},{7,6},{8,9},{9,8},{10,11... | collective-permute-start | bytes 196616 | tf_op jit(solution)/shard_map/ppermute | solution.py:356
  75.9 6.1 %collective-permute-start.14 = (bf16[32,8,128]{2,1,0:T(8,128)(2,1)S(1)}, bf16[32,8,128]{2,1,0:T(8,128)(2,1)S(1)}, u32[]{:S(2)}, u32[]{:S(2)}) collective-permute-start(bf16[32,8,128]{2,1,0:T(8,128)(2,1)S(1)} %get-tuple-element.58), channel_id=1, source_target_pairs={{0,1},{1,0},{2,3},{3,2},{4,5},{5,4},{6,7},{7,6},{8,9},{9,8},{10,11... | collective-permute-start | bytes 196616 | tf_op jit(solution)/shard_map/ppermute | solution.py:356
  76.5 5.4 %collective-permute-start.16 = (bf16[32,8,128]{2,1,0:T(8,128)(2,1)S(1)}, bf16[32,8,128]{2,1,0:T(8,128)(2,1)S(1)}, u32[]{:S(2)}, u32[]{:S(2)}) collective-permute-start(bf16[32,8,128]{2,1,0:T(8,128)(2,1)S(1)} %shard_map.88), channel_id=1, source_target_pairs={{0,64},{64,128},{128,192},{192,0},{1,65},{65,129},{129,193},{193,1... | collective-permute-start | bytes 196616 | tf_op jit(solution)/shard_map/ppermute | solution.py:289
  78.2 6.4 %collective-permute-start.18 = (bf16[32,8,128]{2,1,0:T(8,128)(2,1)S(1)}, bf16[32,8,128]{2,1,0:T(8,128)(2,1)S(1)}, u32[]{:S(2)}, u32[]{:S(2)}) collective-permute-start(bf16[32,8,128]{2,1,0:T(8,128)(2,1)S(1)} %shard_map.89), channel_id=1, source_target_pairs={{0,128},{64,192},{128,0},{192,64},{1,129},{65,193},{129,1},{193,65... | collective-permute-start | bytes 196616 | tf_op jit(solution)/shard_map/ppermute | solution.py:289
  78.6 6.5 %collective-permute-start.20 = (bf16[32,8,128]{2,1,0:T(8,128)(2,1)S(1)}, bf16[32,8,128]{2,1,0:T(8,128)(2,1)S(1)}, u32[]{:S(2)}, u32[]{:S(2)}) collective-permute-start(bf16[32,8,128]{2,1,0:T(8,128)(2,1)S(1)} %shard_map.90), channel_id=1, source_target_pairs={{0,192},{64,0},{128,64},{192,128},{1,193},{65,1},{129,65},{193,129... | collective-permute-start | bytes 196616 | tf_op jit(solution)/shard_map/ppermute | solution.py:289

commit v6 on v5

--- a/solution.py
+++ b/solution.py
@@ -152,7 +152,8 @@
     out_ref[len(bodies) * size] = jnp.where(lane < 8, top, mark).astype(BF)
 
 
-def merge_columns(a_ref, b_ref, c_ref, d_ref, out_ref):
+def merge_columns(a_ref, b_ref, c_ref, d_ref, after_ref, out_ref):
+    del after_ref
     bodies, top, high, low = merge_tiles([a_ref, b_ref, c_ref, d_ref])
     size = bodies[0].shape[0]
     lane = iota(top.shape, 1)
@@ -188,7 +189,14 @@
     return u * cdf, cdf + u * pdf
 
 
-def experts(own_ref, a_ref, b_ref, c_ref, win_ref, wout_ref, *out_refs):
+def turn_weights(win_ref, wout_ref, after_ref, win_t_ref, wout_t_ref):
+    del after_ref
+    for e in range(win_ref.shape[0]):
+        win_t_ref[e] = win_ref[e].T
+        wout_t_ref[e] = wout_ref[e].T
+
+
+def experts(own_ref, a_ref, b_ref, c_ref, win_ref, wout_ref, win_t_ref, wout_t_ref, *out_refs):
     blocks = [r[...].astype(F32) for r in (own_ref, a_ref, b_ref, c_ref)]
     fwd = jnp.concatenate([x[:4] for x in blocks], axis=0).astype(BF)
     bwd = jnp.concatenate([x[4:] for x in blocks], axis=0).astype(BF)
@@ -199,8 +207,8 @@
         w1, w2 = win_ref[e], wout_ref[e]
         gelu, slope = gelu_parts(dot(fwd, w1))
         out += dot(jnp.where(mine, gelu, 0.0).astype(BF), w2)
-        dact = dot(bwd, w2, ((1,), (1,)))
-        back += dot(jnp.where(mine, dact * slope, 0.0).astype(BF), w1, ((1,), (1,)))
+        dact = dot(bwd, wout_t_ref[e])
+        back += dot(jnp.where(mine, dact * slope, 0.0).astype(BF), win_t_ref[e])
     for v, ref in enumerate(out_refs):
         ref[...] = jnp.concatenate([out[4 * v:4 * v + 4], back[4 * v:4 * v + 4]], axis=0).astype(BF)
 
@@ -322,11 +330,24 @@
     shares = {}
     for k in order:
         (share,) = call(merge_cores, [shape(tiles, BF)], blocks[k], others[k], flops=10 * unit)
+        if k:
+            last = share
         shares[k] = shifted(share, k, rows_y, "y") if k else share
-    (merged,) = call(
-        merge_columns, [shape((depth, width // STAT + 1, 8, STAT), BF)],
-        *[shares[k] for k in range(rows_y)],
-    )
+    win_t, wout_t = pl.pallas_call(
+        turn_weights,
+        out_shape=[shape(w_in.shape, BF), shape(w_out.shape, BF)],
+        in_specs=[vmem, vmem, pl.BlockSpec(memory_space=pl.ANY)],
+        out_specs=[vmem, vmem],
+        compiler_params=PARAMS,
+        cost_estimate=pl.CostEstimate(flops=20 * unit, bytes_accessed=8 * w_in.size, transcendentals=0),
+    )(w_in, w_out, last)
+    merged = pl.pallas_call(
+        merge_columns,
+        out_shape=shape((depth, width // STAT + 1, 8, STAT), BF),
+        in_specs=[vmem] * rows_y + [pl.BlockSpec(memory_space=pl.ANY)],
+        out_specs=vmem,
+        compiler_params=PARAMS,
+    )(*[shares[k] for k in range(rows_y)], wout_t)
     shards = lax.all_to_all(merged, "z", 0, 0, tiled=True)
     pay, full, side = call(
         merge_shards,
@@ -335,7 +356,7 @@
     )
     behind = [shifted(pay, k, videos) for k in range(1, videos)]
     partial = call(
-        experts, [shape((8, width), BF)] * videos, pay, *behind, w_in, w_out,
+        experts, [shape((8, width), BF)] * videos, pay, *behind, w_in, w_out, win_t, wout_t,
         flops=32 * videos * w_in.size,
     )
     parts = [shifted(partial[k], -k, videos) for k in range(1, videos)]

time: 100 us -> 98.9 us (0.989)
  waiting for transfers between devices: 15.6 us -> 11.2 us
  local copies, waits for them, and re-layouts: 0.02 us -> 1.92 us
  Pallas kernels: 12.6 us -> 14 us
    ppermute x12, waiting for transfers between devices: 13 us -> 8.58 us  [shifted(): lax.ppermute(value, axis, [(i, (i + step) % size) for i in range(size)])]
    pallas_call x0 -> x2, Pallas kernels: none -> 2.59 us  [the longest x1 2.4 us: on_device(): pl.pallas_call(turn_weights, out_shape=[shape(w_in.shape, BF), shape(w_ou...]
    unnamed x10, local copies, waits for them, and re-layouts: 0.02 us -> 1.92 us
    pallas_call x15 -> x14, Pallas kernels: 8.99 us -> 7.74 us  [call(): pl.pallas_call(body, out_shape=outs, in_specs=[pl.BlockSpec(memory_space=...]
  transfers between devices with their start and end apart: 21 -> 21, of which waited for: 12 -> 11; matrix products, arithmetic and copies ran while one was open for 0% -> 0% of each run, Pallas kernels for 3% -> 5%
where the time goes in v6:
time: 98.9 us; the launch traced here: 98.7 us
  blocking collectives  50.5 us (51%)
  starting transfers between devices  20.4 us (21%)
  Pallas kernels  14 us (14%)
  waiting for transfers between devices  11.2 us (11%)
  local copies, waits for them, and re-layouts  1.92 us (2%)
    all_to_all x1, blocking collectives, on_device(): mine = lax.all_to_all(block, ZY, 0, 0, tiled=True)  18.8 us
    ppermute x12, starting transfers between devices, shifted(): lax.ppermute(value, axis, [(i, (i + step) % size) for i in range(size)])  18.1 us
    all_to_all x1, blocking collectives, on_device(): shards = lax.all_to_all(merged, 'z', 0, 0, tiled=True)  17.5 us
    all_to_all x1, blocking collectives, on_device(): pieces = lax.all_to_all(half, ZY, 0, 0, tiled=True)  14.2 us
    ppermute x12, waiting for transfers between devices, shifted(): lax.ppermute(value, axis, [(i, (i + step) % size) for i in range(size)])  8.58 us
    pallas_call x14, Pallas kernels, call(): pl.pallas_call(body, out_shape=outs, in_specs=[pl.BlockSpec(memory_space=...  7.74 us
    pallas_call x1, Pallas kernels, on_device(): pl.pallas_call(reduce_tokens, out_shape=[shape(tiles, BF)] * (2 * rows_y)...  3.6 us
    pallas_call x1, Pallas kernels, on_device(): pl.pallas_call(turn_weights, out_shape=[shape(w_in.shape, BF), shape(w_ou...  2.4 us
  transfers between devices with their start and end apart: 21, of which 11 were waited for; matrix products, arithmetic and copies ran while one was open for 0% of the time, Pallas kernels for 5%

profile of v6, /device:TPU:6, one launch (start us, length us, event | category | flops | bytes accessed | tf_op | source)
XLA Modules:
  0.0 98.7 jit_solution(2887968045307876645)
XLA Ops:
  0.6 3.6 %shard_map.76 = (bf16[65,8,128]{2,1,0:T(8,128)(2,1)S(1)}, bf16[65,8,128]{2,1,0:T(8,128)(2,1)S(1)}, bf16[65,8,128]{2,1,0:T(8,128)(2,1)S(1)}, bf16[65,8,128]{2,1,0...) custom-call(bf16[512,1024]{1,0:T(8,128)(2,1)} %bitcast.4, ...), custom_call_target="tpu_custom_call" | custom-call | flops 1073741824 | bytes 4194304 | tf_op jit(solution)/shard_map/pallas_call | solution.py:314
  4.2 0.1 collective-permute-start.1
  4.3 0.5 collective-permute-start
  4.8 0.1 collective-permute-start.3
  4.9 0.4 collective-permute-start.5
  5.3 0.3 collective-permute-done.1.b_ref
  5.7 0.1 shard_map.78
  5.8 1.7 %collective-permute-start.2 = (bf16[65,8,128]{2,1,0:T(8,128)(2,1)S(1)}, bf16[65,8,128]{2,1,0:T(8,128)(2,1)S(1)}, u32[]{:S(2)}, u32[]{:S(2)}) collective-permute-start(bf16[65,8,128]{2,1,0:T(8,128)(2,1)S(1)} %shard_map.78), channel_id=1, source_target_pairs={{0,2},{2,4},{4,6},{6,0},{1,3},{3,5},{5,7},{7,1},{8,10},{10,12},{12... | collective-permute-start | bytes 399368 | tf_op jit(solution)/shard_map/ppermute | solution.py:297
  7.5 0.0 collective-permute-done.3.b_ref
  7.5 0.1 shard_map.79
  7.6 3.0 %collective-permute-start.4 = (bf16[65,8,128]{2,1,0:T(8,128)(2,1)S(1)}, bf16[65,8,128]{2,1,0:T(8,128)(2,1)S(1)}, u32[]{:S(2)}, u32[]{:S(2)}) collective-permute-start(bf16[65,8,128]{2,1,0:T(8,128)(2,1)S(1)} %shard_map.79), channel_id=1, source_target_pairs={{0,4},{2,6},{4,0},{6,2},{1,5},{3,7},{5,1},{7,3},{8,12},{10,14},{12... | collective-permute-start | bytes 399368 | tf_op jit(solution)/shard_map/ppermute | solution.py:297
  10.6 0.0 collective-permute-done.5.b_ref
  10.6 0.0 copy-start
  10.6 0.1 shard_map.80.after_ref
  10.8 1.4 %collective-permute-start.6 = (bf16[65,8,128]{2,1,0:T(8,128)(2,1)S(1)}, bf16[65,8,128]{2,1,0:T(8,128)(2,1)S(1)}, u32[]{:S(2)}, u32[]{:S(2)}) collective-permute-start(bf16[65,8,128]{2,1,0:T(8,128)(2,1)S(1)} %shard_map.80.after_ref), channel_id=1, source_target_pairs={{0,6},{2,0},{4,2},{6,4},{1,7},{3,1},{5,3},{7,5},{8,14},{10,8},{12,... | collective-permute-start | bytes 399368 | tf_op jit(solution)/shard_map/ppermute | solution.py:297
  12.2 0.6 copy-done
  12.8 1.3 %copy-done.1 = bf16[2,1024,1024]{2,1,0:T(8,128)(2,1)S(1)} copy-done((bf16[2,1024,1024]{2,1,0:T(8,128)(2,1)S(1)}, bf16[2,1024,1024]{2,1,0:T(8,128)(2,1)}, u32[]{:S(2)}) %copy-start.1) | copy-done | bytes 4194328
  14.1 2.4 %shard_map.81 = (bf16[2,1024,1024]{2,1,0:T(8,128)(2,1)S(1)}, bf16[2,1024,1024]{2,1,0:T(8,128)(2,1)S(1)}) custom-call(bf16[2,1024,1024]{2,1,0:T(8,128)(2,1)S(1)} %copy-done, bf16[2,1024,1024]{2,1,0:T(8,128)(2,1)S(1)} %copy-done.1, bf16[65,8,128]{2,1,0:T(8,128)(2,1)S(1)} %shard_map.80.after_ref), custom_call_target="tpu_custom_call" | custom-call | flops 5368709120 | bytes 16777216 | tf_op jit(solution)/shard_map/pallas_call | solution.py:336
  16.5 0.0 collective-permute-done.b_ref
  16.5 0.1 shard_map.77.a_ref
  16.7 0.0 collective-permute-done.2.b_ref
  16.7 0.2 collective-permute-done.4.c_ref
  16.8 0.0 collective-permute-done.6.d_ref
  16.8 0.2 shard_map.82
  17.0 17.5 %all_to_all.15.in_ref = bf16[8,9,8,128]{3,2,1,0:T(8,128)(2,1)S(1)} all-to-all(bf16[8,9,8,128]{3,2,1,0:T(8,128)(2,1)S(1)} %shard_map.82), channel_id=1, replica_groups=mesh['x'=4,'z'=8,'y'=4,'c'=2] {'z'}, dimensions={0} | all-to-all | bytes 294912 | tf_op jit(solution)/shard_map/all_to_all | solution.py:351
  34.5 0.2 shard_map.83
  34.8 0.9 collective-permute-start.9
  35.7 1.1 %collective-permute-start.8 = (bf16[8,1024]{1,0:T(8,128)(2,1)S(1)}, bf16[8,1024]{1,0:T(8,128)(2,1)S(1)}, u32[]{:S(2)}, u32[]{:S(2)}) collective-permute-start(bf16[8,1024]{1,0:T(8,128)(2,1)S(1)} %get-tuple-element.46.own_ref), channel_id=1, source_target_pairs={{0,128},{64,192},{128,0},{192,64},{1,129},{65,193},{129,1},{193,65... | collective-permute-start | bytes 49160 | tf_op jit(solution)/shard_map/ppermute | solution.py:297
  36.8 2.1 %collective-permute-start.7 = (bf16[8,1024]{1,0:T(8,128)(2,1)S(1)}, bf16[8,1024]{1,0:T(8,128)(2,1)S(1)}, u32[]{:S(2)}, u32[]{:S(2)}) collective-permute-start(bf16[8,1024]{1,0:T(8,128)(2,1)S(1)} %get-tuple-element.46.own_ref), channel_id=1, source_target_pairs={{0,64},{64,128},{128,192},{192,0},{1,65},{65,129},{129,193},{193,1... | collective-permute-start | bytes 49160 | tf_op jit(solution)/shard_map/ppermute | solution.py:297
  38.9 0.9 collective-permute-done.9.c_ref
  39.8 1.1 %collective-permute-done.8.b_ref = bf16[8,1024]{1,0:T(8,128)(2,1)S(1)} collective-permute-done((bf16[8,1024]{1,0:T(8,128)(2,1)S(1)}, bf16[8,1024]{1,0:T(8,128)(2,1)S(1)}, u32[]{:S(2)}, u32[]{:S(2)}) %collective-permute-start.8) | collective-permute-done | bytes 16416 | tf_op jit(solution)/shard_map/ppermute | solution.py:297
  40.9 0.0 collective-permute-done.7.a_ref
  40.9 2.3 %shard_map.84 = (bf16[8,1024]{1,0:T(8,128)(2,1)S(1)}, bf16[8,1024]{1,0:T(8,128)(2,1)S(1)}, bf16[8,1024]{1,0:T(8,128)(2,1)S(1)}, bf16[8,1024]{1,0:T(8,128)(2,1)S(1)}) custom-call(bf16[8,1024]{1,0:T(8,128)(2,1)S(1)} %get-tuple-element.46.own_ref, bf16[8,1024]{1,0:T(8,128)(2,1)S(1)} %collective-permute-done.7.a_ref, ...), custom_call_target="tpu_custom_call" | custom-call | flops 268435456 | bytes 16973824 | tf_op jit(solution)/shard_map/pallas_call | solution.py:30
  43.3 1.8 %collective-permute-start.10 = (bf16[8,1024]{1,0:T(8,128)(2,1)S(1)}, bf16[8,1024]{1,0:T(8,128)(2,1)S(1)}, u32[]{:S(2)}, u32[]{:S(2)}) collective-permute-start(bf16[8,1024]{1,0:T(8,128)(2,1)S(1)} %get-tuple-element.49), channel_id=1, source_target_pairs={{0,192},{64,0},{128,64},{192,128},{1,193},{65,1},{129,65},{193,129... | collective-permute-start | bytes 49160 | tf_op jit(solution)/shard_map/ppermute | solution.py:297
  45.1 2.6 %collective-permute-start.11 = (bf16[8,1024]{1,0:T(8,128)(2,1)S(1)}, bf16[8,1024]{1,0:T(8,128)(2,1)S(1)}, u32[]{:S(2)}, u32[]{:S(2)}) collective-permute-start(bf16[8,1024]{1,0:T(8,128)(2,1)S(1)} %get-tuple-element.50), channel_id=1, source_target_pairs={{0,128},{64,192},{128,0},{192,64},{1,129},{65,193},{129,1},{193,65... | collective-permute-start | bytes 49160 | tf_op jit(solution)/shard_map/ppermute | solution.py:297
  47.7 0.3 collective-permute-start.12
  48.0 0.3 collective-permute-done.10.a_ref
  48.3 2.0 %collective-permute-done.11.b_ref = bf16[8,1024]{1,0:T(8,128)(2,1)S(1)} collective-permute-done((bf16[8,1024]{1,0:T(8,128)(2,1)S(1)}, bf16[8,1024]{1,0:T(8,128)(2,1)S(1)}, u32[]{:S(2)}, u32[]{:S(2)}) %collective-permute-start.11) | collective-permute-done | bytes 16416 | tf_op jit(solution)/shard_map/ppermute | solution.py:297
  50.3 1.1 %collective-permute-done.12.c_ref = bf16[8,1024]{1,0:T(8,128)(2,1)S(1)} collective-permute-done((bf16[8,1024]{1,0:T(8,128)(2,1)S(1)}, bf16[8,1024]{1,0:T(8,128)(2,1)S(1)}, u32[]{:S(2)}, u32[]{:S(2)}) %collective-permute-start.12) | collective-permute-done | bytes 16416 | tf_op jit(solution)/shard_map/ppermute | solution.py:297
  51.4 0.3 shard_map.85
  51.7 18.8 %all_to_all.16.own_ref = bf16[32,8,1152]{2,1,0:T(8,128)(2,1)S(1)} all-to-all(bf16[32,8,1152]{2,1,0:T(8,128)(2,1)S(1)} %shard_map.85), channel_id=1, replica_groups=mesh['x'=4,'z'=8,'y'=4,'c'=2] {'z','y'}, dimensions={0} | all-to-all | bytes 1179648 | tf_op jit(solution)/shard_map/all_to_all | solution.py:364
  70.6 0.0 collective-permute-start.13
  70.6 2.0 %collective-permute-done.13.oth_ref = bf16[32,8,1152]{2,1,0:T(8,128)(2,1)S(1)} collective-permute-done((bf16[32,8,1152]{2,1,0:T(8,128)(2,1)S(1)}, bf16[32,8,1152]{2,1,0:T(8,128)(2,1)S(1)}, u32[]{:S(2)}, u32[]{:S(2)}) %collective-permute-start.13) | collective-permute-done | bytes 589856 | tf_op jit(solution)/shard_map/ppermute | solution.py:365
  72.6 0.0 copy-done.2
  72.6 0.0 copy-done.3
  72.6 1.5 %shard_map.86 = (bf16[32,8,128]{2,1,0:T(8,128)(2,1)S(1)}, bf16[32,8,128]{2,1,0:T(8,128)(2,1)S(1)}, bf16[32,8,128]{2,1,0:T(8,128)(2,1)S(1)}, bf16[32,8,128]{2,1,0...) custom-call(f32[512,256]{1,0:T(8,128)S(1)} %get-tuple-element.36.log, ...), custom_call_target="tpu_custom_call" | custom-call | flops 1342177280 | bytes 8519680 | tf_op jit(solution)/shard_map/pallas_call | solution.py:30
  74.1 0.2 collective-permute-start.15
  74.3 0.4 collective-permute-start.17
  74.7 0.1 collective-permute-start.19
  74.8 0.4 collective-permute-start.14
  75.2 0.2 collective-permute-done.15.b_ref
  75.4 1.5 %collective-permute-start.16 = (bf16[32,8,128]{2,1,0:T(8,128)(2,1)S(1)}, bf16[32,8,128]{2,1,0:T(8,128)(2,1)S(1)}, u32[]{:S(2)}, u32[]{:S(2)}) collective-permute-start(bf16[32,8,128]{2,1,0:T(8,128)(2,1)S(1)} %shard_map.89), channel_id=1, source_target_pairs={{0,64},{64,128},{128,192},{192,0},{1,65},{65,129},{129,193},{193,1... | collective-permute-start | bytes 196616 | tf_op jit(solution)/shard_map/ppermute | solution.py:297
  77.0 0.0 collective-permute-done.17.b_ref
  77.0 0.4 collective-permute-start.18
  77.4 0.0 collective-permute-done.19.b_ref
  77.5 1.3 %collective-permute-start.20 = (bf16[32,8,128]{2,1,0:T(8,128)(2,1)S(1)}, bf16[32,8,128]{2,1,0:T(8,128)(2,1)S(1)}, u32[]{:S(2)}, u32[]{:S(2)}) collective-permute-start(bf16[32,8,128]{2,1,0:T(8,128)(2,1)S(1)} %shard_map.91), channel_id=1, source_target_pairs={{0,192},{64,0},{128,64},{192,128},{1,193},{65,1},{129,65},{193,129... | collective-permute-start | bytes 196616 | tf_op jit(solution)/shard_map/ppermute | solution.py:297
  78.7 0.0 copy-done.4
  78.7 2.2 %shard_map.87 = (bf16[512,1024]{1,0:T(8,128)(2,1)}, bf16[512,1024]{1,0:T(8,128)(2,1)}) custom-call(bf16[512,256]{1,0:T(8,128)(2,1)S(1)} %get-tuple-element.54.comb_ref, bf16[256,1024]{1,0:T(8,128)(2,1)S(1)} %get-tuple-element.55.so_ref, bf16[512,256]{1,0:T(8,128)(2,1)S(1)} %get-tuple-element.56.dlog_ref, bf16[1024,256]{1,0:T(8,128)(2,1)S(1)} %copy-done.4, ...), custom_call_target="tpu_custom_call" | custom-call | flops 805306368 | bytes 6553600 | tf_op jit(solution)/shard_map/pallas_call | solution.py:30
  80.9 0.0 collective-permute-done.14.b_ref
  80.9 0.0 collective-permute-done.16.a_ref
  80.9 2.5 %collective-permute-done.18.b_ref = bf16[32,8,128]{2,1,0:T(8,128)(2,1)S(1)} collective-permute-done((bf16[32,8,128]{2,1,0:T(8,128)(2,1)S(1)}, bf16[32,8,128]{2,1,0:T(8,128)(2,1)S(1)}, u32[]{:S(2)}, u32[]{:S(2)}) %collective-permute-start.18) | collective-permute-done | bytes 65568 | tf_op jit(solution)/shard_map/ppermute | solution.py:297
  83.5 0.4 collective-permute-done.20.c_ref
  83.9 14.2 %all_to_all.17.in_ref = bf16[32,8,128]{2,1,0:T(8,128)(2,1)S(1)} all-to-all(bf16[32,8,128]{2,1,0:T(8,128)(2,1)S(1)} %shard_map.92), channel_id=1, replica_groups=mesh['x'=4,'z'=8,'y'=4,'c'=2] {'z','y'}, dimensions={0} | all-to-all | bytes 131072 | tf_op jit(solution)/shard_map/all_to_all | solution.py:394
  98.1 0.6 shard_map.93
  (9 shorter events, 0.1 us)
Async XLA Ops:
  4.2 1.4 %collective-permute-start.1 = (bf16[65,8,128]{2,1,0:T(8,128)(2,1)S(1)}, bf16[65,8,128]{2,1,0:T(8,128)(2,1)S(1)}, u32[]{:S(2)}, u32[]{:S(2)}) collective-permute-start(bf16[65,8,128]{2,1,0:T(8,128)(2,1)S(1)} %get-tuple-element.40), channel_id=1, source_target_pairs={{0,1},{1,0},{2,3},{3,2},{4,5},{5,4},{6,7},{7,6},{8,9},{9,8},{10,11... | collective-permute-start | bytes 399368 | tf_op jit(solution)/shard_map/ppermute | solution.py:329
  4.3 12.2 %collective-permute-start = (bf16[65,8,128]{2,1,0:T(8,128)(2,1)S(1)}, bf16[65,8,128]{2,1,0:T(8,128)(2,1)S(1)}, u32[]{:S(2)}, u32[]{:S(2)}) collective-permute-start(bf16[65,8,128]{2,1,0:T(8,128)(2,1)S(1)} %get-tuple-element.38), channel_id=1, source_target_pairs={{0,1},{1,0},{2,3},{3,2},{4,5},{5,4},{6,7},{7,6},{8,9},{9,8},{10,11... | collective-permute-start | bytes 399368 | tf_op jit(solution)/shard_map/ppermute | solution.py:329
  4.8 2.6 %collective-permute-start.3 = (bf16[65,8,128]{2,1,0:T(8,128)(2,1)S(1)}, bf16[65,8,128]{2,1,0:T(8,128)(2,1)S(1)}, u32[]{:S(2)}, u32[]{:S(2)}) collective-permute-start(bf16[65,8,128]{2,1,0:T(8,128)(2,1)S(1)} %get-tuple-element.42), channel_id=1, source_target_pairs={{0,1},{1,0},{2,3},{3,2},{4,5},{5,4},{6,7},{7,6},{8,9},{9,8},{10,11... | collective-permute-start | bytes 399368 | tf_op jit(solution)/shard_map/ppermute | solution.py:329
  4.9 5.7 %collective-permute-start.5 = (bf16[65,8,128]{2,1,0:T(8,128)(2,1)S(1)}, bf16[65,8,128]{2,1,0:T(8,128)(2,1)S(1)}, u32[]{:S(2)}, u32[]{:S(2)}) collective-permute-start(bf16[65,8,128]{2,1,0:T(8,128)(2,1)S(1)} %get-tuple-element.44), channel_id=1, source_target_pairs={{0,1},{1,0},{2,3},{3,2},{4,5},{5,4},{6,7},{7,6},{8,9},{9,8},{10,11... | collective-permute-start | bytes 399368 | tf_op jit(solution)/shard_map/ppermute | solution.py:329
  5.8 10.8 %collective-permute-start.2 = (bf16[65,8,128]{2,1,0:T(8,128)(2,1)S(1)}, bf16[65,8,128]{2,1,0:T(8,128)(2,1)S(1)}, u32[]{:S(2)}, u32[]{:S(2)}) collective-permute-start(bf16[65,8,128]{2,1,0:T(8,128)(2,1)S(1)} %shard_map.78), channel_id=1, source_target_pairs={{0,2},{2,4},{4,6},{6,0},{1,3},{3,5},{5,7},{7,1},{8,10},{10,12},{12... | collective-permute-start | bytes 399368 | tf_op jit(solution)/shard_map/ppermute | solution.py:297
  7.6 9.2 %collective-permute-start.4 = (bf16[65,8,128]{2,1,0:T(8,128)(2,1)S(1)}, bf16[65,8,128]{2,1,0:T(8,128)(2,1)S(1)}, u32[]{:S(2)}, u32[]{:S(2)}) collective-permute-start(bf16[65,8,128]{2,1,0:T(8,128)(2,1)S(1)} %shard_map.79), channel_id=1, source_target_pairs={{0,4},{2,6},{4,0},{6,2},{1,5},{3,7},{5,1},{7,3},{8,12},{10,14},{12... | collective-permute-start | bytes 399368 | tf_op jit(solution)/shard_map/ppermute | solution.py:297
  10.6 2.2 %copy-start = (bf16[2,1024,1024]{2,1,0:T(8,128)(2,1)S(1)}, bf16[2,1024,1024]{2,1,0:T(8,128)(2,1)}, u32[]{:S(2)}) copy-start(bf16[2,1024,1024]{2,1,0:T(8,128)(2,1)} %win_ref.3) | copy-start | bytes 12582916
  10.6 3.5 %copy-start.1 = (bf16[2,1024,1024]{2,1,0:T(8,128)(2,1)S(1)}, bf16[2,1024,1024]{2,1,0:T(8,128)(2,1)}, u32[]{:S(2)}) copy-start(bf16[2,1024,1024]{2,1,0:T(8,128)(2,1)} %wout_ref.3) | copy-start | bytes 12582916
  10.8 6.0 %collective-permute-start.6 = (bf16[65,8,128]{2,1,0:T(8,128)(2,1)S(1)}, bf16[65,8,128]{2,1,0:T(8,128)(2,1)S(1)}, u32[]{:S(2)}, u32[]{:S(2)}) collective-permute-start(bf16[65,8,128]{2,1,0:T(8,128)(2,1)S(1)} %shard_map.80.after_ref), channel_id=1, source_target_pairs={{0,6},{2,0},{4,2},{6,4},{1,7},{3,1},{5,3},{7,5},{8,14},{10,8},{12,... | collective-permute-start | bytes 399368 | tf_op jit(solution)/shard_map/ppermute | solution.py:297
  34.8 5.0 %collective-permute-start.9 = (bf16[8,1024]{1,0:T(8,128)(2,1)S(1)}, bf16[8,1024]{1,0:T(8,128)(2,1)S(1)}, u32[]{:S(2)}, u32[]{:S(2)}) collective-permute-start(bf16[8,1024]{1,0:T(8,128)(2,1)S(1)} %get-tuple-element.46.own_ref), channel_id=1, source_target_pairs={{0,192},{64,0},{128,64},{192,128},{1,193},{65,1},{129,65},{193,129... | collective-permute-start | bytes 49160 | tf_op jit(solution)/shard_map/ppermute | solution.py:297
  35.7 5.2 %collective-permute-start.8 = (bf16[8,1024]{1,0:T(8,128)(2,1)S(1)}, bf16[8,1024]{1,0:T(8,128)(2,1)S(1)}, u32[]{:S(2)}, u32[]{:S(2)}) collective-permute-start(bf16[8,1024]{1,0:T(8,128)(2,1)S(1)} %get-tuple-element.46.own_ref), channel_id=1, source_target_pairs={{0,128},{64,192},{128,0},{192,64},{1,129},{65,193},{129,1},{193,65... | collective-permute-start | bytes 49160 | tf_op jit(solution)/shard_map/ppermute | solution.py:297
  36.8 4.1 %collective-permute-start.7 = (bf16[8,1024]{1,0:T(8,128)(2,1)S(1)}, bf16[8,1024]{1,0:T(8,128)(2,1)S(1)}, u32[]{:S(2)}, u32[]{:S(2)}) collective-permute-start(bf16[8,1024]{1,0:T(8,128)(2,1)S(1)} %get-tuple-element.46.own_ref), channel_id=1, source_target_pairs={{0,64},{64,128},{128,192},{192,0},{1,65},{65,129},{129,193},{193,1... | collective-permute-start | bytes 49160 | tf_op jit(solution)/shard_map/ppermute | solution.py:297
  40.9 31.6 %copy-start.2 = (bf16[1,512,1024]{2,1,0:T(8,128)(2,1)S(1)}, bf16[1,512,1024]{2,1,0:T(8,128)(2,1)}, u32[]{:S(2)}) copy-start(bf16[1,512,1024]{2,1,0:T(8,128)(2,1)} %param.5) | copy-start | bytes 3145732
  40.9 31.6 %copy-start.3 = (bf16[1,512,1024]{2,1,0:T(8,128)(2,1)S(1)}, bf16[1,512,1024]{2,1,0:T(8,128)(2,1)}, u32[]{:S(2)}) copy-start(bf16[1,512,1024]{2,1,0:T(8,128)(2,1)} %param.9) | copy-start | bytes 3145732
  43.3 35.5 %copy-start.4 = (bf16[1024,256]{1,0:T(8,128)(2,1)S(1)}, bf16[1024,256]{1,0:T(8,128)(2,1)}, u32[]{:S(2)}) copy-start(bf16[1024,256]{1,0:T(8,128)(2,1)} %par_ref.1) | copy-start | bytes 1572868
  43.3 5.0 %collective-permute-start.10 = (bf16[8,1024]{1,0:T(8,128)(2,1)S(1)}, bf16[8,1024]{1,0:T(8,128)(2,1)S(1)}, u32[]{:S(2)}, u32[]{:S(2)}) collective-permute-start(bf16[8,1024]{1,0:T(8,128)(2,1)S(1)} %get-tuple-element.49), channel_id=1, source_target_pairs={{0,192},{64,0},{128,64},{192,128},{1,193},{65,1},{129,65},{193,129... | collective-permute-start | bytes 49160 | tf_op jit(solution)/shard_map/ppermute | solution.py:297
  45.1 5.2 %collective-permute-start.11 = (bf16[8,1024]{1,0:T(8,128)(2,1)S(1)}, bf16[8,1024]{1,0:T(8,128)(2,1)S(1)}, u32[]{:S(2)}, u32[]{:S(2)}) collective-permute-start(bf16[8,1024]{1,0:T(8,128)(2,1)S(1)} %get-tuple-element.50), channel_id=1, source_target_pairs={{0,128},{64,192},{128,0},{192,64},{1,129},{65,193},{129,1},{193,65... | collective-permute-start | bytes 49160 | tf_op jit(solution)/shard_map/ppermute | solution.py:297
  47.7 3.7 %collective-permute-start.12 = (bf16[8,1024]{1,0:T(8,128)(2,1)S(1)}, bf16[8,1024]{1,0:T(8,128)(2,1)S(1)}, u32[]{:S(2)}, u32[]{:S(2)}) collective-permute-start(bf16[8,1024]{1,0:T(8,128)(2,1)S(1)} %get-tuple-element.51), channel_id=1, source_target_pairs={{0,64},{64,128},{128,192},{192,0},{1,65},{65,129},{129,193},{193,1... | collective-permute-start | bytes 49160 | tf_op jit(solution)/shard_map/ppermute | solution.py:297
  70.6 2.0 %collective-permute-start.13 = (bf16[32,8,1152]{2,1,0:T(8,128)(2,1)S(1)}, bf16[32,8,1152]{2,1,0:T(8,128)(2,1)S(1)}, u32[]{:S(2)}, u32[]{:S(2)}) collective-permute-start(bf16[32,8,1152]{2,1,0:T(8,128)(2,1)S(1)} %all_to_all.16.own_ref), channel_id=1, source_target_pairs={{0,1},{1,0},{2,3},{3,2},{4,5},{5,4},{6,7},{7,6},{8,9},{9,8},{10,11... | collective-permute-start | bytes 1769480 | tf_op jit(solution)/shard_map/ppermute | solution.py:365
  74.1 1.3 %collective-permute-start.15 = (bf16[32,8,128]{2,1,0:T(8,128)(2,1)S(1)}, bf16[32,8,128]{2,1,0:T(8,128)(2,1)S(1)}, u32[]{:S(2)}, u32[]{:S(2)}) collective-permute-start(bf16[32,8,128]{2,1,0:T(8,128)(2,1)S(1)} %get-tuple-element.64), channel_id=1, source_target_pairs={{0,1},{1,0},{2,3},{3,2},{4,5},{5,4},{6,7},{7,6},{8,9},{9,8},{10,11... | collective-permute-start | bytes 196616 | tf_op jit(solution)/shard_map/ppermute | solution.py:377
  74.3 2.7 %collective-permute-start.17 = (bf16[32,8,128]{2,1,0:T(8,128)(2,1)S(1)}, bf16[32,8,128]{2,1,0:T(8,128)(2,1)S(1)}, u32[]{:S(2)}, u32[]{:S(2)}) collective-permute-start(bf16[32,8,128]{2,1,0:T(8,128)(2,1)S(1)} %get-tuple-element.66), channel_id=1, source_target_pairs={{0,1},{1,0},{2,3},{3,2},{4,5},{5,4},{6,7},{7,6},{8,9},{9,8},{10,11... | collective-permute-start | bytes 196616 | tf_op jit(solution)/shard_map/ppermute | solution.py:377
  74.7 2.8 %collective-permute-start.19 = (bf16[32,8,128]{2,1,0:T(8,128)(2,1)S(1)}, bf16[32,8,128]{2,1,0:T(8,128)(2,1)S(1)}, u32[]{:S(2)}, u32[]{:S(2)}) collective-permute-start(bf16[32,8,128]{2,1,0:T(8,128)(2,1)S(1)} %get-tuple-element.68), channel_id=1, source_target_pairs={{0,1},{1,0},{2,3},{3,2},{4,5},{5,4},{6,7},{7,6},{8,9},{9,8},{10,11... | collective-permute-start | bytes 196616 | tf_op jit(solution)/shard_map/ppermute | solution.py:377
  74.8 6.1 %collective-permute-start.14 = (bf16[32,8,128]{2,1,0:T(8,128)(2,1)S(1)}, bf16[32,8,128]{2,1,0:T(8,128)(2,1)S(1)}, u32[]{:S(2)}, u32[]{:S(2)}) collective-permute-start(bf16[32,8,128]{2,1,0:T(8,128)(2,1)S(1)} %get-tuple-element.62), channel_id=1, source_target_pairs={{0,1},{1,0},{2,3},{3,2},{4,5},{5,4},{6,7},{7,6},{8,9},{9,8},{10,11... | collective-permute-start | bytes 196616 | tf_op jit(solution)/shard_map/ppermute | solution.py:377
  75.4 5.5 %collective-permute-start.16 = (bf16[32,8,128]{2,1,0:T(8,128)(2,1)S(1)}, bf16[32,8,128]{2,1,0:T(8,128)(2,1)S(1)}, u32[]{:S(2)}, u32[]{:S(2)}) collective-permute-start(bf16[32,8,128]{2,1,0:T(8,128)(2,1)S(1)} %shard_map.89), channel_id=1, source_target_pairs={{0,64},{64,128},{128,192},{192,0},{1,65},{65,129},{129,193},{193,1... | collective-permute-start | bytes 196616 | tf_op jit(solution)/shard_map/ppermute | solution.py:297
  77.0 6.5 %collective-permute-start.18 = (bf16[32,8,128]{2,1,0:T(8,128)(2,1)S(1)}, bf16[32,8,128]{2,1,0:T(8,128)(2,1)S(1)}, u32[]{:S(2)}, u32[]{:S(2)}) collective-permute-start(bf16[32,8,128]{2,1,0:T(8,128)(2,1)S(1)} %shard_map.90), channel_id=1, source_target_pairs={{0,128},{64,192},{128,0},{192,64},{1,129},{65,193},{129,1},{193,65... | collective-permute-start | bytes 196616 | tf_op jit(solution)/shard_map/ppermute | solution.py:297
  77.5 6.4 %collective-permute-start.20 = (bf16[32,8,128]{2,1,0:T(8,128)(2,1)S(1)}, bf16[32,8,128]{2,1,0:T(8,128)(2,1)S(1)}, u32[]{:S(2)}, u32[]{:S(2)}) collective-permute-start(bf16[32,8,128]{2,1,0:T(8,128)(2,1)S(1)} %shard_map.91), channel_id=1, source_target_pairs={{0,192},{64,0},{128,64},{192,128},{1,193},{65,1},{129,65},{193,129... | collective-permute-start | bytes 196616 | tf_op jit(solution)/shard_map/ppermute | solution.py:297

commit v7 on v6

--- a/solution.py
+++ b/solution.py
@@ -225,8 +225,8 @@
     shift = jnp.sum(full_ref[:slots, :] * wide[slots:, :], axis=1, keepdims=True)
     shift = jnp.concatenate([shift, shift], axis=0)
     high, low = split(shift)
-    st = stats(iota((2 * slots, STAT), 1), side[:, 0:1], high, low).astype(BF)
-    block = jnp.concatenate([body, st], axis=1)
+    st = stats(iota((2 * slots, STAT), 1), side[:, 0:1], high, low)
+    block = jnp.concatenate([wide[:slots], pltpu.roll(wide, slots, 0)[:slots], st[:slots]], axis=1).astype(BF)
     out_ref[...] = jnp.broadcast_to(block[None], out_ref.shape)
 
 
@@ -240,12 +240,11 @@
     upper = iota((1, 8, 1), 1) < 4
     own, oth = own_ref[...].astype(F32), oth_ref[...].astype(F32)
     even, odd = jnp.where(zero, own, oth), jnp.where(zero, oth, own)
-    first = jnp.where(upper, even, swap_halves(odd)).reshape(n, width + STAT)
-    second = jnp.where(upper, swap_halves(even), odd).reshape(n, width + STAT)
-    slot_out, scaled = first[:, :width].astype(BF), second[:, :width].astype(BF)
+    both = jnp.concatenate([even, odd], axis=1).reshape(n, 2 * width + STAT)
+    slot_out, scaled = both[:, :width].astype(BF), both[:, width:2 * width].astype(BF)
     so_ref[...] = slot_out
     sc_ref[...] = scaled
-    side = first[:, width:].T
+    side = both[:, 2 * width:].T
     point, shift = side[0:1, :], side[1:2, :] + side[2:3, :]
     comb = softmax_rows(logits)
     comb_ref[...] = comb.astype(BF)
@@ -360,7 +359,7 @@
         flops=32 * videos * w_in.size,
     )
     parts = [shifted(partial[k], -k, videos) for k in range(1, videos)]
-    (block,) = call(finish_slots, [shape((owners, 8, wide), BF)], partial[0], *parts, full, side)
+    (block,) = call(finish_slots, [shape((owners, 4, 2 * width + STAT), BF)], partial[0], *parts, full, side)
     mine = lax.all_to_all(block, ZY, 0, 0, tiled=True)
     theirs = lax.ppermute(mine, "c", swap)
 

time: 98.9 us -> 98.3 us (level)
  no operation moved by 1% of the time
where the time goes in v7:
time: 98.3 us; the launch traced here: 98.1 us
  blocking collectives  50 us (51%)
  starting transfers between devices  20.3 us (21%)
  Pallas kernels  14 us (14%)
  waiting for transfers between devices  11.2 us (11%)
  local copies, waits for them, and re-layouts  1.92 us (2%)
    all_to_all x1, blocking collectives, on_device(): mine = lax.all_to_all(block, ZY, 0, 0, tiled=True)  18.6 us
    ppermute x12, starting transfers between devices, shifted(): lax.ppermute(value, axis, [(i, (i + step) % size) for i in range(size)])  18.1 us
    all_to_all x1, blocking collectives, on_device(): shards = lax.all_to_all(merged, 'z', 0, 0, tiled=True)  17.5 us
    all_to_all x1, blocking collectives, on_device(): pieces = lax.all_to_all(half, ZY, 0, 0, tiled=True)  14 us
    ppermute x12, waiting for transfers between devices, shifted(): lax.ppermute(value, axis, [(i, (i + step) % size) for i in range(size)])  8.67 us
    pallas_call x14, Pallas kernels, call(): pl.pallas_call(body, out_shape=outs, in_specs=[pl.BlockSpec(memory_space=...  7.77 us
    pallas_call x1, Pallas kernels, on_device(): pl.pallas_call(reduce_tokens, out_shape=[shape(tiles, BF)] * (2 * rows_y)...  3.6 us
    pallas_call x1, Pallas kernels, on_device(): pl.pallas_call(turn_weights, out_shape=[shape(w_in.shape, BF), shape(w_ou...  2.4 us
  transfers between devices with their start and end apart: 21, of which 11 were waited for; matrix products, arithmetic and copies ran while one was open for 0% of the time, Pallas kernels for 5%

profile of v7, /device:TPU:6, one launch (start us, length us, event | category | flops | bytes accessed | tf_op | source)
XLA Modules:
  0.0 98.1 jit_solution(10325523481953952836)
XLA Ops:
  0.6 3.6 %shard_map.76 = (bf16[65,8,128]{2,1,0:T(8,128)(2,1)S(1)}, bf16[65,8,128]{2,1,0:T(8,128)(2,1)S(1)}, bf16[65,8,128]{2,1,0:T(8,128)(2,1)S(1)}, bf16[65,8,128]{2,1,0...) custom-call(bf16[512,1024]{1,0:T(8,128)(2,1)} %bitcast.4, ...), custom_call_target="tpu_custom_call" | custom-call | flops 1073741824 | bytes 4194304 | tf_op jit(solution)/shard_map/pallas_call | solution.py:313
  4.2 0.1 collective-permute-start.1
  4.3 0.5 collective-permute-start
  4.8 0.1 collective-permute-start.3
  4.9 0.4 collective-permute-start.5
  5.3 0.3 collective-permute-done.1.b_ref
  5.7 0.1 shard_map.78
  5.8 1.7 %collective-permute-start.2 = (bf16[65,8,128]{2,1,0:T(8,128)(2,1)S(1)}, bf16[65,8,128]{2,1,0:T(8,128)(2,1)S(1)}, u32[]{:S(2)}, u32[]{:S(2)}) collective-permute-start(bf16[65,8,128]{2,1,0:T(8,128)(2,1)S(1)} %shard_map.78), channel_id=1, source_target_pairs={{0,2},{2,4},{4,6},{6,0},{1,3},{3,5},{5,7},{7,1},{8,10},{10,12},{12... | collective-permute-start | bytes 399368 | tf_op jit(solution)/shard_map/ppermute | solution.py:296
  7.5 0.0 collective-permute-done.3.b_ref
  7.5 0.1 shard_map.79
  7.6 3.0 %collective-permute-start.4 = (bf16[65,8,128]{2,1,0:T(8,128)(2,1)S(1)}, bf16[65,8,128]{2,1,0:T(8,128)(2,1)S(1)}, u32[]{:S(2)}, u32[]{:S(2)}) collective-permute-start(bf16[65,8,128]{2,1,0:T(8,128)(2,1)S(1)} %shard_map.79), channel_id=1, source_target_pairs={{0,4},{2,6},{4,0},{6,2},{1,5},{3,7},{5,1},{7,3},{8,12},{10,14},{12... | collective-permute-start | bytes 399368 | tf_op jit(solution)/shard_map/ppermute | solution.py:296
  10.6 0.0 collective-permute-done.5.b_ref
  10.6 0.0 copy-start
  10.6 0.1 shard_map.80.after_ref
  10.8 1.4 %collective-permute-start.6 = (bf16[65,8,128]{2,1,0:T(8,128)(2,1)S(1)}, bf16[65,8,128]{2,1,0:T(8,128)(2,1)S(1)}, u32[]{:S(2)}, u32[]{:S(2)}) collective-permute-start(bf16[65,8,128]{2,1,0:T(8,128)(2,1)S(1)} %shard_map.80.after_ref), channel_id=1, source_target_pairs={{0,6},{2,0},{4,2},{6,4},{1,7},{3,1},{5,3},{7,5},{8,14},{10,8},{12,... | collective-permute-start | bytes 399368 | tf_op jit(solution)/shard_map/ppermute | solution.py:296
  12.2 0.6 copy-done
  12.8 1.3 %copy-done.1 = bf16[2,1024,1024]{2,1,0:T(8,128)(2,1)S(1)} copy-done((bf16[2,1024,1024]{2,1,0:T(8,128)(2,1)S(1)}, bf16[2,1024,1024]{2,1,0:T(8,128)(2,1)}, u32[]{:S(2)}) %copy-start.1) | copy-done | bytes 4194328
  14.1 2.4 %shard_map.81 = (bf16[2,1024,1024]{2,1,0:T(8,128)(2,1)S(1)}, bf16[2,1024,1024]{2,1,0:T(8,128)(2,1)S(1)}) custom-call(bf16[2,1024,1024]{2,1,0:T(8,128)(2,1)S(1)} %copy-done, bf16[2,1024,1024]{2,1,0:T(8,128)(2,1)S(1)} %copy-done.1, bf16[65,8,128]{2,1,0:T(8,128)(2,1)S(1)} %shard_map.80.after_ref), custom_call_target="tpu_custom_call" | custom-call | flops 5368709120 | bytes 16777216 | tf_op jit(solution)/shard_map/pallas_call | solution.py:335
  16.5 0.0 collective-permute-done.b_ref
  16.5 0.1 shard_map.77.a_ref
  16.7 0.0 collective-permute-done.2.b_ref
  16.7 0.2 collective-permute-done.4.c_ref
  16.8 0.0 collective-permute-done.6.d_ref
  16.8 0.2 shard_map.82
  17.0 17.5 %all_to_all.15.in_ref = bf16[8,9,8,128]{3,2,1,0:T(8,128)(2,1)S(1)} all-to-all(bf16[8,9,8,128]{3,2,1,0:T(8,128)(2,1)S(1)} %shard_map.82), channel_id=1, replica_groups=mesh['x'=4,'z'=8,'y'=4,'c'=2] {'z'}, dimensions={0} | all-to-all | bytes 294912 | tf_op jit(solution)/shard_map/all_to_all | solution.py:350
  34.5 0.2 shard_map.83
  34.8 0.9 collective-permute-start.9
  35.7 1.1 %collective-permute-start.8 = (bf16[8,1024]{1,0:T(8,128)(2,1)S(1)}, bf16[8,1024]{1,0:T(8,128)(2,1)S(1)}, u32[]{:S(2)}, u32[]{:S(2)}) collective-permute-start(bf16[8,1024]{1,0:T(8,128)(2,1)S(1)} %get-tuple-element.46.own_ref), channel_id=1, source_target_pairs={{0,128},{64,192},{128,0},{192,64},{1,129},{65,193},{129,1},{193,65... | collective-permute-start | bytes 49160 | tf_op jit(solution)/shard_map/ppermute | solution.py:296
  36.8 2.1 %collective-permute-start.7 = (bf16[8,1024]{1,0:T(8,128)(2,1)S(1)}, bf16[8,1024]{1,0:T(8,128)(2,1)S(1)}, u32[]{:S(2)}, u32[]{:S(2)}) collective-permute-start(bf16[8,1024]{1,0:T(8,128)(2,1)S(1)} %get-tuple-element.46.own_ref), channel_id=1, source_target_pairs={{0,64},{64,128},{128,192},{192,0},{1,65},{65,129},{129,193},{193,1... | collective-permute-start | bytes 49160 | tf_op jit(solution)/shard_map/ppermute | solution.py:296
  38.9 0.9 collective-permute-done.9.c_ref
  39.8 1.1 %collective-permute-done.8.b_ref = bf16[8,1024]{1,0:T(8,128)(2,1)S(1)} collective-permute-done((bf16[8,1024]{1,0:T(8,128)(2,1)S(1)}, bf16[8,1024]{1,0:T(8,128)(2,1)S(1)}, u32[]{:S(2)}, u32[]{:S(2)}) %collective-permute-start.8) | collective-permute-done | bytes 16416 | tf_op jit(solution)/shard_map/ppermute | solution.py:296
  40.9 0.0 collective-permute-done.7.a_ref
  40.9 2.3 %shard_map.84 = (bf16[8,1024]{1,0:T(8,128)(2,1)S(1)}, bf16[8,1024]{1,0:T(8,128)(2,1)S(1)}, bf16[8,1024]{1,0:T(8,128)(2,1)S(1)}, bf16[8,1024]{1,0:T(8,128)(2,1)S(1)}) custom-call(bf16[8,1024]{1,0:T(8,128)(2,1)S(1)} %get-tuple-element.46.own_ref, bf16[8,1024]{1,0:T(8,128)(2,1)S(1)} %collective-permute-done.7.a_ref, ...), custom_call_target="tpu_custom_call" | custom-call | flops 268435456 | bytes 16973824 | tf_op jit(solution)/shard_map/pallas_call | solution.py:30
  43.3 1.8 %collective-permute-start.10 = (bf16[8,1024]{1,0:T(8,128)(2,1)S(1)}, bf16[8,1024]{1,0:T(8,128)(2,1)S(1)}, u32[]{:S(2)}, u32[]{:S(2)}) collective-permute-start(bf16[8,1024]{1,0:T(8,128)(2,1)S(1)} %get-tuple-element.49), channel_id=1, source_target_pairs={{0,192},{64,0},{128,64},{192,128},{1,193},{65,1},{129,65},{193,129... | collective-permute-start | bytes 49160 | tf_op jit(solution)/shard_map/ppermute | solution.py:296
  45.1 2.6 %collective-permute-start.11 = (bf16[8,1024]{1,0:T(8,128)(2,1)S(1)}, bf16[8,1024]{1,0:T(8,128)(2,1)S(1)}, u32[]{:S(2)}, u32[]{:S(2)}) collective-permute-start(bf16[8,1024]{1,0:T(8,128)(2,1)S(1)} %get-tuple-element.50), channel_id=1, source_target_pairs={{0,128},{64,192},{128,0},{192,64},{1,129},{65,193},{129,1},{193,65... | collective-permute-start | bytes 49160 | tf_op jit(solution)/shard_map/ppermute | solution.py:296
  47.7 0.3 collective-permute-start.12
  48.0 0.3 collective-permute-done.10.a_ref
  48.3 2.0 %collective-permute-done.11.b_ref = bf16[8,1024]{1,0:T(8,128)(2,1)S(1)} collective-permute-done((bf16[8,1024]{1,0:T(8,128)(2,1)S(1)}, bf16[8,1024]{1,0:T(8,128)(2,1)S(1)}, u32[]{:S(2)}, u32[]{:S(2)}) %collective-permute-start.11) | collective-permute-done | bytes 16416 | tf_op jit(solution)/shard_map/ppermute | solution.py:296
  50.3 1.1 %collective-permute-done.12.c_ref = bf16[8,1024]{1,0:T(8,128)(2,1)S(1)} collective-permute-done((bf16[8,1024]{1,0:T(8,128)(2,1)S(1)}, bf16[8,1024]{1,0:T(8,128)(2,1)S(1)}, u32[]{:S(2)}, u32[]{:S(2)}) %collective-permute-start.12) | collective-permute-done | bytes 16416 | tf_op jit(solution)/shard_map/ppermute | solution.py:296
  51.4 0.3 shard_map.85
  51.7 18.6 %all_to_all.16.own_ref = bf16[32,4,2176]{2,1,0:T(4,128)(2,1)S(1)} all-to-all(bf16[32,4,2176]{2,1,0:T(4,128)(2,1)S(1)} %shard_map.85), channel_id=1, replica_groups=mesh['x'=4,'z'=8,'y'=4,'c'=2] {'z','y'}, dimensions={0} | all-to-all | bytes 1114112 | tf_op jit(solution)/shard_map/all_to_all | solution.py:363
  70.3 0.0 collective-permute-start.13
  70.3 2.0 %collective-permute-done.13.oth_ref = bf16[32,4,2176]{2,1,0:T(4,128)(2,1)S(1)} collective-permute-done((bf16[32,4,2176]{2,1,0:T(4,128)(2,1)S(1)}, bf16[32,4,2176]{2,1,0:T(4,128)(2,1)S(1)}, u32[]{:S(2)}, u32[]{:S(2)}) %collective-permute-start.13) | collective-permute-done | bytes 557088 | tf_op jit(solution)/shard_map/ppermute | solution.py:364
  72.2 0.0 copy-done.2
  72.2 0.0 copy-done.3
  72.2 1.5 %shard_map.86 = (bf16[32,8,128]{2,1,0:T(8,128)(2,1)S(1)}, bf16[32,8,128]{2,1,0:T(8,128)(2,1)S(1)}, bf16[32,8,128]{2,1,0:T(8,128)(2,1)S(1)}, bf16[32,8,128]{2,1,0...) custom-call(f32[512,256]{1,0:T(8,128)S(1)} %get-tuple-element.36.log, ...), custom_call_target="tpu_custom_call" | custom-call | flops 1342177280 | bytes 8454144 | tf_op jit(solution)/shard_map/pallas_call | solution.py:30
  73.7 0.2 collective-permute-start.15
  74.0 0.4 collective-permute-start.17
  74.3 0.1 collective-permute-start.19
  74.5 0.4 collective-permute-start.14
  74.8 0.2 collective-permute-done.15.b_ref
  75.1 1.5 %collective-permute-start.16 = (bf16[32,8,128]{2,1,0:T(8,128)(2,1)S(1)}, bf16[32,8,128]{2,1,0:T(8,128)(2,1)S(1)}, u32[]{:S(2)}, u32[]{:S(2)}) collective-permute-start(bf16[32,8,128]{2,1,0:T(8,128)(2,1)S(1)} %shard_map.89), channel_id=1, source_target_pairs={{0,64},{64,128},{128,192},{192,0},{1,65},{65,129},{129,193},{193,1... | collective-permute-start | bytes 196616 | tf_op jit(solution)/shard_map/ppermute | solution.py:296
  76.6 0.0 collective-permute-done.17.b_ref
  76.7 0.4 collective-permute-start.18
  77.1 0.0 collective-permute-done.19.b_ref
  77.1 1.2 %collective-permute-start.20 = (bf16[32,8,128]{2,1,0:T(8,128)(2,1)S(1)}, bf16[32,8,128]{2,1,0:T(8,128)(2,1)S(1)}, u32[]{:S(2)}, u32[]{:S(2)}) collective-permute-start(bf16[32,8,128]{2,1,0:T(8,128)(2,1)S(1)} %shard_map.91), channel_id=1, source_target_pairs={{0,192},{64,0},{128,64},{192,128},{1,193},{65,1},{129,65},{193,129... | collective-permute-start | bytes 196616 | tf_op jit(solution)/shard_map/ppermute | solution.py:296
  78.3 0.0 copy-done.4
  78.3 2.2 %shard_map.87 = (bf16[512,1024]{1,0:T(8,128)(2,1)}, bf16[512,1024]{1,0:T(8,128)(2,1)}) custom-call(bf16[512,256]{1,0:T(8,128)(2,1)S(1)} %get-tuple-element.54.comb_ref, bf16[256,1024]{1,0:T(8,128)(2,1)S(1)} %get-tuple-element.55.so_ref, bf16[512,256]{1,0:T(8,128)(2,1)S(1)} %get-tuple-element.56.dlog_ref, bf16[1024,256]{1,0:T(8,128)(2,1)S(1)} %copy-done.4, ...), custom_call_target="tpu_custom_call" | custom-call | flops 805306368 | bytes 6553600 | tf_op jit(solution)/shard_map/pallas_call | solution.py:30
  80.5 0.0 collective-permute-done.14.b_ref
  80.5 0.0 collective-permute-done.16.a_ref
  80.5 2.6 %collective-permute-done.18.b_ref = bf16[32,8,128]{2,1,0:T(8,128)(2,1)S(1)} collective-permute-done((bf16[32,8,128]{2,1,0:T(8,128)(2,1)S(1)}, bf16[32,8,128]{2,1,0:T(8,128)(2,1)S(1)}, u32[]{:S(2)}, u32[]{:S(2)}) %collective-permute-start.18) | collective-permute-done | bytes 65568 | tf_op jit(solution)/shard_map/ppermute | solution.py:296
  83.1 0.4 collective-permute-done.20.c_ref
  83.6 14.0 %all_to_all.17.in_ref = bf16[32,8,128]{2,1,0:T(8,128)(2,1)S(1)} all-to-all(bf16[32,8,128]{2,1,0:T(8,128)(2,1)S(1)} %shard_map.92), channel_id=1, replica_groups=mesh['x'=4,'z'=8,'y'=4,'c'=2] {'z','y'}, dimensions={0} | all-to-all | bytes 131072 | tf_op jit(solution)/shard_map/all_to_all | solution.py:393
  97.5 0.6 shard_map.93
  (9 shorter events, 0.1 us)
Async XLA Ops:
  4.2 1.4 %collective-permute-start.1 = (bf16[65,8,128]{2,1,0:T(8,128)(2,1)S(1)}, bf16[65,8,128]{2,1,0:T(8,128)(2,1)S(1)}, u32[]{:S(2)}, u32[]{:S(2)}) collective-permute-start(bf16[65,8,128]{2,1,0:T(8,128)(2,1)S(1)} %get-tuple-element.40), channel_id=1, source_target_pairs={{0,1},{1,0},{2,3},{3,2},{4,5},{5,4},{6,7},{7,6},{8,9},{9,8},{10,11... | collective-permute-start | bytes 399368 | tf_op jit(solution)/shard_map/ppermute | solution.py:328
  4.3 12.2 %collective-permute-start = (bf16[65,8,128]{2,1,0:T(8,128)(2,1)S(1)}, bf16[65,8,128]{2,1,0:T(8,128)(2,1)S(1)}, u32[]{:S(2)}, u32[]{:S(2)}) collective-permute-start(bf16[65,8,128]{2,1,0:T(8,128)(2,1)S(1)} %get-tuple-element.38), channel_id=1, source_target_pairs={{0,1},{1,0},{2,3},{3,2},{4,5},{5,4},{6,7},{7,6},{8,9},{9,8},{10,11... | collective-permute-start | bytes 399368 | tf_op jit(solution)/shard_map/ppermute | solution.py:328
  4.8 2.6 %collective-permute-start.3 = (bf16[65,8,128]{2,1,0:T(8,128)(2,1)S(1)}, bf16[65,8,128]{2,1,0:T(8,128)(2,1)S(1)}, u32[]{:S(2)}, u32[]{:S(2)}) collective-permute-start(bf16[65,8,128]{2,1,0:T(8,128)(2,1)S(1)} %get-tuple-element.42), channel_id=1, source_target_pairs={{0,1},{1,0},{2,3},{3,2},{4,5},{5,4},{6,7},{7,6},{8,9},{9,8},{10,11... | collective-permute-start | bytes 399368 | tf_op jit(solution)/shard_map/ppermute | solution.py:328
  4.9 5.7 %collective-permute-start.5 = (bf16[65,8,128]{2,1,0:T(8,128)(2,1)S(1)}, bf16[65,8,128]{2,1,0:T(8,128)(2,1)S(1)}, u32[]{:S(2)}, u32[]{:S(2)}) collective-permute-start(bf16[65,8,128]{2,1,0:T(8,128)(2,1)S(1)} %get-tuple-element.44), channel_id=1, source_target_pairs={{0,1},{1,0},{2,3},{3,2},{4,5},{5,4},{6,7},{7,6},{8,9},{9,8},{10,11... | collective-permute-start | bytes 399368 | tf_op jit(solution)/shard_map/ppermute | solution.py:328
  5.8 10.8 %collective-permute-start.2 = (bf16[65,8,128]{2,1,0:T(8,128)(2,1)S(1)}, bf16[65,8,128]{2,1,0:T(8,128)(2,1)S(1)}, u32[]{:S(2)}, u32[]{:S(2)}) collective-permute-start(bf16[65,8,128]{2,1,0:T(8,128)(2,1)S(1)} %shard_map.78), channel_id=1, source_target_pairs={{0,2},{2,4},{4,6},{6,0},{1,3},{3,5},{5,7},{7,1},{8,10},{10,12},{12... | collective-permute-start | bytes 399368 | tf_op jit(solution)/shard_map/ppermute | solution.py:296
  7.6 9.2 %collective-permute-start.4 = (bf16[65,8,128]{2,1,0:T(8,128)(2,1)S(1)}, bf16[65,8,128]{2,1,0:T(8,128)(2,1)S(1)}, u32[]{:S(2)}, u32[]{:S(2)}) collective-permute-start(bf16[65,8,128]{2,1,0:T(8,128)(2,1)S(1)} %shard_map.79), channel_id=1, source_target_pairs={{0,4},{2,6},{4,0},{6,2},{1,5},{3,7},{5,1},{7,3},{8,12},{10,14},{12... | collective-permute-start | bytes 399368 | tf_op jit(solution)/shard_map/ppermute | solution.py:296
  10.6 2.2 %copy-start = (bf16[2,1024,1024]{2,1,0:T(8,128)(2,1)S(1)}, bf16[2,1024,1024]{2,1,0:T(8,128)(2,1)}, u32[]{:S(2)}) copy-start(bf16[2,1024,1024]{2,1,0:T(8,128)(2,1)} %win_ref.3) | copy-start | bytes 12582916
  10.6 3.5 %copy-start.1 = (bf16[2,1024,1024]{2,1,0:T(8,128)(2,1)S(1)}, bf16[2,1024,1024]{2,1,0:T(8,128)(2,1)}, u32[]{:S(2)}) copy-start(bf16[2,1024,1024]{2,1,0:T(8,128)(2,1)} %wout_ref.3) | copy-start | bytes 12582916
  10.8 6.0 %collective-permute-start.6 = (bf16[65,8,128]{2,1,0:T(8,128)(2,1)S(1)}, bf16[65,8,128]{2,1,0:T(8,128)(2,1)S(1)}, u32[]{:S(2)}, u32[]{:S(2)}) collective-permute-start(bf16[65,8,128]{2,1,0:T(8,128)(2,1)S(1)} %shard_map.80.after_ref), channel_id=1, source_target_pairs={{0,6},{2,0},{4,2},{6,4},{1,7},{3,1},{5,3},{7,5},{8,14},{10,8},{12,... | collective-permute-start | bytes 399368 | tf_op jit(solution)/shard_map/ppermute | solution.py:296
  34.8 5.0 %collective-permute-start.9 = (bf16[8,1024]{1,0:T(8,128)(2,1)S(1)}, bf16[8,1024]{1,0:T(8,128)(2,1)S(1)}, u32[]{:S(2)}, u32[]{:S(2)}) collective-permute-start(bf16[8,1024]{1,0:T(8,128)(2,1)S(1)} %get-tuple-element.46.own_ref), channel_id=1, source_target_pairs={{0,192},{64,0},{128,64},{192,128},{1,193},{65,1},{129,65},{193,129... | collective-permute-start | bytes 49160 | tf_op jit(solution)/shard_map/ppermute | solution.py:296
  35.7 5.2 %collective-permute-start.8 = (bf16[8,1024]{1,0:T(8,128)(2,1)S(1)}, bf16[8,1024]{1,0:T(8,128)(2,1)S(1)}, u32[]{:S(2)}, u32[]{:S(2)}) collective-permute-start(bf16[8,1024]{1,0:T(8,128)(2,1)S(1)} %get-tuple-element.46.own_ref), channel_id=1, source_target_pairs={{0,128},{64,192},{128,0},{192,64},{1,129},{65,193},{129,1},{193,65... | collective-permute-start | bytes 49160 | tf_op jit(solution)/shard_map/ppermute | solution.py:296
  36.8 4.1 %collective-permute-start.7 = (bf16[8,1024]{1,0:T(8,128)(2,1)S(1)}, bf16[8,1024]{1,0:T(8,128)(2,1)S(1)}, u32[]{:S(2)}, u32[]{:S(2)}) collective-permute-start(bf16[8,1024]{1,0:T(8,128)(2,1)S(1)} %get-tuple-element.46.own_ref), channel_id=1, source_target_pairs={{0,64},{64,128},{128,192},{192,0},{1,65},{65,129},{129,193},{193,1... | collective-permute-start | bytes 49160 | tf_op jit(solution)/shard_map/ppermute | solution.py:296
  40.9 31.3 %copy-start.2 = (bf16[1,512,1024]{2,1,0:T(8,128)(2,1)S(1)}, bf16[1,512,1024]{2,1,0:T(8,128)(2,1)}, u32[]{:S(2)}) copy-start(bf16[1,512,1024]{2,1,0:T(8,128)(2,1)} %param.5) | copy-start | bytes 3145732
  40.9 31.3 %copy-start.3 = (bf16[1,512,1024]{2,1,0:T(8,128)(2,1)S(1)}, bf16[1,512,1024]{2,1,0:T(8,128)(2,1)}, u32[]{:S(2)}) copy-start(bf16[1,512,1024]{2,1,0:T(8,128)(2,1)} %param.9) | copy-start | bytes 3145732
  43.3 35.1 %copy-start.4 = (bf16[1024,256]{1,0:T(8,128)(2,1)S(1)}, bf16[1024,256]{1,0:T(8,128)(2,1)}, u32[]{:S(2)}) copy-start(bf16[1024,256]{1,0:T(8,128)(2,1)} %par_ref.1) | copy-start | bytes 1572868
  43.3 5.0 %collective-permute-start.10 = (bf16[8,1024]{1,0:T(8,128)(2,1)S(1)}, bf16[8,1024]{1,0:T(8,128)(2,1)S(1)}, u32[]{:S(2)}, u32[]{:S(2)}) collective-permute-start(bf16[8,1024]{1,0:T(8,128)(2,1)S(1)} %get-tuple-element.49), channel_id=1, source_target_pairs={{0,192},{64,0},{128,64},{192,128},{1,193},{65,1},{129,65},{193,129... | collective-permute-start | bytes 49160 | tf_op jit(solution)/shard_map/ppermute | solution.py:296
  45.1 5.2 %collective-permute-start.11 = (bf16[8,1024]{1,0:T(8,128)(2,1)S(1)}, bf16[8,1024]{1,0:T(8,128)(2,1)S(1)}, u32[]{:S(2)}, u32[]{:S(2)}) collective-permute-start(bf16[8,1024]{1,0:T(8,128)(2,1)S(1)} %get-tuple-element.50), channel_id=1, source_target_pairs={{0,128},{64,192},{128,0},{192,64},{1,129},{65,193},{129,1},{193,65... | collective-permute-start | bytes 49160 | tf_op jit(solution)/shard_map/ppermute | solution.py:296
  47.7 3.7 %collective-permute-start.12 = (bf16[8,1024]{1,0:T(8,128)(2,1)S(1)}, bf16[8,1024]{1,0:T(8,128)(2,1)S(1)}, u32[]{:S(2)}, u32[]{:S(2)}) collective-permute-start(bf16[8,1024]{1,0:T(8,128)(2,1)S(1)} %get-tuple-element.51), channel_id=1, source_target_pairs={{0,64},{64,128},{128,192},{192,0},{1,65},{65,129},{129,193},{193,1... | collective-permute-start | bytes 49160 | tf_op jit(solution)/shard_map/ppermute | solution.py:296
  70.3 2.0 %collective-permute-start.13 = (bf16[32,4,2176]{2,1,0:T(4,128)(2,1)S(1)}, bf16[32,4,2176]{2,1,0:T(4,128)(2,1)S(1)}, u32[]{:S(2)}, u32[]{:S(2)}) collective-permute-start(bf16[32,4,2176]{2,1,0:T(4,128)(2,1)S(1)} %all_to_all.16.own_ref), channel_id=1, source_target_pairs={{0,1},{1,0},{2,3},{3,2},{4,5},{5,4},{6,7},{7,6},{8,9},{9,8},{10,11... | collective-permute-start | bytes 1671176 | tf_op jit(solution)/shard_map/ppermute | solution.py:364
  73.7 1.3 %collective-permute-start.15 = (bf16[32,8,128]{2,1,0:T(8,128)(2,1)S(1)}, bf16[32,8,128]{2,1,0:T(8,128)(2,1)S(1)}, u32[]{:S(2)}, u32[]{:S(2)}) collective-permute-start(bf16[32,8,128]{2,1,0:T(8,128)(2,1)S(1)} %get-tuple-element.64), channel_id=1, source_target_pairs={{0,1},{1,0},{2,3},{3,2},{4,5},{5,4},{6,7},{7,6},{8,9},{9,8},{10,11... | collective-permute-start | bytes 196616 | tf_op jit(solution)/shard_map/ppermute | solution.py:376
  74.0 2.7 %collective-permute-start.17 = (bf16[32,8,128]{2,1,0:T(8,128)(2,1)S(1)}, bf16[32,8,128]{2,1,0:T(8,128)(2,1)S(1)}, u32[]{:S(2)}, u32[]{:S(2)}) collective-permute-start(bf16[32,8,128]{2,1,0:T(8,128)(2,1)S(1)} %get-tuple-element.66), channel_id=1, source_target_pairs={{0,1},{1,0},{2,3},{3,2},{4,5},{5,4},{6,7},{7,6},{8,9},{9,8},{10,11... | collective-permute-start | bytes 196616 | tf_op jit(solution)/shard_map/ppermute | solution.py:376
  74.3 2.7 %collective-permute-start.19 = (bf16[32,8,128]{2,1,0:T(8,128)(2,1)S(1)}, bf16[32,8,128]{2,1,0:T(8,128)(2,1)S(1)}, u32[]{:S(2)}, u32[]{:S(2)}) collective-permute-start(bf16[32,8,128]{2,1,0:T(8,128)(2,1)S(1)} %get-tuple-element.68), channel_id=1, source_target_pairs={{0,1},{1,0},{2,3},{3,2},{4,5},{5,4},{6,7},{7,6},{8,9},{9,8},{10,11... | collective-permute-start | bytes 196616 | tf_op jit(solution)/shard_map/ppermute | solution.py:376
  74.5 6.0 %collective-permute-start.14 = (bf16[32,8,128]{2,1,0:T(8,128)(2,1)S(1)}, bf16[32,8,128]{2,1,0:T(8,128)(2,1)S(1)}, u32[]{:S(2)}, u32[]{:S(2)}) collective-permute-start(bf16[32,8,128]{2,1,0:T(8,128)(2,1)S(1)} %get-tuple-element.62), channel_id=1, source_target_pairs={{0,1},{1,0},{2,3},{3,2},{4,5},{5,4},{6,7},{7,6},{8,9},{9,8},{10,11... | collective-permute-start | bytes 196616 | tf_op jit(solution)/shard_map/ppermute | solution.py:376
  75.1 5.4 %collective-permute-start.16 = (bf16[32,8,128]{2,1,0:T(8,128)(2,1)S(1)}, bf16[32,8,128]{2,1,0:T(8,128)(2,1)S(1)}, u32[]{:S(2)}, u32[]{:S(2)}) collective-permute-start(bf16[32,8,128]{2,1,0:T(8,128)(2,1)S(1)} %shard_map.89), channel_id=1, source_target_pairs={{0,64},{64,128},{128,192},{192,0},{1,65},{65,129},{129,193},{193,1... | collective-permute-start | bytes 196616 | tf_op jit(solution)/shard_map/ppermute | solution.py:296
  76.7 6.5 %collective-permute-start.18 = (bf16[32,8,128]{2,1,0:T(8,128)(2,1)S(1)}, bf16[32,8,128]{2,1,0:T(8,128)(2,1)S(1)}, u32[]{:S(2)}, u32[]{:S(2)}) collective-permute-start(bf16[32,8,128]{2,1,0:T(8,128)(2,1)S(1)} %shard_map.90), channel_id=1, source_target_pairs={{0,128},{64,192},{128,0},{192,64},{1,129},{65,193},{129,1},{193,65... | collective-permute-start | bytes 196616 | tf_op jit(solution)/shard_map/ppermute | solution.py:296
  77.1 6.4 %collective-permute-start.20 = (bf16[32,8,128]{2,1,0:T(8,128)(2,1)S(1)}, bf16[32,8,128]{2,1,0:T(8,128)(2,1)S(1)}, u32[]{:S(2)}, u32[]{:S(2)}) collective-permute-start(bf16[32,8,128]{2,1,0:T(8,128)(2,1)S(1)} %shard_map.91), channel_id=1, source_target_pairs={{0,192},{64,0},{128,64},{192,128},{1,193},{65,1},{129,65},{193,129... | collective-permute-start | bytes 196616 | tf_op jit(solution)/shard_map/ppermute | solution.py:296

commit v8 on v7

--- a/solution.py
+++ b/solution.py
@@ -43,8 +43,16 @@
     return high, (value - high).astype(BF).astype(F32)
 
 
-def stats(lane, first, second, third):
-    return jnp.where(lane == 0, first, jnp.where(lane == 1, second, jnp.where(lane == 2, third, 0.0)))
+def split3(value):
+    high = value.astype(BF).astype(F32)
+    return (high,) + split(value - high)
+
+
+def stats(lane, *values):
+    tile = jnp.zeros(lane.shape, F32)
+    for i, value in enumerate(values):
+        tile = jnp.where(lane == i, value, tile)
+    return tile
 
 
 def softmax_rows(logits):
@@ -80,12 +88,12 @@
         comb_ref[rows, :] = softmax_rows(piece).astype(BF)
         high = jnp.max(piece, axis=0, keepdims=True)
         peak = high if peak is None else jnp.maximum(peak, high)
-    refpoint = peak.astype(BF).astype(F32)
+    refpoint = peak
     dexp = jnp.exp(logit_ref[...] - refpoint).astype(BF)
     numer = dot(dexp, tok_ref[...], ((0,), (0,))).reshape(n // 8, 8, width)
     total = dot(dexp, jnp.ones((count, STAT), BF), ((0,), (0,)))
-    diag = jnp.where(iota((n, n), 0) == iota((n, n), 1), refpoint, 0.0).astype(BF)
-    point = dot(diag, jnp.ones((n, STAT), BF))
+    same, ones = iota((n, n), 0) == iota((n, n), 1), jnp.ones((n, STAT), BF)
+    point, middle, last = [dot(jnp.where(same, v, 0.0).astype(BF), ones) for v in split3(refpoint)]
     high, low = split(total)
     copies[1 + PARTS].wait()
     dslot = dot(comb_ref[...], cot_ref[...], ((0,), (0,))).reshape(n // 8, 8, width)
@@ -93,7 +101,7 @@
     zero = core == 0
     even = jnp.where(upper, numer, swap_halves(dslot)).astype(BF)
     odd = jnp.where(upper, swap_halves(numer), dslot).astype(BF)
-    sides = [value.reshape(n // 8, 8, STAT) for value in (point, high, low)]
+    sides = [value.reshape(n // 8, 8, STAT) for value in (point, high, low, middle, last)]
     even_sides = [jnp.where(upper, value, 0.0) for value in sides]
     odd_sides = [jnp.where(upper, swap_halves(value), 0.0) for value in sides]
     columns = all_ref.shape[1]
@@ -124,10 +132,11 @@
     count = parts[0].shape[0] - 1
     groups = 8
     marks = [p[count].astype(F32) for p in parts]
-    top = marks[0]
-    for mark in marks[1:]:
-        top = jnp.maximum(top, mark)
-    scales = [jnp.exp(mark - top) for mark in marks]
+    points = [mark + pltpu.roll(mark, STAT - 3 * groups, 1) + pltpu.roll(mark, STAT - 4 * groups, 1) for mark in marks]
+    top = points[0]
+    for point in points[1:]:
+        top = jnp.maximum(top, point)
+    scales = [jnp.exp(point - top) for point in points]
     total = 0.0
     for scale, mark in zip(scales, marks):
         total += scale * (pltpu.roll(mark, STAT - groups, 1) + pltpu.roll(mark, STAT - 2 * groups, 1))
@@ -148,8 +157,11 @@
     for z, body in enumerate(bodies):
         out_ref[z * size:(z + 1) * size] = body
     lane = iota(top.shape, 1)
-    mark = jnp.where(lane < 16, pltpu.roll(high, 8, 1), jnp.where(lane < 24, pltpu.roll(low, 16, 1), 0.0))
-    out_ref[len(bodies) * size] = jnp.where(lane < 8, top, mark).astype(BF)
+    point, middle, last = split3(top)
+    tile = jnp.zeros(top.shape, F32)
+    for i, mark in enumerate((point, high, low, middle, last)):
+        tile = jnp.where(lane // 8 == i, pltpu.roll(mark, 8 * i, 1) if i else mark, tile)
+    out_ref[len(bodies) * size] = tile.astype(BF)
 
 
 def merge_columns(a_ref, b_ref, c_ref, d_ref, after_ref, out_ref):
@@ -159,18 +171,20 @@
     lane = iota(top.shape, 1)
     for z, body in enumerate(bodies):
         out_ref[z, :size] = body
-        out_ref[z, size] = stats(lane, top[:, z:z + 1], high[:, z:z + 1], low[:, z:z + 1]).astype(BF)
+        point, middle, last = split3(top[:, z:z + 1])
+        out_ref[z, size] = stats(lane, point, high[:, z:z + 1], low[:, z:z + 1], middle, last).astype(BF)
 
 
 def merge_shards(in_ref, pay_ref, full_ref, side_ref):
     size = in_ref.shape[1] - 1
     marks = [in_ref[i, size].astype(F32) for i in range(in_ref.shape[0])]
-    top = marks[0][:, 0:1]
-    for mark in marks[1:]:
-        top = jnp.maximum(top, mark[:, 0:1])
+    points = [mark[:, 0:1] + mark[:, 3:4] + mark[:, 4:5] for mark in marks]
+    top = points[0]
+    for point in points[1:]:
+        top = jnp.maximum(top, point)
     acc, total = 0.0, 0.0
     for i, mark in enumerate(marks):
-        scale = jnp.exp(mark[:, 0:1] - top)
+        scale = jnp.exp(points[i] - top)
         acc += scale[None] * in_ref[i, :size].astype(F32)
         total += scale * (mark[:, 1:2] + mark[:, 2:3])
     slots = total.shape[0] // 2
@@ -225,7 +239,8 @@
     shift = jnp.sum(full_ref[:slots, :] * wide[slots:, :], axis=1, keepdims=True)
     shift = jnp.concatenate([shift, shift], axis=0)
     high, low = split(shift)
-    st = stats(iota((2 * slots, STAT), 1), side[:, 0:1], high, low)
+    point, middle, last = split3(side[:, 0:1])
+    st = stats(iota((2 * slots, STAT), 1), point, high, low, middle, last)
     block = jnp.concatenate([wide[:slots], pltpu.roll(wide, slots, 0)[:slots], st[:slots]], axis=1).astype(BF)
     out_ref[...] = jnp.broadcast_to(block[None], out_ref.shape)
 
@@ -245,7 +260,7 @@
     so_ref[...] = slot_out
     sc_ref[...] = scaled
     side = both[:, 2 * width:].T
-    point, shift = side[0:1, :], side[1:2, :] + side[2:3, :]
+    point, shift = side[0:1, :] + side[3:4, :] + side[4:5, :], side[1:2, :] + side[2:3, :]
     comb = softmax_rows(logits)
     comb_ref[...] = comb.astype(BF)
     dexp = jnp.exp(logits - point).astype(BF)

time: 98.3 us -> 98.8 us (level)
  transfers between devices with their start and end apart: 21 -> 21, of which waited for: 11 -> 10; matrix products, arithmetic and copies ran while one was open for 0% -> 0% of each run, Pallas kernels for 5% -> 5%
where the time goes in v8:
time: 98.8 us; the launch traced here: 98.6 us
  blocking collectives  50.1 us (51%)
  starting transfers between devices  20.3 us (21%)
  Pallas kernels  14.5 us (15%)
  waiting for transfers between devices  11.1 us (11%)
  local copies, waits for them, and re-layouts  1.86 us (2%)
    all_to_all x1, blocking collectives, on_device(): mine = lax.all_to_all(block, ZY, 0, 0, tiled=True)  18.6 us
    ppermute x12, starting transfers between devices, shifted(): lax.ppermute(value, axis, [(i, (i + step) % size) for i in range(size)])  18.1 us
    all_to_all x1, blocking collectives, on_device(): shards = lax.all_to_all(merged, 'z', 0, 0, tiled=True)  17.5 us
    all_to_all x1, blocking collectives, on_device(): pieces = lax.all_to_all(half, ZY, 0, 0, tiled=True)  13.9 us
    ppermute x12, waiting for transfers between devices, shifted(): lax.ppermute(value, axis, [(i, (i + step) % size) for i in range(size)])  8.54 us
    pallas_call x14, Pallas kernels, call(): pl.pallas_call(body, out_shape=outs, in_specs=[pl.BlockSpec(memory_space=...  7.99 us
    pallas_call x1, Pallas kernels, on_device(): pl.pallas_call(reduce_tokens, out_shape=[shape(tiles, BF)] * (2 * rows_y)...  3.8 us
    pallas_call x1, Pallas kernels, on_device(): pl.pallas_call(turn_weights, out_shape=[shape(w_in.shape, BF), shape(w_ou...  2.4 us
  transfers between devices with their start and end apart: 21, of which 10 were waited for; matrix products, arithmetic and copies ran while one was open for 0% of the time, Pallas kernels for 5%

profile of v8, /device:TPU:6, one launch (start us, length us, event | category | flops | bytes accessed | tf_op | source)
XLA Modules:
  0.0 98.6 jit_solution(4918325006581098643)
XLA Ops:
  0.6 3.8 %shard_map.76 = (bf16[65,8,128]{2,1,0:T(8,128)(2,1)S(1)}, bf16[65,8,128]{2,1,0:T(8,128)(2,1)S(1)}, bf16[65,8,128]{2,1,0:T(8,128)(2,1)S(1)}, bf16[65,8,128]{2,1,0...) custom-call(bf16[512,1024]{1,0:T(8,128)(2,1)} %bitcast.4, ...), custom_call_target="tpu_custom_call" | custom-call | flops 1073741824 | bytes 4194304 | tf_op jit(solution)/shard_map/pallas_call | solution.py:328
  4.4 0.1 collective-permute-start.1
  4.5 0.5 collective-permute-start
  5.0 0.1 collective-permute-start.3
  5.1 0.4 collective-permute-start.5
  5.5 0.3 collective-permute-done.1.b_ref
  5.9 0.2 shard_map.78
  6.1 1.7 %collective-permute-start.2 = (bf16[65,8,128]{2,1,0:T(8,128)(2,1)S(1)}, bf16[65,8,128]{2,1,0:T(8,128)(2,1)S(1)}, u32[]{:S(2)}, u32[]{:S(2)}) collective-permute-start(bf16[65,8,128]{2,1,0:T(8,128)(2,1)S(1)} %shard_map.78), channel_id=1, source_target_pairs={{0,2},{2,4},{4,6},{6,0},{1,3},{3,5},{5,7},{7,1},{8,10},{10,12},{12... | collective-permute-start | bytes 399368 | tf_op jit(solution)/shard_map/ppermute | solution.py:311
  7.7 0.0 collective-permute-done.3.b_ref
  7.8 0.2 shard_map.79
  8.0 3.0 %collective-permute-start.4 = (bf16[65,8,128]{2,1,0:T(8,128)(2,1)S(1)}, bf16[65,8,128]{2,1,0:T(8,128)(2,1)S(1)}, u32[]{:S(2)}, u32[]{:S(2)}) collective-permute-start(bf16[65,8,128]{2,1,0:T(8,128)(2,1)S(1)} %shard_map.79), channel_id=1, source_target_pairs={{0,4},{2,6},{4,0},{6,2},{1,5},{3,7},{5,1},{7,3},{8,12},{10,14},{12... | collective-permute-start | bytes 399368 | tf_op jit(solution)/shard_map/ppermute | solution.py:311
  11.0 0.0 collective-permute-done.5.b_ref
  11.0 0.0 copy-start
  11.0 0.2 shard_map.80.after_ref
  11.2 1.4 %collective-permute-start.6 = (bf16[65,8,128]{2,1,0:T(8,128)(2,1)S(1)}, bf16[65,8,128]{2,1,0:T(8,128)(2,1)S(1)}, u32[]{:S(2)}, u32[]{:S(2)}) collective-permute-start(bf16[65,8,128]{2,1,0:T(8,128)(2,1)S(1)} %shard_map.80.after_ref), channel_id=1, source_target_pairs={{0,6},{2,0},{4,2},{6,4},{1,7},{3,1},{5,3},{7,5},{8,14},{10,8},{12,... | collective-permute-start | bytes 399368 | tf_op jit(solution)/shard_map/ppermute | solution.py:311
  12.6 0.6 copy-done
  13.2 1.3 %copy-done.1 = bf16[2,1024,1024]{2,1,0:T(8,128)(2,1)S(1)} copy-done((bf16[2,1024,1024]{2,1,0:T(8,128)(2,1)S(1)}, bf16[2,1024,1024]{2,1,0:T(8,128)(2,1)}, u32[]{:S(2)}) %copy-start.1) | copy-done | bytes 4194328
  14.4 2.4 %shard_map.81 = (bf16[2,1024,1024]{2,1,0:T(8,128)(2,1)S(1)}, bf16[2,1024,1024]{2,1,0:T(8,128)(2,1)S(1)}) custom-call(bf16[2,1024,1024]{2,1,0:T(8,128)(2,1)S(1)} %copy-done, bf16[2,1024,1024]{2,1,0:T(8,128)(2,1)S(1)} %copy-done.1, bf16[65,8,128]{2,1,0:T(8,128)(2,1)S(1)} %shard_map.80.after_ref), custom_call_target="tpu_custom_call" | custom-call | flops 5368709120 | bytes 16777216 | tf_op jit(solution)/shard_map/pallas_call | solution.py:350
  16.8 0.0 collective-permute-done.b_ref
  16.9 0.2 shard_map.77.a_ref
  17.1 0.0 collective-permute-done.2.b_ref
  17.1 0.0 collective-permute-done.4.c_ref
  17.1 0.0 collective-permute-done.6.d_ref
  17.1 0.3 shard_map.82
  17.4 17.5 %all_to_all.15.in_ref = bf16[8,9,8,128]{3,2,1,0:T(8,128)(2,1)S(1)} all-to-all(bf16[8,9,8,128]{3,2,1,0:T(8,128)(2,1)S(1)} %shard_map.82), channel_id=1, replica_groups=mesh['x'=4,'z'=8,'y'=4,'c'=2] {'z'}, dimensions={0} | all-to-all | bytes 294912 | tf_op jit(solution)/shard_map/all_to_all | solution.py:365
  34.9 0.2 shard_map.83
  35.1 0.9 collective-permute-start.9
  36.0 1.1 %collective-permute-start.8 = (bf16[8,1024]{1,0:T(8,128)(2,1)S(1)}, bf16[8,1024]{1,0:T(8,128)(2,1)S(1)}, u32[]{:S(2)}, u32[]{:S(2)}) collective-permute-start(bf16[8,1024]{1,0:T(8,128)(2,1)S(1)} %get-tuple-element.46.own_ref), channel_id=1, source_target_pairs={{0,128},{64,192},{128,0},{192,64},{1,129},{65,193},{129,1},{193,65... | collective-permute-start | bytes 49160 | tf_op jit(solution)/shard_map/ppermute | solution.py:311
  37.1 2.1 %collective-permute-start.7 = (bf16[8,1024]{1,0:T(8,128)(2,1)S(1)}, bf16[8,1024]{1,0:T(8,128)(2,1)S(1)}, u32[]{:S(2)}, u32[]{:S(2)}) collective-permute-start(bf16[8,1024]{1,0:T(8,128)(2,1)S(1)} %get-tuple-element.46.own_ref), channel_id=1, source_target_pairs={{0,64},{64,128},{128,192},{192,0},{1,65},{65,129},{129,193},{193,1... | collective-permute-start | bytes 49160 | tf_op jit(solution)/shard_map/ppermute | solution.py:311
  39.2 0.9 collective-permute-done.9.c_ref
  40.1 1.1 %collective-permute-done.8.b_ref = bf16[8,1024]{1,0:T(8,128)(2,1)S(1)} collective-permute-done((bf16[8,1024]{1,0:T(8,128)(2,1)S(1)}, bf16[8,1024]{1,0:T(8,128)(2,1)S(1)}, u32[]{:S(2)}, u32[]{:S(2)}) %collective-permute-start.8) | collective-permute-done | bytes 16416 | tf_op jit(solution)/shard_map/ppermute | solution.py:311
  41.3 0.0 collective-permute-done.7.a_ref
  41.3 2.3 %shard_map.84 = (bf16[8,1024]{1,0:T(8,128)(2,1)S(1)}, bf16[8,1024]{1,0:T(8,128)(2,1)S(1)}, bf16[8,1024]{1,0:T(8,128)(2,1)S(1)}, bf16[8,1024]{1,0:T(8,128)(2,1)S(1)}) custom-call(bf16[8,1024]{1,0:T(8,128)(2,1)S(1)} %get-tuple-element.46.own_ref, bf16[8,1024]{1,0:T(8,128)(2,1)S(1)} %collective-permute-done.7.a_ref, ...), custom_call_target="tpu_custom_call" | custom-call | flops 268435456 | bytes 16973824 | tf_op jit(solution)/shard_map/pallas_call | solution.py:30
  43.6 1.8 %collective-permute-start.10 = (bf16[8,1024]{1,0:T(8,128)(2,1)S(1)}, bf16[8,1024]{1,0:T(8,128)(2,1)S(1)}, u32[]{:S(2)}, u32[]{:S(2)}) collective-permute-start(bf16[8,1024]{1,0:T(8,128)(2,1)S(1)} %get-tuple-element.49), channel_id=1, source_target_pairs={{0,192},{64,0},{128,64},{192,128},{1,193},{65,1},{129,65},{193,129... | collective-permute-start | bytes 49160 | tf_op jit(solution)/shard_map/ppermute | solution.py:311
  45.4 2.6 %collective-permute-start.11 = (bf16[8,1024]{1,0:T(8,128)(2,1)S(1)}, bf16[8,1024]{1,0:T(8,128)(2,1)S(1)}, u32[]{:S(2)}, u32[]{:S(2)}) collective-permute-start(bf16[8,1024]{1,0:T(8,128)(2,1)S(1)} %get-tuple-element.50), channel_id=1, source_target_pairs={{0,128},{64,192},{128,0},{192,64},{1,129},{65,193},{129,1},{193,65... | collective-permute-start | bytes 49160 | tf_op jit(solution)/shard_map/ppermute | solution.py:311
  48.0 0.3 collective-permute-start.12
  48.3 0.3 collective-permute-done.10.a_ref
  48.6 2.0 %collective-permute-done.11.b_ref = bf16[8,1024]{1,0:T(8,128)(2,1)S(1)} collective-permute-done((bf16[8,1024]{1,0:T(8,128)(2,1)S(1)}, bf16[8,1024]{1,0:T(8,128)(2,1)S(1)}, u32[]{:S(2)}, u32[]{:S(2)}) %collective-permute-start.11) | collective-permute-done | bytes 16416 | tf_op jit(solution)/shard_map/ppermute | solution.py:311
  50.7 1.1 %collective-permute-done.12.c_ref = bf16[8,1024]{1,0:T(8,128)(2,1)S(1)} collective-permute-done((bf16[8,1024]{1,0:T(8,128)(2,1)S(1)}, bf16[8,1024]{1,0:T(8,128)(2,1)S(1)}, u32[]{:S(2)}, u32[]{:S(2)}) %collective-permute-start.12) | collective-permute-done | bytes 16416 | tf_op jit(solution)/shard_map/ppermute | solution.py:311
  51.8 0.3 shard_map.85
  52.1 18.6 %all_to_all.16.own_ref = bf16[32,4,2176]{2,1,0:T(4,128)(2,1)S(1)} all-to-all(bf16[32,4,2176]{2,1,0:T(4,128)(2,1)S(1)} %shard_map.85), channel_id=1, replica_groups=mesh['x'=4,'z'=8,'y'=4,'c'=2] {'z','y'}, dimensions={0} | all-to-all | bytes 1114112 | tf_op jit(solution)/shard_map/all_to_all | solution.py:378
  70.7 0.0 collective-permute-start.13
  70.7 2.0 %collective-permute-done.13.oth_ref = bf16[32,4,2176]{2,1,0:T(4,128)(2,1)S(1)} collective-permute-done((bf16[32,4,2176]{2,1,0:T(4,128)(2,1)S(1)}, bf16[32,4,2176]{2,1,0:T(4,128)(2,1)S(1)}, u32[]{:S(2)}, u32[]{:S(2)}) %collective-permute-start.13) | collective-permute-done | bytes 557088 | tf_op jit(solution)/shard_map/ppermute | solution.py:379
  72.6 0.0 copy-done.2
  72.6 0.0 copy-done.3
  72.6 1.5 %shard_map.86 = (bf16[32,8,128]{2,1,0:T(8,128)(2,1)S(1)}, bf16[32,8,128]{2,1,0:T(8,128)(2,1)S(1)}, bf16[32,8,128]{2,1,0:T(8,128)(2,1)S(1)}, bf16[32,8,128]{2,1,0...) custom-call(f32[512,256]{1,0:T(8,128)S(1)} %get-tuple-element.36.log, ...), custom_call_target="tpu_custom_call" | custom-call | flops 1342177280 | bytes 8454144 | tf_op jit(solution)/shard_map/pallas_call | solution.py:30
  74.2 0.2 collective-permute-start.15
  74.4 0.4 collective-permute-start.17
  74.8 0.1 collective-permute-start.19
  74.9 0.4 collective-permute-start.14
  75.3 0.2 collective-permute-done.15.b_ref
  75.5 1.5 %collective-permute-start.16 = (bf16[32,8,128]{2,1,0:T(8,128)(2,1)S(1)}, bf16[32,8,128]{2,1,0:T(8,128)(2,1)S(1)}, u32[]{:S(2)}, u32[]{:S(2)}) collective-permute-start(bf16[32,8,128]{2,1,0:T(8,128)(2,1)S(1)} %shard_map.89), channel_id=1, source_target_pairs={{0,64},{64,128},{128,192},{192,0},{1,65},{65,129},{129,193},{193,1... | collective-permute-start | bytes 196616 | tf_op jit(solution)/shard_map/ppermute | solution.py:311
  77.1 0.0 collective-permute-done.17.b_ref
  77.1 0.4 collective-permute-start.18
  77.5 0.0 collective-permute-done.19.b_ref
  77.6 1.2 %collective-permute-start.20 = (bf16[32,8,128]{2,1,0:T(8,128)(2,1)S(1)}, bf16[32,8,128]{2,1,0:T(8,128)(2,1)S(1)}, u32[]{:S(2)}, u32[]{:S(2)}) collective-permute-start(bf16[32,8,128]{2,1,0:T(8,128)(2,1)S(1)} %shard_map.91), channel_id=1, source_target_pairs={{0,192},{64,0},{128,64},{192,128},{1,193},{65,1},{129,65},{193,129... | collective-permute-start | bytes 196616 | tf_op jit(solution)/shard_map/ppermute | solution.py:311
  78.8 0.0 copy-done.4
  78.8 2.2 %shard_map.87 = (bf16[512,1024]{1,0:T(8,128)(2,1)}, bf16[512,1024]{1,0:T(8,128)(2,1)}) custom-call(bf16[512,256]{1,0:T(8,128)(2,1)S(1)} %get-tuple-element.54.comb_ref, bf16[256,1024]{1,0:T(8,128)(2,1)S(1)} %get-tuple-element.55.so_ref, bf16[512,256]{1,0:T(8,128)(2,1)S(1)} %get-tuple-element.56.dlog_ref, bf16[1024,256]{1,0:T(8,128)(2,1)S(1)} %copy-done.4, ...), custom_call_target="tpu_custom_call" | custom-call | flops 805306368 | bytes 6553600 | tf_op jit(solution)/shard_map/pallas_call | solution.py:30
  80.9 0.0 collective-permute-done.14.b_ref
  81.0 0.0 collective-permute-done.16.a_ref
  81.0 2.6 %collective-permute-done.18.b_ref = bf16[32,8,128]{2,1,0:T(8,128)(2,1)S(1)} collective-permute-done((bf16[32,8,128]{2,1,0:T(8,128)(2,1)S(1)}, bf16[32,8,128]{2,1,0:T(8,128)(2,1)S(1)}, u32[]{:S(2)}, u32[]{:S(2)}) %collective-permute-start.18) | collective-permute-done | bytes 65568 | tf_op jit(solution)/shard_map/ppermute | solution.py:311
  83.6 0.4 collective-permute-done.20.c_ref
  84.0 13.9 %all_to_all.17.in_ref = bf16[32,8,128]{2,1,0:T(8,128)(2,1)S(1)} all-to-all(bf16[32,8,128]{2,1,0:T(8,128)(2,1)S(1)} %shard_map.92), channel_id=1, replica_groups=mesh['x'=4,'z'=8,'y'=4,'c'=2] {'z','y'}, dimensions={0} | all-to-all | bytes 131072 | tf_op jit(solution)/shard_map/all_to_all | solution.py:408
  98.0 0.6 shard_map.93
  (9 shorter events, 0.1 us)
Async XLA Ops:
  4.4 1.4 %collective-permute-start.1 = (bf16[65,8,128]{2,1,0:T(8,128)(2,1)S(1)}, bf16[65,8,128]{2,1,0:T(8,128)(2,1)S(1)}, u32[]{:S(2)}, u32[]{:S(2)}) collective-permute-start(bf16[65,8,128]{2,1,0:T(8,128)(2,1)S(1)} %get-tuple-element.40), channel_id=1, source_target_pairs={{0,1},{1,0},{2,3},{3,2},{4,5},{5,4},{6,7},{7,6},{8,9},{9,8},{10,11... | collective-permute-start | bytes 399368 | tf_op jit(solution)/shard_map/ppermute | solution.py:343
  4.5 12.3 %collective-permute-start = (bf16[65,8,128]{2,1,0:T(8,128)(2,1)S(1)}, bf16[65,8,128]{2,1,0:T(8,128)(2,1)S(1)}, u32[]{:S(2)}, u32[]{:S(2)}) collective-permute-start(bf16[65,8,128]{2,1,0:T(8,128)(2,1)S(1)} %get-tuple-element.38), channel_id=1, source_target_pairs={{0,1},{1,0},{2,3},{3,2},{4,5},{5,4},{6,7},{7,6},{8,9},{9,8},{10,11... | collective-permute-start | bytes 399368 | tf_op jit(solution)/shard_map/ppermute | solution.py:343
  5.0 2.7 %collective-permute-start.3 = (bf16[65,8,128]{2,1,0:T(8,128)(2,1)S(1)}, bf16[65,8,128]{2,1,0:T(8,128)(2,1)S(1)}, u32[]{:S(2)}, u32[]{:S(2)}) collective-permute-start(bf16[65,8,128]{2,1,0:T(8,128)(2,1)S(1)} %get-tuple-element.42), channel_id=1, source_target_pairs={{0,1},{1,0},{2,3},{3,2},{4,5},{5,4},{6,7},{7,6},{8,9},{9,8},{10,11... | collective-permute-start | bytes 399368 | tf_op jit(solution)/shard_map/ppermute | solution.py:343
  5.1 5.8 %collective-permute-start.5 = (bf16[65,8,128]{2,1,0:T(8,128)(2,1)S(1)}, bf16[65,8,128]{2,1,0:T(8,128)(2,1)S(1)}, u32[]{:S(2)}, u32[]{:S(2)}) collective-permute-start(bf16[65,8,128]{2,1,0:T(8,128)(2,1)S(1)} %get-tuple-element.44), channel_id=1, source_target_pairs={{0,1},{1,0},{2,3},{3,2},{4,5},{5,4},{6,7},{7,6},{8,9},{9,8},{10,11... | collective-permute-start | bytes 399368 | tf_op jit(solution)/shard_map/ppermute | solution.py:343
  6.1 11.0 %collective-permute-start.2 = (bf16[65,8,128]{2,1,0:T(8,128)(2,1)S(1)}, bf16[65,8,128]{2,1,0:T(8,128)(2,1)S(1)}, u32[]{:S(2)}, u32[]{:S(2)}) collective-permute-start(bf16[65,8,128]{2,1,0:T(8,128)(2,1)S(1)} %shard_map.78), channel_id=1, source_target_pairs={{0,2},{2,4},{4,6},{6,0},{1,3},{3,5},{5,7},{7,1},{8,10},{10,12},{12... | collective-permute-start | bytes 399368 | tf_op jit(solution)/shard_map/ppermute | solution.py:311
  8.0 9.1 %collective-permute-start.4 = (bf16[65,8,128]{2,1,0:T(8,128)(2,1)S(1)}, bf16[65,8,128]{2,1,0:T(8,128)(2,1)S(1)}, u32[]{:S(2)}, u32[]{:S(2)}) collective-permute-start(bf16[65,8,128]{2,1,0:T(8,128)(2,1)S(1)} %shard_map.79), channel_id=1, source_target_pairs={{0,4},{2,6},{4,0},{6,2},{1,5},{3,7},{5,1},{7,3},{8,12},{10,14},{12... | collective-permute-start | bytes 399368 | tf_op jit(solution)/shard_map/ppermute | solution.py:311
  11.0 2.2 %copy-start = (bf16[2,1024,1024]{2,1,0:T(8,128)(2,1)S(1)}, bf16[2,1024,1024]{2,1,0:T(8,128)(2,1)}, u32[]{:S(2)}) copy-start(bf16[2,1024,1024]{2,1,0:T(8,128)(2,1)} %win_ref.3) | copy-start | bytes 12582916
  11.0 3.5 %copy-start.1 = (bf16[2,1024,1024]{2,1,0:T(8,128)(2,1)S(1)}, bf16[2,1024,1024]{2,1,0:T(8,128)(2,1)}, u32[]{:S(2)}) copy-start(bf16[2,1024,1024]{2,1,0:T(8,128)(2,1)} %wout_ref.3) | copy-start | bytes 12582916
  11.2 5.9 %collective-permute-start.6 = (bf16[65,8,128]{2,1,0:T(8,128)(2,1)S(1)}, bf16[65,8,128]{2,1,0:T(8,128)(2,1)S(1)}, u32[]{:S(2)}, u32[]{:S(2)}) collective-permute-start(bf16[65,8,128]{2,1,0:T(8,128)(2,1)S(1)} %shard_map.80.after_ref), channel_id=1, source_target_pairs={{0,6},{2,0},{4,2},{6,4},{1,7},{3,1},{5,3},{7,5},{8,14},{10,8},{12,... | collective-permute-start | bytes 399368 | tf_op jit(solution)/shard_map/ppermute | solution.py:311
  35.1 5.0 %collective-permute-start.9 = (bf16[8,1024]{1,0:T(8,128)(2,1)S(1)}, bf16[8,1024]{1,0:T(8,128)(2,1)S(1)}, u32[]{:S(2)}, u32[]{:S(2)}) collective-permute-start(bf16[8,1024]{1,0:T(8,128)(2,1)S(1)} %get-tuple-element.46.own_ref), channel_id=1, source_target_pairs={{0,192},{64,0},{128,64},{192,128},{1,193},{65,1},{129,65},{193,129... | collective-permute-start | bytes 49160 | tf_op jit(solution)/shard_map/ppermute | solution.py:311
  36.0 5.2 %collective-permute-start.8 = (bf16[8,1024]{1,0:T(8,128)(2,1)S(1)}, bf16[8,1024]{1,0:T(8,128)(2,1)S(1)}, u32[]{:S(2)}, u32[]{:S(2)}) collective-permute-start(bf16[8,1024]{1,0:T(8,128)(2,1)S(1)} %get-tuple-element.46.own_ref), channel_id=1, source_target_pairs={{0,128},{64,192},{128,0},{192,64},{1,129},{65,193},{129,1},{193,65... | collective-permute-start | bytes 49160 | tf_op jit(solution)/shard_map/ppermute | solution.py:311
  37.1 4.1 %collective-permute-start.7 = (bf16[8,1024]{1,0:T(8,128)(2,1)S(1)}, bf16[8,1024]{1,0:T(8,128)(2,1)S(1)}, u32[]{:S(2)}, u32[]{:S(2)}) collective-permute-start(bf16[8,1024]{1,0:T(8,128)(2,1)S(1)} %get-tuple-element.46.own_ref), channel_id=1, source_target_pairs={{0,64},{64,128},{128,192},{192,0},{1,65},{65,129},{129,193},{193,1... | collective-permute-start | bytes 49160 | tf_op jit(solution)/shard_map/ppermute | solution.py:311
  41.3 31.4 %copy-start.2 = (bf16[1,512,1024]{2,1,0:T(8,128)(2,1)S(1)}, bf16[1,512,1024]{2,1,0:T(8,128)(2,1)}, u32[]{:S(2)}) copy-start(bf16[1,512,1024]{2,1,0:T(8,128)(2,1)} %param.5) | copy-start | bytes 3145732
  41.3 31.4 %copy-start.3 = (bf16[1,512,1024]{2,1,0:T(8,128)(2,1)S(1)}, bf16[1,512,1024]{2,1,0:T(8,128)(2,1)}, u32[]{:S(2)}) copy-start(bf16[1,512,1024]{2,1,0:T(8,128)(2,1)} %param.9) | copy-start | bytes 3145732
  43.6 35.2 %copy-start.4 = (bf16[1024,256]{1,0:T(8,128)(2,1)S(1)}, bf16[1024,256]{1,0:T(8,128)(2,1)}, u32[]{:S(2)}) copy-start(bf16[1024,256]{1,0:T(8,128)(2,1)} %par_ref.1) | copy-start | bytes 1572868
  43.6 5.0 %collective-permute-start.10 = (bf16[8,1024]{1,0:T(8,128)(2,1)S(1)}, bf16[8,1024]{1,0:T(8,128)(2,1)S(1)}, u32[]{:S(2)}, u32[]{:S(2)}) collective-permute-start(bf16[8,1024]{1,0:T(8,128)(2,1)S(1)} %get-tuple-element.49), channel_id=1, source_target_pairs={{0,192},{64,0},{128,64},{192,128},{1,193},{65,1},{129,65},{193,129... | collective-permute-start | bytes 49160 | tf_op jit(solution)/shard_map/ppermute | solution.py:311
  45.4 5.2 %collective-permute-start.11 = (bf16[8,1024]{1,0:T(8,128)(2,1)S(1)}, bf16[8,1024]{1,0:T(8,128)(2,1)S(1)}, u32[]{:S(2)}, u32[]{:S(2)}) collective-permute-start(bf16[8,1024]{1,0:T(8,128)(2,1)S(1)} %get-tuple-element.50), channel_id=1, source_target_pairs={{0,128},{64,192},{128,0},{192,64},{1,129},{65,193},{129,1},{193,65... | collective-permute-start | bytes 49160 | tf_op jit(solution)/shard_map/ppermute | solution.py:311
  48.0 3.7 %collective-permute-start.12 = (bf16[8,1024]{1,0:T(8,128)(2,1)S(1)}, bf16[8,1024]{1,0:T(8,128)(2,1)S(1)}, u32[]{:S(2)}, u32[]{:S(2)}) collective-permute-start(bf16[8,1024]{1,0:T(8,128)(2,1)S(1)} %get-tuple-element.51), channel_id=1, source_target_pairs={{0,64},{64,128},{128,192},{192,0},{1,65},{65,129},{129,193},{193,1... | collective-permute-start | bytes 49160 | tf_op jit(solution)/shard_map/ppermute | solution.py:311
  70.7 2.0 %collective-permute-start.13 = (bf16[32,4,2176]{2,1,0:T(4,128)(2,1)S(1)}, bf16[32,4,2176]{2,1,0:T(4,128)(2,1)S(1)}, u32[]{:S(2)}, u32[]{:S(2)}) collective-permute-start(bf16[32,4,2176]{2,1,0:T(4,128)(2,1)S(1)} %all_to_all.16.own_ref), channel_id=1, source_target_pairs={{0,1},{1,0},{2,3},{3,2},{4,5},{5,4},{6,7},{7,6},{8,9},{9,8},{10,11... | collective-permute-start | bytes 1671176 | tf_op jit(solution)/shard_map/ppermute | solution.py:379
  74.2 1.3 %collective-permute-start.15 = (bf16[32,8,128]{2,1,0:T(8,128)(2,1)S(1)}, bf16[32,8,128]{2,1,0:T(8,128)(2,1)S(1)}, u32[]{:S(2)}, u32[]{:S(2)}) collective-permute-start(bf16[32,8,128]{2,1,0:T(8,128)(2,1)S(1)} %get-tuple-element.64), channel_id=1, source_target_pairs={{0,1},{1,0},{2,3},{3,2},{4,5},{5,4},{6,7},{7,6},{8,9},{9,8},{10,11... | collective-permute-start | bytes 196616 | tf_op jit(solution)/shard_map/ppermute | solution.py:391
  74.4 2.7 %collective-permute-start.17 = (bf16[32,8,128]{2,1,0:T(8,128)(2,1)S(1)}, bf16[32,8,128]{2,1,0:T(8,128)(2,1)S(1)}, u32[]{:S(2)}, u32[]{:S(2)}) collective-permute-start(bf16[32,8,128]{2,1,0:T(8,128)(2,1)S(1)} %get-tuple-element.66), channel_id=1, source_target_pairs={{0,1},{1,0},{2,3},{3,2},{4,5},{5,4},{6,7},{7,6},{8,9},{9,8},{10,11... | collective-permute-start | bytes 196616 | tf_op jit(solution)/shard_map/ppermute | solution.py:391
  74.8 2.8 %collective-permute-start.19 = (bf16[32,8,128]{2,1,0:T(8,128)(2,1)S(1)}, bf16[32,8,128]{2,1,0:T(8,128)(2,1)S(1)}, u32[]{:S(2)}, u32[]{:S(2)}) collective-permute-start(bf16[32,8,128]{2,1,0:T(8,128)(2,1)S(1)} %get-tuple-element.68), channel_id=1, source_target_pairs={{0,1},{1,0},{2,3},{3,2},{4,5},{5,4},{6,7},{7,6},{8,9},{9,8},{10,11... | collective-permute-start | bytes 196616 | tf_op jit(solution)/shard_map/ppermute | solution.py:391
  74.9 6.0 %collective-permute-start.14 = (bf16[32,8,128]{2,1,0:T(8,128)(2,1)S(1)}, bf16[32,8,128]{2,1,0:T(8,128)(2,1)S(1)}, u32[]{:S(2)}, u32[]{:S(2)}) collective-permute-start(bf16[32,8,128]{2,1,0:T(8,128)(2,1)S(1)} %get-tuple-element.62), channel_id=1, source_target_pairs={{0,1},{1,0},{2,3},{3,2},{4,5},{5,4},{6,7},{7,6},{8,9},{9,8},{10,11... | collective-permute-start | bytes 196616 | tf_op jit(solution)/shard_map/ppermute | solution.py:391
  75.5 5.4 %collective-permute-start.16 = (bf16[32,8,128]{2,1,0:T(8,128)(2,1)S(1)}, bf16[32,8,128]{2,1,0:T(8,128)(2,1)S(1)}, u32[]{:S(2)}, u32[]{:S(2)}) collective-permute-start(bf16[32,8,128]{2,1,0:T(8,128)(2,1)S(1)} %shard_map.89), channel_id=1, source_target_pairs={{0,64},{64,128},{128,192},{192,0},{1,65},{65,129},{129,193},{193,1... | collective-permute-start | bytes 196616 | tf_op jit(solution)/shard_map/ppermute | solution.py:311
  77.1 6.5 %collective-permute-start.18 = (bf16[32,8,128]{2,1,0:T(8,128)(2,1)S(1)}, bf16[32,8,128]{2,1,0:T(8,128)(2,1)S(1)}, u32[]{:S(2)}, u32[]{:S(2)}) collective-permute-start(bf16[32,8,128]{2,1,0:T(8,128)(2,1)S(1)} %shard_map.90), channel_id=1, source_target_pairs={{0,128},{64,192},{128,0},{192,64},{1,129},{65,193},{129,1},{193,65... | collective-permute-start | bytes 196616 | tf_op jit(solution)/shard_map/ppermute | solution.py:311
  77.6 6.4 %collective-permute-start.20 = (bf16[32,8,128]{2,1,0:T(8,128)(2,1)S(1)}, bf16[32,8,128]{2,1,0:T(8,128)(2,1)S(1)}, u32[]{:S(2)}, u32[]{:S(2)}) collective-permute-start(bf16[32,8,128]{2,1,0:T(8,128)(2,1)S(1)} %shard_map.91), channel_id=1, source_target_pairs={{0,192},{64,0},{128,64},{192,128},{1,193},{65,1},{129,65},{193,129... | collective-permute-start | bytes 196616 | tf_op jit(solution)/shard_map/ppermute | solution.py:311
